TPU v7x, 32 devices: a whole 2x2x4 slice. The times are simulated.
32 devices in a mesh: group: 2 (over y), dp: 8 (over z, x), latent: 2 (over core).
Axes of the slice: x: 2, y: 2, z: 4, core: 2. Of those that a mesh axis runs over, the one named last changes fastest.
Arguments:
- cur_rows: bfloat16 [32, 4608], P(('group', 'dp')), parts along dimension 0, may hold values from -144 to 144
- cached_rows: bfloat16 [32, 4608], P('group', 'dp'), parts along dimension 0, may hold values from -6 to 6
- shuffle_perm: int32 [32], P('group'), parts along dimension 0, may hold values from 0 to 15, each once
- weight: bfloat16 [8192, 4608], P(('group', 'dp', 'latent')), parts along dimension 0, may hold values from -0.09375 to 0.09375
- enc_bias: float32 [8192], P(('group', 'dp', 'latent')), parts along dimension 0, may hold values from -3 to 3
- dec_bias: float32 [9216], P('group'), parts along dimension 0, may hold values from -3 to 3
Outputs:
- weight_grad: bfloat16 [8192, 4608], P(('group', 'dp', 'latent')), parts along dimension 0
- enc_bias_grad: float32 [8192], P(('group', 'dp', 'latent')), parts along dimension 0
- dec_bias_grad: float32 [9216], P(('group', 'dp', 'latent')), parts along dimension 0
- next_batch: bfloat16 [32, 4608], P(('group', 'dp')), parts along dimension 0
There are 2 independent parts, one for each index of `group`. A program takes and returns all parts, laid end to end along the dimension named above; each array names one. Nothing has to cross between parts.
Inputs may be any that keep to these rules, and one draw needn't show every extreme that they name: Cached row r goes to device shuffle_perm[r] // 2 of dp, slot shuffle_perm[r] % 2; every position once.
All inputs are finite; a program needn't handle non-finite values.
Results may differ from a plain program's by a relative error of at most 0.0055.
Values may be sent and summed in bfloat16 or wider, within the bound.
No kernel may reach another device: no remote copies, remote signals or barrier semaphores. Data moves between devices by JAX's collectives and lax.ppermute only.
A program may use at most 64 MiB of HBM per device.

v0:
```python
import jax
import jax.numpy as jnp
from jax import lax
from jax.sharding import PartitionSpec as P

SPARSITY = 4.0
SHARP = 4.0


def batch_scales(rows_f):
    squares = jnp.sum(rows_f * rows_f, axis=1)
    batch_rows = squares.shape[0] // 2
    means = jnp.stack([jnp.mean(squares[:batch_rows]), jnp.mean(squares[batch_rows:])])
    scales = jnp.sqrt(rows_f.shape[1] / means)
    return jnp.repeat(scales, batch_rows)


def per_device(cur_rows, cached_rows, shuffle_perm, weight, enc_bias, dec_bias):
    gathered = lax.all_gather(cur_rows, "dp", axis=0, tiled=True)
    batch_rows = gathered.shape[0] // 2
    rows_f = gathered.astype(jnp.float32)
    scales = batch_scales(rows_f)
    projected = jnp.einsum("rd,ld->rl", gathered, weight, preferred_element_type=jnp.float32)
    preact = scales[:, None] * projected + enc_bias[None, :]
    latents = jax.nn.softplus(SHARP * preact) / SHARP
    latents_b = latents.astype(jnp.bfloat16)
    weight_f = weight.astype(jnp.float32)
    row_norms = jnp.sqrt(jnp.sum(weight_f * weight_f, axis=1) + 1e-06)
    shares = dec_bias.shape[0] // lax.axis_size(("dp", "latent"))
    offset = lax.axis_index(("dp", "latent")) * shares
    recon_share = lax.psum_scatter(
        jnp.einsum("rl,ld->dr", latents_b, weight, preferred_element_type=jnp.float32),
        ("dp", "latent"),
        scatter_dimension=0,
        tiled=True,
    )
    target_share = lax.dynamic_slice_in_dim(rows_f, offset, shares, 1).T
    bias_share = lax.dynamic_slice_in_dim(dec_bias, offset, shares, 0)
    error_share = recon_share + bias_share[:, None] - target_share * scales[None, :]
    grad_share = (2.0 / batch_rows * error_share).astype(jnp.bfloat16)
    grad_t = lax.all_gather(grad_share, ("dp", "latent"), axis=0, tiled=True)
    dec_bias_grad = 2.0 / batch_rows * jnp.sum(error_share, axis=1)
    grad_latents = (
        jnp.einsum("dr,ld->rl", grad_t, weight, preferred_element_type=jnp.float32)
        + SPARSITY / batch_rows * row_norms[None, :]
    )
    grad_pre = grad_latents * jax.nn.sigmoid(SHARP * preact)
    enc_bias_grad = jnp.sum(grad_pre, axis=0)
    scaled = (grad_pre * scales[:, None]).astype(jnp.bfloat16)
    weight_sum = jnp.einsum("rl,rd->ld", scaled, gathered, preferred_element_type=jnp.float32)
    weight_sum = weight_sum + jnp.einsum(
        "rl,dr->ld", latents_b, grad_t, preferred_element_type=jnp.float32
    )
    weight_sum = (
        weight_sum
        + SPARSITY / batch_rows * jnp.sum(latents, axis=0)[:, None] * weight_f / row_norms[:, None]
    )
    weight_grad = weight_sum.astype(jnp.bfloat16)
    row_total = cached_rows.shape[0]
    slots = jnp.arange(row_total, dtype=jnp.int32)
    selector = (shuffle_perm[None, :] == slots[:, None]).astype(jnp.bfloat16)
    ordered = jnp.dot(selector, cached_rows, preferred_element_type=jnp.float32).astype(
        jnp.bfloat16
    )
    next_batch = lax.all_to_all(ordered, "dp", split_axis=0, concat_axis=1, tiled=True)
    return (weight_grad, enc_bias_grad, dec_bias_grad, next_batch)


def solution(mesh):
    return jax.shard_map(
        per_device,
        mesh=mesh,
        in_specs=(
            P(("group", "dp"), None),
            P("group", "dp"),
            P("group"),
            P(("group", "dp", "latent"), None),
            P(("group", "dp", "latent")),
            P("group"),
        ),
        out_specs=(
            P(("group", "dp", "latent"), None),
            P(("group", "dp", "latent")),
            P(("group", "dp", "latent")),
            P(("group", "dp"), None),
        ),
        check_vma=False,
    )
```

profile of v0, /device:TPU:0, one launch (start us, length us, event | category | flops | bytes accessed | tf_op | source)
XLA Modules:
  0.0 144.9 jit_solution(2189887187617611683)
XLA Ops:
  7.2 0.0 copy-start
  7.2 0.0 copy-start.1
  7.2 0.0 reduce-scatter.4.cloned.1.call-start
  7.2 32.7 %all-gather = bf16[8,2,4608]{2,1,0:T(2,128)(2,1)S(1)} all-gather(bf16[1,2,4608]{2,1,0:T(2,128)(2,1)} %bitcast.26), channel_id=1, replica_groups=mesh['group'=2,'dp'=8,'latent'=2] {'dp'}, dimensions={0}, use_global_device_ids=true | all-gather | bytes 165888 | tf_op jit(solution)/shard_map/all_gather | solution.py:19
  39.9 0.1 reshape.31
  40.0 0.2 multiply_reduce_fusion
  40.1 0.7 slice_reduce_fusion.1
  42.1 0.1 fusion.14
  42.2 0.1 broadcast_in_dim.2
  42.3 0.1 mul.87
  42.4 2.4 %fusion.11 = (f32[256]{0:T(256)S(1)}, f32[16,256]{1,0:T(8,128)S(1)}) fusion(f32[256]{0:T(256)} %param.10, bf16[16,4608]{1,0:T(8,128)(2,1)S(1)} %reshape.31, bf16[256,4608]{1,0:T(8,128)(2,1)} %param.9, f32[16]{0:T(128)S(1)} %mul.87), kind=kOutput, calls=%fused_computation.24 | convolution fusion | flops 37793536 | bytes 2525248 | tf_op jit(solution)/shard_map/rd,ld->rl/dot_general | solution.py:23
  44.8 0.0 copy-done.1
  44.8 0.4 convolution_bitcast_fusion
  45.2 0.0 copy-start.2
  45.2 2.1 %copy.15 = f32[4608,16]{1,0:T(8,128)} copy(f32[4608,16]{0,1:T(8,128)S(1)} %convolution_bitcast_fusion) | data formatting | bytes 589824
  47.3 0.0 reduce-scatter.4.cloned.1.call-update
  47.3 0.0 copy-done
  47.3 0.0 copy-done.2
  47.4 0.1 convolution_convert_fusion
  47.5 0.6 all_to_all.14
  48.1 5.5 %all-to-all-start = ((bf16[8,2,576]{2,1,0:T(2,128)(2,1)}), bf16[8,2,576]{2,1,0:T(2,128)(2,1)S(1)}, u32[]{:S(2)}, u32[]{:S(2)}) async-start(bf16[8,2,576]{2,1,0:T(2,128)(2,1)} %all_to_all.14), calls=%async_computation | async-start | bytes 40960 | tf_op jit(solution)/shard_map/all_to_all | solution.py:65
  53.6 0.5 fusion.2
  54.2 0.8 dynamic_slice.6
  54.9 5.2 %all-to-all-done = bf16[8,2,576]{2,1,0:T(2,128)(2,1)S(1)} async-done(((bf16[8,2,576]{2,1,0:T(2,128)(2,1)}), bf16[8,2,576]{2,1,0:T(2,128)(2,1)S(1)}, u32[]{:S(2)}, u32[]{:S(2)}) %all-to-all-start) | async-done | bytes 18464 | tf_op jit(solution)/shard_map/all_to_all | solution.py:65
  60.2 0.7 all_to_all.17
  60.9 50.5 %reduce-scatter.4.cloned.1.call-done = f32[288,16]{1,0:T(8,128)} async-done(((f32[4608,16]{1,0:T(8,128)}), f32[288,16]{1,0:T(8,128)}) %reduce-scatter.4.cloned.1.call-update) | async-done | bytes 18448
  111.3 1.0 copy.16
  112.3 0.1 fusion.15
  112.4 20.0 %all-gather.1 = bf16[16,288,16]{1,2,0:T(8,128)(2,1)S(1)} all-gather(bf16[1,288,16]{1,2,0:T(8,128)(2,1)S(1)} %get-tuple-element.7), channel_id=1, replica_groups=mesh['group'=2,'dp'=8,'latent'=2] {'dp','latent'}, dimensions={0}, use_global_device_ids=true | all-gather | bytes 156672 | tf_op jit(solution)/shard_map/all_gather | solution.py:41
  132.4 0.2 reshape.33
  132.7 1.3 fusion.18
  134.0 0.9 fusion.9
  134.8 0.6 broadcast_multiply_fusion
  135.4 2.7 %fusion.1 = bf16[256,4608]{1,0:T(8,128)(2,1)} fusion(f32[256,4608]{1,0:T(8,128)S(1)} %fusion.9, bf16[4608,16]{0,1:T(8,128)(2,1)S(1)} %reshape.33, bf16[256,4608]{1,0:T(8,128)(2,1)S(1)} %copy-done.1, f32[256]{0:T(256)S(1)} %get-tuple-element.8, f32[256]{0:T(256)S(1)} %broadcast_multiply_fusion.1, f32[16,256]{1,0:T(8,128)S(1)} %get-tuple-element.11), kind=kOutput, calls=%fused_computation.2 | convolution fusion | flops 44859392 | bytes 9603072 | tf_op jit(solution)/shard_map/rl,dr->ld/dot_general | solution.py:51
  (5 shorter events, 0.1 us)
Async XLA Ops:
  7.2 40.2 %copy-start = (bf16[16,576]{1,0:T(8,128)(2,1)S(1)}, bf16[16,576]{1,0:T(8,128)(2,1)}, u32[]{:S(2)}) copy-start(bf16[16,576]{1,0:T(8,128)(2,1)} %param.7) | copy-start | bytes 55300
  7.2 37.6 %copy-start.1 = (bf16[256,4608]{1,0:T(8,128)(2,1)S(1)}, bf16[256,4608]{1,0:T(8,128)(2,1)}, u32[]{:S(2)}) copy-start(bf16[256,4608]{1,0:T(8,128)(2,1)} %param.9) | copy-start | bytes 7077892
  7.2 104.1 %reduce-scatter.4.cloned.1.call-start = ((), (), s32[]{:S(2)}) async-start(), calls=%async_computation.2 | async-start | bytes 2506752
  45.2 2.1 %copy-start.2 = (s32[16]{0:T(128)S(1)}, s32[16]{0:T(128)}, u32[]{:S(2)}) copy-start(s32[16]{0:T(128)} %param.8) | copy-start | bytes 196
  48.1 12.1 %all-to-all-start = ((bf16[8,2,576]{2,1,0:T(2,128)(2,1)}), bf16[8,2,576]{2,1,0:T(2,128)(2,1)S(1)}, u32[]{:S(2)}, u32[]{:S(2)}) async-start(bf16[8,2,576]{2,1,0:T(2,128)(2,1)} %all_to_all.14), calls=%async_computation | async-start | bytes 40960 | tf_op jit(solution)/shard_map/all_to_all | solution.py:65
Sparse Core Ops, SparseCore 0:
  47.5 63.8 reduce-scatter.3
where the time goes:
time: 145 us
  waiting for transfers between devices  55.7 us (38%)
  blocking collectives  52.6 us (36%)
  between operations  15.4 us (11%)
  matrix products  7.79 us (5%)
  local copies, waits for them, and re-layouts  5.67 us (4%)
  starting transfers between devices  5.49 us (4%)
  other arithmetic  2.19 us (2%)
    unnamed x2, waiting for transfers between devices  50.5 us
    all_gather x1, blocking collectives, per_device(): gathered = lax.all_gather(cur_rows, 'dp', axis=0, tiled=True)  32.7 us
    all_gather x1, blocking collectives, per_device(): grad_t = lax.all_gather(grad_share, ('dp', 'latent'), axis=0, tiled=True)  20 us
    all_to_all x1, starting transfers between devices, per_device(): lax.all_to_all(ordered, 'dp', split_axis=0, concat_axis=1, tiled=True)  5.46 us
    all_to_all x1, waiting for transfers between devices, per_device(): lax.all_to_all(ordered, 'dp', split_axis=0, concat_axis=1, tiled=True)  5.21 us
    unnamed x10, local copies, waits for them, and re-layouts  3.36 us
  transfers between devices with their start and end apart: 2, of which 2 were waited for; matrix products, arithmetic and copies ran while one was open for 1% of the time, Pallas kernels for 0%

commit v1 on v0

v1 whole, which is shorter than its diff:
```python
import jax
import jax.numpy as jnp
from jax import lax
from jax.sharding import PartitionSpec as P

SPARSITY = 4.0
SHARP = 4.0


def batch_scales(rows_f):
    squares = jnp.sum(rows_f * rows_f, axis=1)
    batch_rows = squares.shape[0] // 2
    means = jnp.stack([jnp.mean(squares[:batch_rows]), jnp.mean(squares[batch_rows:])])
    scales = jnp.sqrt(rows_f.shape[1] / means)
    return jnp.repeat(scales, batch_rows)


def exchange(value, axis, distance):
    size = lax.axis_size(axis)
    return lax.ppermute(value, axis, [(k, k ^ distance) for k in range(size)])


def per_device(cur_rows, cached_rows, shuffle_perm, weight, enc_bias, dec_bias):
    dp = lax.axis_size("dp")
    own, width = cur_rows.shape
    half = width // 2
    core = lax.axis_index("latent")

    row_total, columns = cached_rows.shape
    slots = jnp.arange(row_total, dtype=jnp.int32)
    selector = (shuffle_perm[None, :] == slots[:, None]).astype(jnp.bfloat16)
    ordered = jnp.dot(selector, cached_rows, preferred_element_type=jnp.float32).astype(
        jnp.bfloat16
    )
    message = jnp.concatenate(
        [jnp.broadcast_to(cur_rows[None], (dp, own, width)), ordered.reshape(dp, own, columns)],
        axis=2,
    )
    arrived = lax.all_to_all(message, "dp", 0, 0)
    gathered = arrived[:, :, :width].reshape(dp * own, width)
    next_batch = arrived[:, :, width:].transpose(1, 0, 2).reshape(own, dp * columns)

    batch_rows = gathered.shape[0] // 2
    rows_f = gathered.astype(jnp.float32)
    scales = batch_scales(rows_f)
    projected = jnp.einsum("rd,ld->rl", gathered, weight, preferred_element_type=jnp.float32)
    preact = scales[:, None] * projected + enc_bias[None, :]
    latents = jax.nn.softplus(SHARP * preact) / SHARP
    latents_b = latents.astype(jnp.bfloat16)
    weight_f = weight.astype(jnp.float32)
    row_norms = jnp.sqrt(jnp.sum(weight_f * weight_f, axis=1) + 1e-06)

    partial = jnp.einsum("rl,ld->rd", latents_b, weight, preferred_element_type=jnp.float32)
    mine = lax.dynamic_slice_in_dim(partial, core * half, half, 1)
    other = lax.dynamic_slice_in_dim(partial, (1 - core) * half, half, 1)
    total = mine + exchange(other.astype(jnp.bfloat16), "latent", 1).astype(jnp.float32)
    distance = 1
    while distance < dp:
        total = total + exchange(total.astype(jnp.bfloat16), "dp", distance).astype(jnp.float32)
        distance *= 2

    target = lax.dynamic_slice_in_dim(rows_f, core * half, half, 1)
    bias = lax.dynamic_slice_in_dim(dec_bias, core * half, half, 0)
    error = total + bias[None, :] - target * scales[:, None]
    grad_mine = (2.0 / batch_rows * error).astype(jnp.bfloat16)
    grad_other = exchange(grad_mine, "latent", 1)
    low = jnp.where(core == 0, grad_mine, grad_other)
    high = jnp.where(core == 0, grad_other, grad_mine)
    grad_out = jnp.concatenate([low, high], axis=1)

    shares = width // (2 * dp)
    offset = lax.axis_index(("dp", "latent")) * shares
    column_sums = jnp.sum(grad_out.astype(jnp.float32), axis=0)
    dec_bias_grad = lax.dynamic_slice_in_dim(column_sums, offset, shares, 0)

    grad_latents = (
        jnp.einsum("rd,ld->rl", grad_out, weight, preferred_element_type=jnp.float32)
        + SPARSITY / batch_rows * row_norms[None, :]
    )
    grad_pre = grad_latents * jax.nn.sigmoid(SHARP * preact)
    enc_bias_grad = jnp.sum(grad_pre, axis=0)
    scaled = (grad_pre * scales[:, None]).astype(jnp.bfloat16)
    left = jnp.concatenate([scaled, latents_b], axis=0)
    right = jnp.concatenate([gathered, grad_out], axis=0)
    weight_sum = jnp.einsum("rl,rd->ld", left, right, preferred_element_type=jnp.float32)
    pull = SPARSITY / batch_rows * jnp.sum(latents, axis=0) / row_norms
    weight_grad = (weight_sum + pull[:, None] * weight_f).astype(jnp.bfloat16)
    return (weight_grad, enc_bias_grad, dec_bias_grad, next_batch)


def solution(mesh):
    return jax.shard_map(
        per_device,
        mesh=mesh,
        in_specs=(
            P(("group", "dp"), None),
            P("group", "dp"),
            P("group"),
            P(("group", "dp", "latent"), None),
            P(("group", "dp", "latent")),
            P("group"),
        ),
        out_specs=(
            P(("group", "dp", "latent"), None),
            P(("group", "dp", "latent")),
            P(("group", "dp", "latent")),
            P(("group", "dp"), None),
        ),
        check_vma=False,
    )
```

time: 145 us -> 46.2 us (0.32)
  blocking collectives: 52.6 us -> 0 us
  waiting for transfers between devices: 55.7 us -> 21.4 us
  between operations: 15.4 us -> 2.08 us
  starting transfers between devices: 5.49 us -> 9.37 us
  local copies, waits for them, and re-layouts: 5.67 us -> 3.34 us
    all_gather x2 -> x0, blocking collectives: 52.6 us -> none  [the longest x1 32.7 us: per_device(): gathered = lax.all_gather(cur_rows, 'dp', axis=0, tiled=True)]
    unnamed x2 -> x0, waiting for transfers between devices: 50.5 us -> none
    ppermute x0 -> x5, waiting for transfers between devices: none -> 13.8 us  [exchange(): return lax.ppermute(value, axis, [(k, k ^ distance) for k in range(size)])]
    unnamed x10 -> x6, local copies, waits for them, and re-layouts: 3.36 us -> 0.73 us
    all_to_all x1, waiting for transfers between devices: 5.21 us -> 7.59 us  [per_device(): arrived = lax.all_to_all(message, 'dp', 0, 0)]
    ppermute x0 -> x5, starting transfers between devices: none -> 2.12 us  [exchange(): return lax.ppermute(value, axis, [(k, k ^ distance) for k in range(size)])]
    all_to_all x1, starting transfers between devices: 5.46 us -> 7.25 us  [per_device(): arrived = lax.all_to_all(message, 'dp', 0, 0)]
    dot_general x4 -> x3, matrix products: 5.24 us -> 3.93 us  [the longest x1 2.21 us: per_device(): jnp.einsum('rl,rd->ld', left, right, preferred_element_type=jnp.float32)]
  transfers between devices with their start and end apart: 2 -> 6, of which waited for: 2 -> 6; matrix products, arithmetic and copies ran while one was open for 1% -> 3% of each run, Pallas kernels for 0% -> 0%
where the time goes in v1:
time: 46.2 us; the launch traced here: 45.9 us
  waiting for transfers between devices  21.4 us (46%)
  starting transfers between devices  9.37 us (20%)
  matrix products  7.13 us (15%)
  local copies, waits for them, and re-layouts  3.34 us (7%)
  other arithmetic  2.55 us (6%)
  between operations  2.08 us (5%)
    ppermute x5, waiting for transfers between devices, exchange(): return lax.ppermute(value, axis, [(k, k ^ distance) for k in range(size)])  13.8 us
    all_to_all x1, waiting for transfers between devices, per_device(): arrived = lax.all_to_all(message, 'dp', 0, 0)  7.59 us
    all_to_all x1, starting transfers between devices, per_device(): arrived = lax.all_to_all(message, 'dp', 0, 0)  7.25 us
    dot_general x1, matrix products, per_device(): jnp.einsum('rd,ld->rl', gathered, weight, preferred_element_type=jnp.floa...  2.43 us
    dot_general x1, matrix products, per_device(): jnp.einsum('rl,rd->ld', left, right, preferred_element_type=jnp.float32)  2.21 us
    ppermute x5, starting transfers between devices, exchange(): return lax.ppermute(value, axis, [(k, k ^ distance) for k in range(size)])  2.12 us
    dot_general x1, matrix products, per_device(): jnp.einsum('rd,ld->rl', grad_out, weight, preferred_element_type=jnp.floa...  1.3 us
  transfers between devices with their start and end apart: 6, of which 6 were waited for; matrix products, arithmetic and copies ran while one was open for 3% of the time, Pallas kernels for 0%

profile of v1, /device:TPU:0, one launch (start us, length us, event | category | flops | bytes accessed | tf_op | source)
XLA Modules:
  0.0 45.9 jit_solution(12484218186224702316)
XLA Ops:
  0.6 0.0 copy-start
  0.6 0.0 copy-start.1
  0.7 0.7 %copy-done = bf16[16,576]{1,0:T(8,128)(2,1)S(1)} copy-done((bf16[16,576]{1,0:T(8,128)(2,1)S(1)}, bf16[16,576]{1,0:T(8,128)(2,1)}, u32[]{:S(2)}) %copy-start) | copy-done | bytes 18456
  1.4 0.8 %convolution_convert_fusion = bf16[16,576]{1,0:T(8,128)(2,1)S(1)} fusion(bf16[16,576]{1,0:T(8,128)(2,1)S(1)} %copy-done, s32[16]{0:T(128)} %param.8), kind=kOutput, calls=%fused_computation.5 | convolution fusion | flops 304384 | bytes 36928 | tf_op jit(solution)/shard_map/dot_general | solution.py:32
  2.2 0.8 %broadcast_in_dim.4 = bf16[8,2,4608]{2,1,0:T(2,128)(2,1)S(1)} broadcast(bf16[2,4608]{1,0:T(2,128)(2,1)} %param.6), dimensions={1,2} | broadcast | bytes 165888 | tf_op jit(solution)/shard_map/broadcast_in_dim | solution.py:36
  3.0 0.8 %pad_maximum_fusion = bf16[8,2,5184]{2,1,0:T(2,128)(2,1)} fusion(bf16[8,2,576]{2,1,0:T(2,128)(2,1)S(1)} %reshape.39, bf16[8,2,4608]{2,1,0:T(2,128)(2,1)S(1)} %broadcast_in_dim.4), kind=kLoop, calls=%fused_computation.18 | loop fusion | flops 331776 | bytes 331776 | tf_op jit(solution)/shard_map/concatenate | solution.py:35
  3.8 7.3 %all-to-all-start = ((bf16[8,2,5184]{2,1,0:T(2,128)(2,1)}), bf16[8,2,5184]{2,1,0:T(2,128)(2,1)S(1)}, u32[]{:S(2)}, u32[]{:S(2)}) async-start(bf16[8,2,5184]{2,1,0:T(2,128)(2,1)} %pad_maximum_fusion), calls=%async_computation | async-start | bytes 335872 | tf_op jit(solution)/shard_map/all_to_all | solution.py:39
  11.0 7.6 %all-to-all-done = bf16[8,2,5184]{2,1,0:T(2,128)(2,1)S(1)} async-done(((bf16[8,2,5184]{2,1,0:T(2,128)(2,1)}), bf16[8,2,5184]{2,1,0:T(2,128)(2,1)S(1)}, u32[]{:S(2)}, u32[]{:S(2)}) %all-to-all-start) | async-done | bytes 165920 | tf_op jit(solution)/shard_map/all_to_all | solution.py:39
  18.6 0.2 multiply_reduce_fusion
  18.9 0.6 %slice_reduce_fusion.1 = (f32[]{:T(128)}, f32[]{:T(128)}) fusion(f32[8,2]{1,0:T(8,128)S(1)} %multiply_reduce_fusion), kind=kLoop, calls=%fused_computation.41 | loop fusion | flops 14 | bytes 72 | tf_op jit(solution)/shard_map/reduce_sum | solution.py:13
  20.8 0.1 fusion.19
  20.9 0.1 broadcast_in_dim.5
  20.9 0.1 mul.86
  21.0 0.1 slice.18
  21.1 0.1 reshape.40
  21.2 2.4 %fusion.17 = (bf16[16,256]{1,0:T(8,128)(2,1)S(1)}, f32[256]{0:T(256)S(1)}, f32[16,256]{1,0:T(8,128)S(1)}) fusion(f32[256]{0:T(256)} %param.10, bf16[16,4608]{1,0:T(8,128)(2,1)S(1)} %reshape.40, bf16[256,4608]{1,0:T(8,128)(2,1)} %param.9, f32[16]{0:T(128)S(1)} %mul.86), kind=kOutput, calls=%fused_computation.38 | convolution fusion | flops 37797632 | bytes 2533440 | tf_op jit(solution)/shard_map/rd,ld->rl/dot_general | solution.py:46
  23.6 0.0 copy-done.1
  23.6 0.0 copy-start.2
  23.7 0.4 fusion.24
  24.1 0.1 collective-permute-start
  24.2 1.2 %collective-permute-done = bf16[16,2304]{1,0:T(8,128)(2,1)S(1)} collective-permute-done((bf16[16,2304]{1,0:T(8,128)(2,1)S(1)}, bf16[16,2304]{1,0:T(8,128)(2,1)S(1)}, u32[]{:S(2)}, u32[]{:S(2)}) %collective-permute-start) | collective-permute-done | bytes 73760 | tf_op jit(solution)/shard_map/ppermute | solution.py:20
  25.5 1.0 %collective-permute-start.1 = (bf16[16,2304]{1,0:T(8,128)(2,1)S(1)}, bf16[16,2304]{1,0:T(8,128)(2,1)S(1)}, u32[]{:S(2)}, u32[]{:S(2)}) collective-permute-start(bf16[16,2304]{1,0:T(8,128)(2,1)S(1)} %fusion.22), channel_id=1, source_target_pairs={{0,2},{2,0},{4,6},{6,4},{8,10},{10,8},{12,14},{14,12},{1,3},{3,1},... | collective-permute-start | bytes 221192 | tf_op jit(solution)/shard_map/ppermute | solution.py:20
  26.5 3.4 %collective-permute-done.1 = bf16[16,2304]{1,0:T(8,128)(2,1)S(1)} collective-permute-done((bf16[16,2304]{1,0:T(8,128)(2,1)S(1)}, bf16[16,2304]{1,0:T(8,128)(2,1)S(1)}, u32[]{:S(2)}, u32[]{:S(2)}) %collective-permute-start.1) | collective-permute-done | bytes 73760 | tf_op jit(solution)/shard_map/ppermute | solution.py:20
  29.9 0.3 collective-permute-start.2
  30.2 0.5 %fusion.1 = f32[256]{0:T(256)S(1)} fusion(bf16[256,4608]{1,0:T(8,128)(2,1)S(1)} %copy-done.1), kind=kLoop, calls=%fused_computation.4 | loop fusion | flops 3538688 | bytes 2360320 | tf_op jit(solution)/shard_map/reduce_sum | solution.py:51
  30.8 0.0 copy-done.2
  30.8 0.1 dynamic_slice.17
  30.9 3.4 %collective-permute-done.2 = bf16[16,2304]{1,0:T(8,128)(2,1)S(1)} collective-permute-done((bf16[16,2304]{1,0:T(8,128)(2,1)S(1)}, bf16[16,2304]{1,0:T(8,128)(2,1)S(1)}, u32[]{:S(2)}, u32[]{:S(2)}) %collective-permute-start.2) | collective-permute-done | bytes 73760 | tf_op jit(solution)/shard_map/ppermute | solution.py:20
  34.4 0.6 %collective-permute-start.3 = (bf16[16,2304]{1,0:T(8,128)(2,1)S(1)}, bf16[16,2304]{1,0:T(8,128)(2,1)S(1)}, u32[]{:S(2)}, u32[]{:S(2)}) collective-permute-start(bf16[16,2304]{1,0:T(8,128)(2,1)S(1)} %fusion.11), channel_id=1, source_target_pairs={{0,8},{2,10},{4,12},{6,14},{8,0},{10,2},{12,4},{14,6},{1,9},{3,11}... | collective-permute-start | bytes 221192 | tf_op jit(solution)/shard_map/ppermute | solution.py:20
  35.0 5.2 %collective-permute-done.3 = bf16[16,2304]{1,0:T(8,128)(2,1)S(1)} collective-permute-done((bf16[16,2304]{1,0:T(8,128)(2,1)S(1)}, bf16[16,2304]{1,0:T(8,128)(2,1)S(1)}, u32[]{:S(2)}, u32[]{:S(2)}) %collective-permute-start.3) | collective-permute-done | bytes 73760 | tf_op jit(solution)/shard_map/ppermute | solution.py:20
  40.2 0.1 multiply_convert_fusion
  40.3 0.1 collective-permute-start.4
  40.4 0.7 %reshape.41 = bf16[2,4608]{1,0:T(2,128)(2,1)} reshape(bf16[2,8,576]{2,1,0:T(8,128)(2,1)S(1)} %copy.14) | data formatting | bytes 36864 | tf_op jit(solution)/shard_map/reshape | solution.py:41
  41.1 0.5 %collective-permute-done.4 = bf16[16,2304]{1,0:T(8,128)(2,1)S(1)} collective-permute-done((bf16[16,2304]{1,0:T(8,128)(2,1)S(1)}, bf16[16,2304]{1,0:T(8,128)(2,1)S(1)}, u32[]{:S(2)}, u32[]{:S(2)}) %collective-permute-start.4) | collective-permute-done | bytes 73760 | tf_op jit(solution)/shard_map/ppermute | solution.py:20
  41.6 0.1 convert_reduce_fusion
  41.7 1.3 %fusion.23 = (f32[256]{0:T(256)}, bf16[16,256]{1,0:T(8,128)(2,1)S(1)}) fusion(f32[16]{0:T(128)S(1)} %mul.86, f32[16,256]{1,0:T(8,128)S(1)} %get-tuple-element.14, f32[256]{0:T(256)S(1)} %get-tuple-element.12, bf16[256,4608]{1,0:T(8,128)(2,1)S(1)} %copy-done.1, bf16[16,2304]{1,0:T(8,128)(2,1)S(1)} %get-tuple-element.7, bf16[16,2304]{1,0:T(8,128)(2,1)S(1)} %get-tuple-element.6), kind=kOutput, calls=%fused_computation.49 | convolution fusion | flops 38076160 | bytes 2533440 | tf_op jit(solution)/shard_map/rd,ld->rl/dot_general | solution.py:77
  43.0 0.7 %dynamic_slice.19 = f32[288]{0:T(512)} dynamic-slice(f32[4608]{0:T(1024)S(1)} %convert_reduce_fusion, s32[]{:T(128)S(6)} %select_n.33), dynamic_slice_sizes={288} | dynamic-slice | bytes 2308 | tf_op jit(solution)/shard_map/dynamic_slice | solution.py:74
  43.6 2.2 %fusion = bf16[256,4608]{1,0:T(8,128)(2,1)} fusion(bf16[256,4608]{1,0:T(8,128)(2,1)S(1)} %copy-done.1, f32[256]{0:T(256)S(1)} %get-tuple-element.13, bf16[16,2304]{1,0:T(8,128)(2,1)S(1)} %get-tuple-element.7, bf16[16,2304]{1,0:T(8,128)(2,1)S(1)} %get-tuple-element.6, bf16[16,4608]{1,0:T(8,128)(2,1)S(1)} %reshape.40, ...), kind=kOutput, calls=%fused_computation.1 | convolution fusion | flops 81133568 | bytes 5030912 | tf_op jit(solution)/shard_map/rl,rd->ld/dot_general | solution.py:85
  (9 shorter events, 0.2 us)
Async XLA Ops:
  0.6 0.7 %copy-start = (bf16[16,576]{1,0:T(8,128)(2,1)S(1)}, bf16[16,576]{1,0:T(8,128)(2,1)}, u32[]{:S(2)}) copy-start(bf16[16,576]{1,0:T(8,128)(2,1)} %param.7) | copy-start | bytes 55300
  0.6 23.0 %copy-start.1 = (bf16[256,4608]{1,0:T(8,128)(2,1)S(1)}, bf16[256,4608]{1,0:T(8,128)(2,1)}, u32[]{:S(2)}) copy-start(bf16[256,4608]{1,0:T(8,128)(2,1)} %param.9) | copy-start | bytes 7077892
  3.8 14.8 %all-to-all-start = ((bf16[8,2,5184]{2,1,0:T(2,128)(2,1)}), bf16[8,2,5184]{2,1,0:T(2,128)(2,1)S(1)}, u32[]{:S(2)}, u32[]{:S(2)}) async-start(bf16[8,2,5184]{2,1,0:T(2,128)(2,1)} %pad_maximum_fusion), calls=%async_computation | async-start | bytes 335872 | tf_op jit(solution)/shard_map/all_to_all | solution.py:39
  23.6 7.1 %copy-start.2 = (f32[4608]{0:T(1024)S(1)}, f32[4608]{0:T(1024)}, u32[]{:S(2)}) copy-start(f32[4608]{0:T(1024)} %param.11) | copy-start | bytes 55300
  24.1 1.3 %collective-permute-start = (bf16[16,2304]{1,0:T(8,128)(2,1)S(1)}, bf16[16,2304]{1,0:T(8,128)(2,1)S(1)}, u32[]{:S(2)}, u32[]{:S(2)}) collective-permute-start(bf16[16,2304]{1,0:T(8,128)(2,1)S(1)} %dynamic-slice_convert_fusion), channel_id=1, source_target_pairs={{0,1},{1,0},{2,3},{3,2},{4,5},{5,4},{6,7},{7,6},{8,9},{9,8},{10,11... | collective-permute-start | bytes 221192 | tf_op jit(solution)/shard_map/ppermute | solution.py:20
  25.5 4.4 %collective-permute-start.1 = (bf16[16,2304]{1,0:T(8,128)(2,1)S(1)}, bf16[16,2304]{1,0:T(8,128)(2,1)S(1)}, u32[]{:S(2)}, u32[]{:S(2)}) collective-permute-start(bf16[16,2304]{1,0:T(8,128)(2,1)S(1)} %fusion.22), channel_id=1, source_target_pairs={{0,2},{2,0},{4,6},{6,4},{8,10},{10,8},{12,14},{14,12},{1,3},{3,1},... | collective-permute-start | bytes 221192 | tf_op jit(solution)/shard_map/ppermute | solution.py:20
  29.9 4.4 %collective-permute-start.2 = (bf16[16,2304]{1,0:T(8,128)(2,1)S(1)}, bf16[16,2304]{1,0:T(8,128)(2,1)S(1)}, u32[]{:S(2)}, u32[]{:S(2)}) collective-permute-start(bf16[16,2304]{1,0:T(8,128)(2,1)S(1)} %fusion.10), channel_id=1, source_target_pairs={{0,4},{2,6},{4,0},{6,2},{8,12},{10,14},{12,8},{14,10},{1,5},{3,7},... | collective-permute-start | bytes 221192 | tf_op jit(solution)/shard_map/ppermute | solution.py:20
  34.4 5.8 %collective-permute-start.3 = (bf16[16,2304]{1,0:T(8,128)(2,1)S(1)}, bf16[16,2304]{1,0:T(8,128)(2,1)S(1)}, u32[]{:S(2)}, u32[]{:S(2)}) collective-permute-start(bf16[16,2304]{1,0:T(8,128)(2,1)S(1)} %fusion.11), channel_id=1, source_target_pairs={{0,8},{2,10},{4,12},{6,14},{8,0},{10,2},{12,4},{14,6},{1,9},{3,11}... | collective-permute-start | bytes 221192 | tf_op jit(solution)/shard_map/ppermute | solution.py:20
  40.3 1.3 %collective-permute-start.4 = (bf16[16,2304]{1,0:T(8,128)(2,1)S(1)}, bf16[16,2304]{1,0:T(8,128)(2,1)S(1)}, u32[]{:S(2)}, u32[]{:S(2)}) collective-permute-start(bf16[16,2304]{1,0:T(8,128)(2,1)S(1)} %multiply_convert_fusion), channel_id=1, source_target_pairs={{0,1},{1,0},{2,3},{3,2},{4,5},{5,4},{6,7},{7,6},{8,9},{9,8},{10,11... | collective-permute-start | bytes 221192 | tf_op jit(solution)/shard_map/ppermute | solution.py:20

commit v2 on v1

--- a/solution.py
+++ b/solution.py
@@ -54,7 +54,11 @@
     mine = lax.dynamic_slice_in_dim(partial, core * half, half, 1)
     other = lax.dynamic_slice_in_dim(partial, (1 - core) * half, half, 1)
     total = mine + exchange(other.astype(jnp.bfloat16), "latent", 1).astype(jnp.float32)
-    distance = 1
+    corner = min(4, dp)
+    sent = total.astype(jnp.bfloat16)
+    for distance in range(1, corner):
+        total = total + exchange(sent, "dp", distance).astype(jnp.float32)
+    distance = corner
     while distance < dp:
         total = total + exchange(total.astype(jnp.bfloat16), "dp", distance).astype(jnp.float32)
         distance *= 2

time: 46.2 us -> 44.3 us (0.959)
  waiting for transfers between devices: 21.4 us -> 17.4 us
  starting transfers between devices: 9.37 us -> 11.5 us
    ppermute x5 -> x6, waiting for transfers between devices: 13.8 us -> 9.78 us  [exchange(): return lax.ppermute(value, axis, [(k, k ^ distance) for k in range(size)])]
    ppermute x5 -> x6, starting transfers between devices: 2.12 us -> 4.24 us  [exchange(): return lax.ppermute(value, axis, [(k, k ^ distance) for k in range(size)])]
  transfers between devices with their start and end apart: 6 -> 7, of which waited for: 6 -> 7; matrix products, arithmetic and copies ran while one was open for 3% -> 3% of each run, Pallas kernels for 0% -> 0%
where the time goes in v2:
time: 44.3 us; the launch traced here: 44 us
  waiting for transfers between devices  17.4 us (39%)
  starting transfers between devices  11.5 us (26%)
  matrix products  7.13 us (16%)
  local copies, waits for them, and re-layouts  3.34 us (8%)
  other arithmetic  2.54 us (6%)
  between operations  2.08 us (5%)
    ppermute x6, waiting for transfers between devices, exchange(): return lax.ppermute(value, axis, [(k, k ^ distance) for k in range(size)])  9.78 us
    all_to_all x1, waiting for transfers between devices, per_device(): arrived = lax.all_to_all(message, 'dp', 0, 0)  7.59 us
    all_to_all x1, starting transfers between devices, per_device(): arrived = lax.all_to_all(message, 'dp', 0, 0)  7.25 us
    ppermute x6, starting transfers between devices, exchange(): return lax.ppermute(value, axis, [(k, k ^ distance) for k in range(size)])  4.24 us
    dot_general x1, matrix products, per_device(): jnp.einsum('rd,ld->rl', gathered, weight, preferred_element_type=jnp.floa...  2.43 us
    dot_general x1, matrix products, per_device(): jnp.einsum('rl,rd->ld', left, right, preferred_element_type=jnp.float32)  2.21 us
    dot_general x1, matrix products, per_device(): jnp.einsum('rd,ld->rl', grad_out, weight, preferred_element_type=jnp.floa...  1.3 us
  transfers between devices with their start and end apart: 7, of which 7 were waited for; matrix products, arithmetic and copies ran while one was open for 3% of the time, Pallas kernels for 0%

profile of v2, /device:TPU:0, one launch (start us, length us, event | category | flops | bytes accessed | tf_op | source)
XLA Modules:
  0.0 44.0 jit_solution(1361032712131579435)
XLA Ops:
  0.6 0.0 copy-start
  0.6 0.0 copy-start.1
  0.7 0.7 %copy-done = bf16[16,576]{1,0:T(8,128)(2,1)S(1)} copy-done((bf16[16,576]{1,0:T(8,128)(2,1)S(1)}, bf16[16,576]{1,0:T(8,128)(2,1)}, u32[]{:S(2)}) %copy-start) | copy-done | bytes 18456
  1.4 0.8 %convolution_convert_fusion = bf16[16,576]{1,0:T(8,128)(2,1)S(1)} fusion(bf16[16,576]{1,0:T(8,128)(2,1)S(1)} %copy-done, s32[16]{0:T(128)} %param.8), kind=kOutput, calls=%fused_computation.5 | convolution fusion | flops 304384 | bytes 36928 | tf_op jit(solution)/shard_map/dot_general | solution.py:32
  2.2 0.8 %broadcast_in_dim.4 = bf16[8,2,4608]{2,1,0:T(2,128)(2,1)S(1)} broadcast(bf16[2,4608]{1,0:T(2,128)(2,1)} %param.6), dimensions={1,2} | broadcast | bytes 165888 | tf_op jit(solution)/shard_map/broadcast_in_dim | solution.py:36
  3.0 0.8 %pad_maximum_fusion = bf16[8,2,5184]{2,1,0:T(2,128)(2,1)} fusion(bf16[8,2,576]{2,1,0:T(2,128)(2,1)S(1)} %reshape.39, bf16[8,2,4608]{2,1,0:T(2,128)(2,1)S(1)} %broadcast_in_dim.4), kind=kLoop, calls=%fused_computation.18 | loop fusion | flops 331776 | bytes 331776 | tf_op jit(solution)/shard_map/concatenate | solution.py:35
  3.8 7.3 %all-to-all-start = ((bf16[8,2,5184]{2,1,0:T(2,128)(2,1)}), bf16[8,2,5184]{2,1,0:T(2,128)(2,1)S(1)}, u32[]{:S(2)}, u32[]{:S(2)}) async-start(bf16[8,2,5184]{2,1,0:T(2,128)(2,1)} %pad_maximum_fusion), calls=%async_computation | async-start | bytes 335872 | tf_op jit(solution)/shard_map/all_to_all | solution.py:39
  11.0 7.6 %all-to-all-done = bf16[8,2,5184]{2,1,0:T(2,128)(2,1)S(1)} async-done(((bf16[8,2,5184]{2,1,0:T(2,128)(2,1)}), bf16[8,2,5184]{2,1,0:T(2,128)(2,1)S(1)}, u32[]{:S(2)}, u32[]{:S(2)}) %all-to-all-start) | async-done | bytes 165920 | tf_op jit(solution)/shard_map/all_to_all | solution.py:39
  18.6 0.2 multiply_reduce_fusion
  18.9 0.6 %slice_reduce_fusion.1 = (f32[]{:T(128)}, f32[]{:T(128)}) fusion(f32[8,2]{1,0:T(8,128)S(1)} %multiply_reduce_fusion), kind=kLoop, calls=%fused_computation.39 | loop fusion | flops 14 | bytes 72 | tf_op jit(solution)/shard_map/reduce_sum | solution.py:13
  20.8 0.1 fusion.18
  20.9 0.1 broadcast_in_dim.5
  20.9 0.1 mul.86
  21.0 0.1 slice.18
  21.1 0.1 reshape.40
  21.2 2.4 %fusion.16 = (bf16[16,256]{1,0:T(8,128)(2,1)S(1)}, f32[256]{0:T(256)S(1)}, f32[16,256]{1,0:T(8,128)S(1)}) fusion(f32[256]{0:T(256)} %param.10, bf16[16,4608]{1,0:T(8,128)(2,1)S(1)} %reshape.40, bf16[256,4608]{1,0:T(8,128)(2,1)} %param.9, f32[16]{0:T(128)S(1)} %mul.86), kind=kOutput, calls=%fused_computation.36 | convolution fusion | flops 37797632 | bytes 2533440 | tf_op jit(solution)/shard_map/rd,ld->rl/dot_general | solution.py:46
  23.6 0.0 copy-done.1
  23.6 0.0 copy-start.2
  23.7 0.4 fusion.23
  24.1 0.1 collective-permute-start
  24.2 1.2 %collective-permute-done = bf16[16,2304]{1,0:T(8,128)(2,1)S(1)} collective-permute-done((bf16[16,2304]{1,0:T(8,128)(2,1)S(1)}, bf16[16,2304]{1,0:T(8,128)(2,1)S(1)}, u32[]{:S(2)}, u32[]{:S(2)}) %collective-permute-start) | collective-permute-done | bytes 73760 | tf_op jit(solution)/shard_map/ppermute | solution.py:20
  25.5 0.9 %collective-permute-start.3 = (bf16[16,2304]{1,0:T(8,128)(2,1)S(1)}, bf16[16,2304]{1,0:T(8,128)(2,1)S(1)}, u32[]{:S(2)}, u32[]{:S(2)}) collective-permute-start(bf16[16,2304]{1,0:T(8,128)(2,1)S(1)} %fusion.10), channel_id=1, source_target_pairs={{0,6},{2,4},{4,2},{6,0},{8,14},{10,12},{12,10},{14,8},{1,7},{3,5},... | collective-permute-start | bytes 221192 | tf_op jit(solution)/shard_map/ppermute | solution.py:20
  26.3 1.6 %collective-permute-start.2 = (bf16[16,2304]{1,0:T(8,128)(2,1)S(1)}, bf16[16,2304]{1,0:T(8,128)(2,1)S(1)}, u32[]{:S(2)}, u32[]{:S(2)}) collective-permute-start(bf16[16,2304]{1,0:T(8,128)(2,1)S(1)} %fusion.10), channel_id=1, source_target_pairs={{0,4},{2,6},{4,0},{6,2},{8,12},{10,14},{12,8},{14,10},{1,5},{3,7},... | collective-permute-start | bytes 221192 | tf_op jit(solution)/shard_map/ppermute | solution.py:20
  27.9 1.1 %collective-permute-start.1 = (bf16[16,2304]{1,0:T(8,128)(2,1)S(1)}, bf16[16,2304]{1,0:T(8,128)(2,1)S(1)}, u32[]{:S(2)}, u32[]{:S(2)}) collective-permute-start(bf16[16,2304]{1,0:T(8,128)(2,1)S(1)} %fusion.10), channel_id=1, source_target_pairs={{0,2},{2,0},{4,6},{6,4},{8,10},{10,8},{12,14},{14,12},{1,3},{3,1},... | collective-permute-start | bytes 221192 | tf_op jit(solution)/shard_map/ppermute | solution.py:20
  29.0 0.5 %fusion.1 = f32[256]{0:T(256)S(1)} fusion(bf16[256,4608]{1,0:T(8,128)(2,1)S(1)} %copy-done.1), kind=kLoop, calls=%fused_computation.4 | loop fusion | flops 3538688 | bytes 2360320 | tf_op jit(solution)/shard_map/reduce_sum | solution.py:51
  29.6 0.0 copy-done.2
  29.6 0.1 dynamic_slice.17
  29.7 1.9 %collective-permute-done.3 = bf16[16,2304]{1,0:T(8,128)(2,1)S(1)} collective-permute-done((bf16[16,2304]{1,0:T(8,128)(2,1)S(1)}, bf16[16,2304]{1,0:T(8,128)(2,1)S(1)}, u32[]{:S(2)}, u32[]{:S(2)}) %collective-permute-start.3) | collective-permute-done | bytes 73760 | tf_op jit(solution)/shard_map/ppermute | solution.py:20
  31.5 0.3 collective-permute-done.2
  31.8 0.6 %collective-permute-done.1 = bf16[16,2304]{1,0:T(8,128)(2,1)S(1)} collective-permute-done((bf16[16,2304]{1,0:T(8,128)(2,1)S(1)}, bf16[16,2304]{1,0:T(8,128)(2,1)S(1)}, u32[]{:S(2)}, u32[]{:S(2)}) %collective-permute-start.1) | collective-permute-done | bytes 73760 | tf_op jit(solution)/shard_map/ppermute | solution.py:20
  32.5 0.5 %collective-permute-start.4 = (bf16[16,2304]{1,0:T(8,128)(2,1)S(1)}, bf16[16,2304]{1,0:T(8,128)(2,1)S(1)}, u32[]{:S(2)}, u32[]{:S(2)}) collective-permute-start(bf16[16,2304]{1,0:T(8,128)(2,1)S(1)} %fusion.21), channel_id=1, source_target_pairs={{0,8},{2,10},{4,12},{6,14},{8,0},{10,2},{12,4},{14,6},{1,9},{3,11}... | collective-permute-start | bytes 221192 | tf_op jit(solution)/shard_map/ppermute | solution.py:20
  33.0 5.3 %collective-permute-done.4 = bf16[16,2304]{1,0:T(8,128)(2,1)S(1)} collective-permute-done((bf16[16,2304]{1,0:T(8,128)(2,1)S(1)}, bf16[16,2304]{1,0:T(8,128)(2,1)S(1)}, u32[]{:S(2)}, u32[]{:S(2)}) %collective-permute-start.4) | collective-permute-done | bytes 73760 | tf_op jit(solution)/shard_map/ppermute | solution.py:20
  38.3 0.1 multiply_convert_fusion
  38.4 0.1 collective-permute-start.5
  38.5 0.7 %reshape.41 = bf16[2,4608]{1,0:T(2,128)(2,1)} reshape(bf16[2,8,576]{2,1,0:T(8,128)(2,1)S(1)} %copy.14) | data formatting | bytes 36864 | tf_op jit(solution)/shard_map/reshape | solution.py:41
  39.2 0.5 %collective-permute-done.5 = bf16[16,2304]{1,0:T(8,128)(2,1)S(1)} collective-permute-done((bf16[16,2304]{1,0:T(8,128)(2,1)S(1)}, bf16[16,2304]{1,0:T(8,128)(2,1)S(1)}, u32[]{:S(2)}, u32[]{:S(2)}) %collective-permute-start.5) | collective-permute-done | bytes 73760 | tf_op jit(solution)/shard_map/ppermute | solution.py:20
  39.7 0.1 convert_reduce_fusion
  39.8 1.3 %fusion.22 = (f32[256]{0:T(256)}, bf16[16,256]{1,0:T(8,128)(2,1)S(1)}) fusion(f32[16]{0:T(128)S(1)} %mul.86, f32[16,256]{1,0:T(8,128)S(1)} %get-tuple-element.14, f32[256]{0:T(256)S(1)} %get-tuple-element.12, bf16[256,4608]{1,0:T(8,128)(2,1)S(1)} %copy-done.1, bf16[16,2304]{1,0:T(8,128)(2,1)S(1)} %get-tuple-element.7, bf16[16,2304]{1,0:T(8,128)(2,1)S(1)} %get-tuple-element.6), kind=kOutput, calls=%fused_computation.47 | convolution fusion | flops 38076160 | bytes 2533440 | tf_op jit(solution)/shard_map/rd,ld->rl/dot_general | solution.py:81
  41.1 0.7 %dynamic_slice.19 = f32[288]{0:T(512)} dynamic-slice(f32[4608]{0:T(1024)S(1)} %convert_reduce_fusion, s32[]{:T(128)S(6)} %select_n.33), dynamic_slice_sizes={288} | dynamic-slice | bytes 2308 | tf_op jit(solution)/shard_map/dynamic_slice | solution.py:78
  41.7 2.2 %fusion = bf16[256,4608]{1,0:T(8,128)(2,1)} fusion(bf16[256,4608]{1,0:T(8,128)(2,1)S(1)} %copy-done.1, f32[256]{0:T(256)S(1)} %get-tuple-element.13, bf16[16,2304]{1,0:T(8,128)(2,1)S(1)} %get-tuple-element.7, bf16[16,2304]{1,0:T(8,128)(2,1)S(1)} %get-tuple-element.6, bf16[16,4608]{1,0:T(8,128)(2,1)S(1)} %reshape.40, ...), kind=kOutput, calls=%fused_computation.1 | convolution fusion | flops 81133568 | bytes 5030912 | tf_op jit(solution)/shard_map/rl,rd->ld/dot_general | solution.py:89
  (8 shorter events, 0.1 us)
Async XLA Ops:
  0.6 0.7 %copy-start = (bf16[16,576]{1,0:T(8,128)(2,1)S(1)}, bf16[16,576]{1,0:T(8,128)(2,1)}, u32[]{:S(2)}) copy-start(bf16[16,576]{1,0:T(8,128)(2,1)} %param.7) | copy-start | bytes 55300
  0.6 23.0 %copy-start.1 = (bf16[256,4608]{1,0:T(8,128)(2,1)S(1)}, bf16[256,4608]{1,0:T(8,128)(2,1)}, u32[]{:S(2)}) copy-start(bf16[256,4608]{1,0:T(8,128)(2,1)} %param.9) | copy-start | bytes 7077892
  3.8 14.8 %all-to-all-start = ((bf16[8,2,5184]{2,1,0:T(2,128)(2,1)}), bf16[8,2,5184]{2,1,0:T(2,128)(2,1)S(1)}, u32[]{:S(2)}, u32[]{:S(2)}) async-start(bf16[8,2,5184]{2,1,0:T(2,128)(2,1)} %pad_maximum_fusion), calls=%async_computation | async-start | bytes 335872 | tf_op jit(solution)/shard_map/all_to_all | solution.py:39
  23.6 5.9 %copy-start.2 = (f32[4608]{0:T(1024)S(1)}, f32[4608]{0:T(1024)}, u32[]{:S(2)}) copy-start(f32[4608]{0:T(1024)} %param.11) | copy-start | bytes 55300
  24.1 1.3 %collective-permute-start = (bf16[16,2304]{1,0:T(8,128)(2,1)S(1)}, bf16[16,2304]{1,0:T(8,128)(2,1)S(1)}, u32[]{:S(2)}, u32[]{:S(2)}) collective-permute-start(bf16[16,2304]{1,0:T(8,128)(2,1)S(1)} %dynamic-slice_convert_fusion), channel_id=1, source_target_pairs={{0,1},{1,0},{2,3},{3,2},{4,5},{5,4},{6,7},{7,6},{8,9},{9,8},{10,11... | collective-permute-start | bytes 221192 | tf_op jit(solution)/shard_map/ppermute | solution.py:20
  25.5 6.1 %collective-permute-start.3 = (bf16[16,2304]{1,0:T(8,128)(2,1)S(1)}, bf16[16,2304]{1,0:T(8,128)(2,1)S(1)}, u32[]{:S(2)}, u32[]{:S(2)}) collective-permute-start(bf16[16,2304]{1,0:T(8,128)(2,1)S(1)} %fusion.10), channel_id=1, source_target_pairs={{0,6},{2,4},{4,2},{6,0},{8,14},{10,12},{12,10},{14,8},{1,7},{3,5},... | collective-permute-start | bytes 221192 | tf_op jit(solution)/shard_map/ppermute | solution.py:20
  26.3 5.5 %collective-permute-start.2 = (bf16[16,2304]{1,0:T(8,128)(2,1)S(1)}, bf16[16,2304]{1,0:T(8,128)(2,1)S(1)}, u32[]{:S(2)}, u32[]{:S(2)}) collective-permute-start(bf16[16,2304]{1,0:T(8,128)(2,1)S(1)} %fusion.10), channel_id=1, source_target_pairs={{0,4},{2,6},{4,0},{6,2},{8,12},{10,14},{12,8},{14,10},{1,5},{3,7},... | collective-permute-start | bytes 221192 | tf_op jit(solution)/shard_map/ppermute | solution.py:20
  27.9 4.5 %collective-permute-start.1 = (bf16[16,2304]{1,0:T(8,128)(2,1)S(1)}, bf16[16,2304]{1,0:T(8,128)(2,1)S(1)}, u32[]{:S(2)}, u32[]{:S(2)}) collective-permute-start(bf16[16,2304]{1,0:T(8,128)(2,1)S(1)} %fusion.10), channel_id=1, source_target_pairs={{0,2},{2,0},{4,6},{6,4},{8,10},{10,8},{12,14},{14,12},{1,3},{3,1},... | collective-permute-start | bytes 221192 | tf_op jit(solution)/shard_map/ppermute | solution.py:20
  32.5 5.8 %collective-permute-start.4 = (bf16[16,2304]{1,0:T(8,128)(2,1)S(1)}, bf16[16,2304]{1,0:T(8,128)(2,1)S(1)}, u32[]{:S(2)}, u32[]{:S(2)}) collective-permute-start(bf16[16,2304]{1,0:T(8,128)(2,1)S(1)} %fusion.21), channel_id=1, source_target_pairs={{0,8},{2,10},{4,12},{6,14},{8,0},{10,2},{12,4},{14,6},{1,9},{3,11}... | collective-permute-start | bytes 221192 | tf_op jit(solution)/shard_map/ppermute | solution.py:20
  38.4 1.3 %collective-permute-start.5 = (bf16[16,2304]{1,0:T(8,128)(2,1)S(1)}, bf16[16,2304]{1,0:T(8,128)(2,1)S(1)}, u32[]{:S(2)}, u32[]{:S(2)}) collective-permute-start(bf16[16,2304]{1,0:T(8,128)(2,1)S(1)} %multiply_convert_fusion), channel_id=1, source_target_pairs={{0,1},{1,0},{2,3},{3,2},{4,5},{5,4},{6,7},{7,6},{8,9},{9,8},{10,11... | collective-permute-start | bytes 221192 | tf_op jit(solution)/shard_map/ppermute | solution.py:20

commit v3 on v2

v3 whole, which is shorter than its diff:
```python
import functools

import jax
import jax.numpy as jnp
from jax import lax
from jax.experimental import pallas as pl
from jax.experimental.pallas import tpu as pltpu
from jax.sharding import PartitionSpec as P

SPARSITY = 4.0
SHARP = 4.0
VMEM_BYTES = 16 * 1024 * 1024
PACK_BYTES = 60 * 1024 * 1024
NT = (((1,), (1,)), ((), ()))
TN = (((0,), (0,)), ((), ()))


def whole(space=pltpu.VMEM):
    return pl.BlockSpec(memory_space=space)


def exchange(value, axis, distance):
    size = lax.axis_size(axis)
    return lax.ppermute(value, axis, [(k, k ^ distance) for k in range(size)])


def pack_kernel(cur_hbm, cached_hbm, perm_hbm, out_ref, cur_ref, cached_ref, perm_ref, sems):
    fetches = [
        pltpu.make_async_copy(source, target, sems.at[index])
        for index, (source, target) in enumerate(
            [(cur_hbm, cur_ref), (perm_hbm, perm_ref), (cached_hbm, cached_ref)]
        )
    ]
    for fetch in fetches:
        fetch.start()
    for fetch in fetches:
        fetch.wait()
    dp, own, _ = out_ref.shape
    width = cur_ref.shape[1]
    row_total = cached_ref.shape[0]
    slots = lax.broadcasted_iota(jnp.int32, (row_total, row_total), 0)
    selector = (jnp.broadcast_to(perm_ref[...], slots.shape) == slots).astype(jnp.bfloat16)
    ordered = jnp.dot(selector, cached_ref[...], preferred_element_type=jnp.float32)
    cur = cur_ref[...]
    for peer in range(dp):
        out_ref[peer, :, :width] = cur
        out_ref[peer, :, width:] = ordered[peer * own : (peer + 1) * own].astype(jnp.bfloat16)


def pack(cur_rows, cached_rows, shuffle_perm, dp):
    own, width = cur_rows.shape
    row_total, columns = cached_rows.shape
    return pl.pallas_call(
        pack_kernel,
        out_shape=jax.ShapeDtypeStruct((dp, own, width + columns), jnp.bfloat16),
        in_specs=[whole(pl.ANY)] * 3,
        out_specs=whole(),
        scratch_shapes=[
            pltpu.VMEM((own, width), jnp.bfloat16),
            pltpu.VMEM((row_total, columns), jnp.bfloat16),
            pltpu.VMEM((1, row_total), jnp.int32),
            pltpu.SemaphoreType.DMA((3,)),
        ],
        compiler_params=pltpu.CompilerParams(vmem_limit_bytes=PACK_BYTES),
        name="pack",
    )(cur_rows, cached_rows, shuffle_perm.reshape(1, row_total))


def encode_kernel(
    rows_ref,
    weight_ref,
    bias_ref,
    norms_ref,
    send_ref,
    mine_ref,
    latents_ref,
    gate_ref,
    scales_ref,
    pull_ref,
):
    rows_total, width = rows_ref.shape
    half = width // 2
    batch_rows = rows_total // 2
    core = lax.axis_index("latent")
    projected = lax.dot_general(
        rows_ref[...], weight_ref[...], NT, preferred_element_type=jnp.float32
    )
    rows_f = rows_ref[...].astype(jnp.float32)
    squares = jnp.sum(rows_f * rows_f, axis=1, keepdims=True)
    first = jnp.sum(squares[:batch_rows], axis=0, keepdims=True) / batch_rows
    second = jnp.sum(squares[batch_rows:], axis=0, keepdims=True) / batch_rows
    row = lax.broadcasted_iota(jnp.int32, (rows_total, 1), 0)
    scales = jnp.sqrt(width / jnp.where(row < batch_rows, first, second))
    scales_ref[...] = scales
    sharp = SHARP * (scales * projected + bias_ref[...])
    latents = jax.nn.softplus(sharp) / SHARP
    latents_ref[...] = latents
    gate_ref[...] = jax.nn.sigmoid(sharp)
    counts = jnp.sum(latents, axis=0, keepdims=True)
    pull_ref[...] = SPARSITY / batch_rows * counts / norms_ref[...]
    latents_b = latents.astype(jnp.bfloat16)
    there = pl.multiple_of((1 - core) * half, 128)
    here = pl.multiple_of(core * half, 128)
    send_ref[...] = jnp.dot(
        latents_b, weight_ref[:, pl.ds(there, half)], preferred_element_type=jnp.float32
    ).astype(jnp.bfloat16)
    mine_ref[...] = jnp.dot(
        latents_b, weight_ref[:, pl.ds(here, half)], preferred_element_type=jnp.float32
    )


def encode(rows, weight, enc_bias, norms):
    rows_total, width = rows.shape
    count = weight.shape[0]
    f32 = jnp.float32
    return pl.pallas_call(
        encode_kernel,
        out_shape=(
            jax.ShapeDtypeStruct((rows_total, width // 2), jnp.bfloat16),
            jax.ShapeDtypeStruct((rows_total, width // 2), f32),
            jax.ShapeDtypeStruct((rows_total, count), f32),
            jax.ShapeDtypeStruct((rows_total, count), f32),
            jax.ShapeDtypeStruct((rows_total, 1), f32),
            jax.ShapeDtypeStruct((1, count), f32),
        ),
        in_specs=[whole()] * 4,
        out_specs=[whole()] * 6,
        compiler_params=pltpu.CompilerParams(vmem_limit_bytes=VMEM_BYTES),
        name="encode",
    )(rows, weight, enc_bias.reshape(1, count), norms)


def finish_kernel(
    tile,
    low_ref,
    high_ref,
    rows_ref,
    weight_ref,
    latents_ref,
    gate_ref,
    scales_ref,
    norms_ref,
    pull_ref,
    weight_grad_ref,
    bias_grad_ref,
    staged_ref,
    sems,
):
    rows_total, width = rows_ref.shape
    half = width // 2
    batch_rows = rows_total // 2
    grad_latents = (
        lax.dot_general(
            low_ref[...], weight_ref[:, :half], NT, preferred_element_type=jnp.float32
        )
        + lax.dot_general(
            high_ref[...], weight_ref[:, half:], NT, preferred_element_type=jnp.float32
        )
        + SPARSITY / batch_rows * norms_ref[...]
    )
    grad_pre = grad_latents * gate_ref[...]
    bias_grad_ref[...] = jnp.sum(grad_pre, axis=0, keepdims=True)
    scaled = (grad_pre * scales_ref[...]).astype(jnp.bfloat16)
    left = jnp.concatenate([scaled, latents_ref[...].astype(jnp.bfloat16)], axis=0)
    pull = pull_ref[...]
    copies = []
    for index in range(width // tile):
        start = index * tile
        columns = slice(start, start + tile)
        if start < half:
            grad = low_ref[:, columns]
        else:
            grad = high_ref[:, start - half : start - half + tile]
        right = jnp.concatenate([rows_ref[:, columns], grad], axis=0)
        total = lax.dot_general(left, right, TN, preferred_element_type=jnp.float32)
        total = total + pull * weight_ref[:, columns].astype(jnp.float32)
        staged_ref[:, columns] = total.astype(jnp.bfloat16)
        copy = pltpu.make_async_copy(
            staged_ref.at[:, columns], weight_grad_ref.at[:, columns], sems.at[index]
        )
        copy.start()
        copies.append(copy)
    for copy in copies:
        copy.wait()


def finish(low, high, rows, weight, latents, gate, scales, norms, pull):
    rows_total, width = rows.shape
    count = weight.shape[0]
    tile = 384
    return pl.pallas_call(
        functools.partial(finish_kernel, tile),
        out_shape=(
            jax.ShapeDtypeStruct((count, width), jnp.bfloat16),
            jax.ShapeDtypeStruct((1, count), jnp.float32),
        ),
        in_specs=[whole()] * 9,
        out_specs=[whole(pl.ANY), whole()],
        scratch_shapes=[
            pltpu.VMEM((count, width), jnp.bfloat16),
            pltpu.SemaphoreType.DMA((width // tile,)),
        ],
        compiler_params=pltpu.CompilerParams(vmem_limit_bytes=VMEM_BYTES),
        name="finish",
    )(low, high, rows, weight, latents, gate, scales, norms, pull)


def per_device(cur_rows, cached_rows, shuffle_perm, weight, enc_bias, dec_bias):
    dp = lax.axis_size("dp")
    own, width = cur_rows.shape
    columns = cached_rows.shape[1]
    half = width // 2
    count = weight.shape[0]
    batch_rows = dp * own // 2
    core = lax.axis_index("latent")

    arrived = lax.all_to_all(pack(cur_rows, cached_rows, shuffle_perm, dp), "dp", 0, 0)
    gathered = arrived[:, :, :width].reshape(dp * own, width)
    next_batch = arrived[:, :, width:].transpose(1, 0, 2).reshape(own, dp * columns)

    weight_f = weight.astype(jnp.float32)
    norms = jnp.sqrt(jnp.sum(weight_f * weight_f, axis=1) + 1e-06).reshape(1, count)
    send, mine, latents, gate, scales, pull = encode(gathered, weight, enc_bias, norms)

    total = mine + exchange(send, "latent", 1).astype(jnp.float32)
    corner = min(4, dp)
    sent = total.astype(jnp.bfloat16)
    for distance in range(1, corner):
        total = total + exchange(sent, "dp", distance).astype(jnp.float32)
    distance = corner
    while distance < dp:
        total = total + exchange(total.astype(jnp.bfloat16), "dp", distance).astype(jnp.float32)
        distance *= 2

    target = lax.dynamic_slice_in_dim(gathered, core * half, half, 1).astype(jnp.float32)
    bias = lax.dynamic_slice_in_dim(dec_bias, core * half, half, 0)
    error = total + bias[None, :] - target * scales
    grad_mine = (2.0 / batch_rows * error).astype(jnp.bfloat16)
    grad_other = exchange(grad_mine, "latent", 1)
    low = jnp.where(core == 0, grad_mine, grad_other)
    high = jnp.where(core == 0, grad_other, grad_mine)

    shares = width // (2 * dp)
    offset = lax.axis_index(("dp", "latent")) * shares
    column_sums = jnp.concatenate(
        [jnp.sum(low.astype(jnp.float32), axis=0), jnp.sum(high.astype(jnp.float32), axis=0)]
    )
    dec_bias_grad = lax.dynamic_slice_in_dim(column_sums, offset, shares, 0)

    weight_grad, enc_bias_grad = finish(
        low,
        high,
        gathered,
        weight,
        latents,
        gate,
        scales,
        norms,
        pull.reshape(count, 1),
    )
    return (weight_grad, enc_bias_grad.reshape(count), dec_bias_grad, next_batch)


def solution(mesh):
    return jax.shard_map(
        per_device,
        mesh=mesh,
        in_specs=(
            P(("group", "dp"), None),
            P("group", "dp"),
            P("group"),
            P(("group", "dp", "latent"), None),
            P(("group", "dp", "latent")),
            P("group"),
        ),
        out_specs=(
            P(("group", "dp", "latent"), None),
            P(("group", "dp", "latent")),
            P(("group", "dp", "latent")),
            P(("group", "dp"), None),
        ),
        check_vma=False,
    )
```

time: 44.3 us -> 39.9 us (0.901)
  Pallas kernels: 0 us -> 7.58 us
  matrix products: 7.13 us -> 0 us
  local copies, waits for them, and re-layouts: 3.34 us -> 1.11 us
  waiting for transfers between devices: 17.4 us -> 15.5 us
  between operations: 2.08 us -> 0.75 us
  other arithmetic: 2.54 us -> 3.23 us
    pallas_call x0 -> x3, Pallas kernels: none -> 7.58 us  [the longest x1 4.08 us: finish(): pl.pallas_call(functools.partial(finish_kernel, tile), out_shape=(jax.Sha...]
    dot_general x5 -> x0, matrix products: 7.13 us -> none  [the longest x1 2.43 us: per_device(): jnp.einsum('rd,ld->rl', gathered, weight, preferred_element_type=jnp.floa...]
    all_to_all x1, waiting for transfers between devices: 7.59 us -> 5.36 us  [per_device(): lax.all_to_all(pack(cur_rows, cached_rows, shuffle_perm, dp), 'dp', 0, 0)]
    broadcast_in_dim x2 -> x0, local copies, waits for them, and re-layouts: 0.88 us -> none  [the longest x1 0.8 us: per_device(): jnp.broadcast_to(cur_rows[None], (dp, own, width))]
    reduce_sum x4 -> x2, other arithmetic: 1.45 us -> 2.28 us  [the longest x1 2.21 us: per_device(): jnp.sum(weight_f * weight_f, axis=1) + 1e-06]
    unnamed x6, local copies, waits for them, and re-layouts: 0.73 us -> 0.01 us
    dynamic_slice x1 -> x0, local copies, waits for them, and re-layouts: 0.65 us -> none  [per_device(): dec_bias_grad = lax.dynamic_slice_in_dim(column_sums, offset, shares, 0)]
  transfers between devices with their start and end apart: 7 -> 7, of which waited for: 7 -> 7; matrix products, arithmetic and copies ran while one was open for 3% -> 8% of each run, Pallas kernels for 0% -> 0%
where the time goes in v3:
time: 39.9 us; the launch traced here: 39.6 us
  waiting for transfers between devices  15.5 us (39%)
  starting transfers between devices  11.4 us (29%)
  Pallas kernels  7.58 us (19%)
  other arithmetic  3.23 us (8%)
  local copies, waits for them, and re-layouts  1.11 us (3%)
  between operations  0.75 us (2%)
    ppermute x6, waiting for transfers between devices, exchange(): return lax.ppermute(value, axis, [(k, k ^ distance) for k in range(size)])  10.1 us
    all_to_all x1, starting transfers between devices, per_device(): lax.all_to_all(pack(cur_rows, cached_rows, shuffle_perm, dp), 'dp', 0, 0)  7.26 us
    all_to_all x1, waiting for transfers between devices, per_device(): lax.all_to_all(pack(cur_rows, cached_rows, shuffle_perm, dp), 'dp', 0, 0)  5.36 us
    ppermute x6, starting transfers between devices, exchange(): return lax.ppermute(value, axis, [(k, k ^ distance) for k in range(size)])  4.18 us
    pallas_call x1, Pallas kernels, finish(): pl.pallas_call(functools.partial(finish_kernel, tile), out_shape=(jax.Sha...  4.08 us
    reduce_sum x1, other arithmetic, per_device(): jnp.sum(weight_f * weight_f, axis=1) + 1e-06  2.21 us
    pallas_call x1, Pallas kernels, encode(): pl.pallas_call(encode_kernel, out_shape=(jax.ShapeDtypeStruct((rows_total...  1.77 us
    pallas_call x1, Pallas kernels, pack(): pl.pallas_call(pack_kernel, out_shape=jax.ShapeDtypeStruct((dp, own, widt...  1.73 us
  transfers between devices with their start and end apart: 7, of which 7 were waited for; matrix products, arithmetic and copies ran while one was open for 8% of the time, Pallas kernels for 0%

profile of v3, /device:TPU:0, one launch (start us, length us, event | category | flops | bytes accessed | tf_op | source)
XLA Modules:
  0.0 39.6 jit_solution(12470728400066206888)
XLA Ops:
  0.6 0.0 copy-start
  0.6 0.0 copy-start.1
  0.7 1.7 %pack.1 = bf16[8,2,5184]{2,1,0:T(2,128)(2,1)} custom-call(bf16[2,4608]{1,0:T(2,128)(2,1)} %cur_hbm.1, bf16[16,576]{1,0:T(8,128)(2,1)} %cached_hbm.1, s32[1,16]{1,0:T(1,128)} %bitcast.11), custom_call_target="tpu_custom_call" | custom-call | tf_op jit(solution)/shard_map/pack/pallas_call | solution.py:53
  2.4 7.3 %all-to-all-start = ((bf16[8,2,5184]{2,1,0:T(2,128)(2,1)}), bf16[8,2,5184]{2,1,0:T(2,128)(2,1)S(1)}, u32[]{:S(2)}, u32[]{:S(2)}) async-start(bf16[8,2,5184]{2,1,0:T(2,128)(2,1)} %pack.1), calls=%async_computation | async-start | bytes 335872 | tf_op jit(solution)/shard_map/all_to_all | solution.py:217
  9.7 2.2 %multiply_reduce_fusion = f32[256]{0:T(256)S(1)} fusion(bf16[256,4608]{1,0:T(8,128)(2,1)} %weight_ref.3), kind=kLoop, calls=%fused_computation | loop fusion | flops 3538688 | bytes 2360320 | tf_op jit(solution)/shard_map/reduce_sum | solution.py:222
  11.9 0.0 copy-start.2
  11.9 5.4 %all-to-all-done = bf16[8,2,5184]{2,1,0:T(2,128)(2,1)S(1)} async-done(((bf16[8,2,5184]{2,1,0:T(2,128)(2,1)}), bf16[8,2,5184]{2,1,0:T(2,128)(2,1)S(1)}, u32[]{:S(2)}, u32[]{:S(2)}) %all-to-all-start) | async-done | bytes 165920 | tf_op jit(solution)/shard_map/all_to_all | solution.py:217
  17.2 0.1 slice.8
  17.4 0.1 reshape.42.rows_ref
  17.4 0.0 copy-done
  17.4 0.0 copy-done.1
  17.4 1.8 %encode.1 = (bf16[16,2304]{1,0:T(8,128)(2,1)S(1)}, f32[16,2304]{1,0:T(8,128)S(1)}, f32[16,256]{1,0:T(8,128)S(1)}, f32[16,256]{1,0:T(8,128)S(1)}, f32[16,1]{1,0:T(8,128)S(1)}, /*index=5*/f32[1,256]{1,0:T(1,128)S(1)}) custom-call(bf16[16,4608]{1,0:T(8,128)(2,1)S(1)} %reshape.42.rows_ref, bf16[256,4608]{1,0:T(8,128)(2,1)S(1)} %copy-done, f32[1,256]{1,0:T(1,128)S(1)} %bitcast.9, ...), custom_call_target="tpu_custom_call" | custom-call | tf_op jit(solution)/shard_map/encode/pallas_call | solution.py:116
  19.2 0.0 collective-permute-start
  19.2 1.3 %collective-permute-done = bf16[16,2304]{1,0:T(8,128)(2,1)S(1)} collective-permute-done((bf16[16,2304]{1,0:T(8,128)(2,1)S(1)}, bf16[16,2304]{1,0:T(8,128)(2,1)S(1)}, u32[]{:S(2)}, u32[]{:S(2)}) %collective-permute-start) | collective-permute-done | bytes 73760 | tf_op jit(solution)/shard_map/ppermute | solution.py:24
  20.5 0.9 %collective-permute-start.3 = (bf16[16,2304]{1,0:T(8,128)(2,1)S(1)}, bf16[16,2304]{1,0:T(8,128)(2,1)S(1)}, u32[]{:S(2)}, u32[]{:S(2)}) collective-permute-start(bf16[16,2304]{1,0:T(8,128)(2,1)S(1)} %fusion), channel_id=1, source_target_pairs={{0,6},{2,4},{4,2},{6,0},{8,14},{10,12},{12,10},{14,8},{1,7},{3,5},... | collective-permute-start | bytes 221192 | tf_op jit(solution)/shard_map/ppermute | solution.py:24
  21.4 1.6 %collective-permute-start.2 = (bf16[16,2304]{1,0:T(8,128)(2,1)S(1)}, bf16[16,2304]{1,0:T(8,128)(2,1)S(1)}, u32[]{:S(2)}, u32[]{:S(2)}) collective-permute-start(bf16[16,2304]{1,0:T(8,128)(2,1)S(1)} %fusion), channel_id=1, source_target_pairs={{0,4},{2,6},{4,0},{6,2},{8,12},{10,14},{12,8},{14,10},{1,5},{3,7},... | collective-permute-start | bytes 221192 | tf_op jit(solution)/shard_map/ppermute | solution.py:24
  23.0 1.1 %collective-permute-start.1 = (bf16[16,2304]{1,0:T(8,128)(2,1)S(1)}, bf16[16,2304]{1,0:T(8,128)(2,1)S(1)}, u32[]{:S(2)}, u32[]{:S(2)}) collective-permute-start(bf16[16,2304]{1,0:T(8,128)(2,1)S(1)} %fusion), channel_id=1, source_target_pairs={{0,2},{2,0},{4,6},{6,4},{8,10},{10,8},{12,14},{14,12},{1,3},{3,1},... | collective-permute-start | bytes 221192 | tf_op jit(solution)/shard_map/ppermute | solution.py:24
  24.1 2.5 %collective-permute-done.3 = bf16[16,2304]{1,0:T(8,128)(2,1)S(1)} collective-permute-done((bf16[16,2304]{1,0:T(8,128)(2,1)S(1)}, bf16[16,2304]{1,0:T(8,128)(2,1)S(1)}, u32[]{:S(2)}, u32[]{:S(2)}) %collective-permute-start.3) | collective-permute-done | bytes 73760 | tf_op jit(solution)/shard_map/ppermute | solution.py:24
  26.6 0.3 collective-permute-done.2
  26.9 0.6 %collective-permute-done.1 = bf16[16,2304]{1,0:T(8,128)(2,1)S(1)} collective-permute-done((bf16[16,2304]{1,0:T(8,128)(2,1)S(1)}, bf16[16,2304]{1,0:T(8,128)(2,1)S(1)}, u32[]{:S(2)}, u32[]{:S(2)}) %collective-permute-start.1) | collective-permute-done | bytes 73760 | tf_op jit(solution)/shard_map/ppermute | solution.py:24
  27.5 0.5 %collective-permute-start.4 = (bf16[16,2304]{1,0:T(8,128)(2,1)S(1)}, bf16[16,2304]{1,0:T(8,128)(2,1)S(1)}, u32[]{:S(2)}, u32[]{:S(2)}) collective-permute-start(bf16[16,2304]{1,0:T(8,128)(2,1)S(1)} %fusion.2), channel_id=1, source_target_pairs={{0,8},{2,10},{4,12},{6,14},{8,0},{10,2},{12,4},{14,6},{1,9},{3,11}... | collective-permute-start | bytes 221192 | tf_op jit(solution)/shard_map/ppermute | solution.py:24
  28.1 0.0 copy-done.2
  28.1 0.1 dynamic_slice.9
  28.1 0.1 reduce
  28.3 5.1 %collective-permute-done.4 = bf16[16,2304]{1,0:T(8,128)(2,1)S(1)} collective-permute-done((bf16[16,2304]{1,0:T(8,128)(2,1)S(1)}, bf16[16,2304]{1,0:T(8,128)(2,1)S(1)}, u32[]{:S(2)}, u32[]{:S(2)}) %collective-permute-start.4) | collective-permute-done | bytes 73760 | tf_op jit(solution)/shard_map/ppermute | solution.py:24
  33.3 0.1 multiply_convert_fusion
  33.4 0.1 collective-permute-start.5
  33.6 0.7 %reshape.46 = bf16[2,4608]{1,0:T(2,128)(2,1)} reshape(bf16[2,8,576]{2,1,0:T(8,128)(2,1)S(1)} %copy.11) | data formatting | bytes 36864 | tf_op jit(solution)/shard_map/reshape | solution.py:219
  34.3 0.1 copy.10.pull_ref
  34.4 0.4 collective-permute-done.5
  34.8 0.1 convert_reduce_fusion
  34.8 0.7 %fusion.1 = f32[288]{0:T(512)} fusion(s32[]{:T(128)S(6)} %select_n.23, f32[2304]{0:T(1024)S(1)} %get-tuple-element.24, f32[2304]{0:T(1024)S(1)} %get-tuple-element.20), kind=kLoop, calls=%fused_computation.12 | loop fusion | flops 288 | bytes 19588 | tf_op jit(solution)/shard_map/concatenate | solution.py:245
  35.5 4.1 %finish.1 = (bf16[256,4608]{1,0:T(8,128)(2,1)}, f32[1,256]{1,0:T(1,128)}) custom-call(bf16[16,2304]{1,0:T(8,128)(2,1)S(1)} %get-tuple-element.25.low_ref, bf16[16,2304]{1,0:T(8,128)(2,1)S(1)} %get-tuple-element.21.high_ref, bf16[16,4608]{1,0:T(8,128)(2,1)S(1)} %reshape.42.rows_ref, bf16[256,4608]{1,0:T(8,128)(2,1)S(1)} %copy-done, ...), custom_call_target="tpu_custom_call" | custom-call | tf_op jit(solution)/shard_map/finish/pallas_call | solution.py:191
  (5 shorter events, 0.1 us)
Async XLA Ops:
  0.6 16.8 %copy-start = (bf16[256,4608]{1,0:T(8,128)(2,1)S(1)}, bf16[256,4608]{1,0:T(8,128)(2,1)}, u32[]{:S(2)}) copy-start(bf16[256,4608]{1,0:T(8,128)(2,1)} %weight_ref.3) | copy-start | bytes 7077892
  0.6 16.8 %copy-start.1 = (f32[256]{0:T(256)S(1)}, f32[256]{0:T(256)}, u32[]{:S(2)}) copy-start(f32[256]{0:T(256)} %param.10) | copy-start | bytes 3076
  2.4 14.9 %all-to-all-start = ((bf16[8,2,5184]{2,1,0:T(2,128)(2,1)}), bf16[8,2,5184]{2,1,0:T(2,128)(2,1)S(1)}, u32[]{:S(2)}, u32[]{:S(2)}) async-start(bf16[8,2,5184]{2,1,0:T(2,128)(2,1)} %pack.1), calls=%async_computation | async-start | bytes 335872 | tf_op jit(solution)/shard_map/all_to_all | solution.py:217
  11.9 16.2 %copy-start.2 = (f32[4608]{0:T(1024)S(1)}, f32[4608]{0:T(1024)}, u32[]{:S(2)}) copy-start(f32[4608]{0:T(1024)} %param.11) | copy-start | bytes 55300
  19.2 1.3 %collective-permute-start = (bf16[16,2304]{1,0:T(8,128)(2,1)S(1)}, bf16[16,2304]{1,0:T(8,128)(2,1)S(1)}, u32[]{:S(2)}, u32[]{:S(2)}) collective-permute-start(bf16[16,2304]{1,0:T(8,128)(2,1)S(1)} %get-tuple-element.13), channel_id=1, source_target_pairs={{0,1},{1,0},{2,3},{3,2},{4,5},{5,4},{6,7},{7,6},{8,9},{9,8},{10,11... | collective-permute-start | bytes 221192 | tf_op jit(solution)/shard_map/ppermute | solution.py:24
  20.5 6.1 %collective-permute-start.3 = (bf16[16,2304]{1,0:T(8,128)(2,1)S(1)}, bf16[16,2304]{1,0:T(8,128)(2,1)S(1)}, u32[]{:S(2)}, u32[]{:S(2)}) collective-permute-start(bf16[16,2304]{1,0:T(8,128)(2,1)S(1)} %fusion), channel_id=1, source_target_pairs={{0,6},{2,4},{4,2},{6,0},{8,14},{10,12},{12,10},{14,8},{1,7},{3,5},... | collective-permute-start | bytes 221192 | tf_op jit(solution)/shard_map/ppermute | solution.py:24
  21.4 5.5 %collective-permute-start.2 = (bf16[16,2304]{1,0:T(8,128)(2,1)S(1)}, bf16[16,2304]{1,0:T(8,128)(2,1)S(1)}, u32[]{:S(2)}, u32[]{:S(2)}) collective-permute-start(bf16[16,2304]{1,0:T(8,128)(2,1)S(1)} %fusion), channel_id=1, source_target_pairs={{0,4},{2,6},{4,0},{6,2},{8,12},{10,14},{12,8},{14,10},{1,5},{3,7},... | collective-permute-start | bytes 221192 | tf_op jit(solution)/shard_map/ppermute | solution.py:24
  23.0 4.5 %collective-permute-start.1 = (bf16[16,2304]{1,0:T(8,128)(2,1)S(1)}, bf16[16,2304]{1,0:T(8,128)(2,1)S(1)}, u32[]{:S(2)}, u32[]{:S(2)}) collective-permute-start(bf16[16,2304]{1,0:T(8,128)(2,1)S(1)} %fusion), channel_id=1, source_target_pairs={{0,2},{2,0},{4,6},{6,4},{8,10},{10,8},{12,14},{14,12},{1,3},{3,1},... | collective-permute-start | bytes 221192 | tf_op jit(solution)/shard_map/ppermute | solution.py:24
  27.5 5.8 %collective-permute-start.4 = (bf16[16,2304]{1,0:T(8,128)(2,1)S(1)}, bf16[16,2304]{1,0:T(8,128)(2,1)S(1)}, u32[]{:S(2)}, u32[]{:S(2)}) collective-permute-start(bf16[16,2304]{1,0:T(8,128)(2,1)S(1)} %fusion.2), channel_id=1, source_target_pairs={{0,8},{2,10},{4,12},{6,14},{8,0},{10,2},{12,4},{14,6},{1,9},{3,11}... | collective-permute-start | bytes 221192 | tf_op jit(solution)/shard_map/ppermute | solution.py:24
  33.4 1.3 %collective-permute-start.5 = (bf16[16,2304]{1,0:T(8,128)(2,1)S(1)}, bf16[16,2304]{1,0:T(8,128)(2,1)S(1)}, u32[]{:S(2)}, u32[]{:S(2)}) collective-permute-start(bf16[16,2304]{1,0:T(8,128)(2,1)S(1)} %multiply_convert_fusion), channel_id=1, source_target_pairs={{0,1},{1,0},{2,3},{3,2},{4,5},{5,4},{6,7},{7,6},{8,9},{9,8},{10,11... | collective-permute-start | bytes 221192 | tf_op jit(solution)/shard_map/ppermute | solution.py:24

commit v4 on v3

v4 whole, which is shorter than its diff:
```python
import functools

import jax
import jax.numpy as jnp
from jax import lax
from jax.experimental import pallas as pl
from jax.experimental.pallas import tpu as pltpu
from jax.sharding import PartitionSpec as P

SPARSITY = 4.0
SHARP = 4.0
VMEM_BYTES = 16 * 1024 * 1024
PACK_BYTES = 60 * 1024 * 1024
NT = (((1,), (1,)), ((), ()))
TN = (((0,), (0,)), ((), ()))


def whole(space=pltpu.VMEM):
    return pl.BlockSpec(memory_space=space)


def exchange(value, axis, distance):
    size = lax.axis_size(axis)
    return lax.ppermute(value, axis, [(k, k ^ distance) for k in range(size)])


def core_columns(half):
    core = lax.axis_index("latent")
    here = pl.ds(pl.multiple_of(core * half, 128), half)
    there = pl.ds(pl.multiple_of((1 - core) * half, 128), half)
    return here, there


def pack_kernel(cur_hbm, cached_hbm, perm_hbm, out_hbm, cached_ref, perm_ref, ordered_ref, sems):
    dp, own, _ = out_hbm.shape
    width = cur_hbm.shape[1]
    row_total, columns = cached_ref.shape
    fetches = [
        pltpu.make_async_copy(cached_hbm, cached_ref, sems.at[0]),
        pltpu.make_async_copy(perm_hbm, perm_ref, sems.at[1]),
    ]
    for fetch in fetches:
        fetch.start()
    spreads = [
        pltpu.make_async_copy(cur_hbm, out_hbm.at[peer, :, pl.ds(0, width)], sems.at[3 + peer])
        for peer in range(dp)
    ]
    for spread in spreads:
        spread.start()
    for fetch in fetches:
        fetch.wait()
    slots = lax.broadcasted_iota(jnp.int32, (row_total, row_total), 0)
    selector = (jnp.broadcast_to(perm_ref[...], slots.shape) == slots).astype(jnp.bfloat16)
    ordered = jnp.dot(selector, cached_ref[...], preferred_element_type=jnp.float32)
    for peer in range(dp):
        ordered_ref[peer] = ordered[peer * own : (peer + 1) * own].astype(jnp.bfloat16)
    last = pltpu.make_async_copy(
        ordered_ref, out_hbm.at[:, :, pl.ds(width, columns)], sems.at[2]
    )
    last.start()
    for spread in spreads:
        spread.wait()
    last.wait()


def pack(cur_rows, cached_rows, shuffle_perm, dp):
    own, width = cur_rows.shape
    row_total, columns = cached_rows.shape
    return pl.pallas_call(
        pack_kernel,
        out_shape=jax.ShapeDtypeStruct((dp, own, width + columns), jnp.bfloat16),
        in_specs=[whole(pl.ANY)] * 3,
        out_specs=whole(pl.ANY),
        scratch_shapes=[
            pltpu.VMEM((row_total, columns), jnp.bfloat16),
            pltpu.VMEM((1, row_total), jnp.int32),
            pltpu.VMEM((dp, own, columns), jnp.bfloat16),
            pltpu.SemaphoreType.DMA((3 + dp,)),
        ],
        compiler_params=pltpu.CompilerParams(vmem_limit_bytes=PACK_BYTES),
        name="pack",
    )(cur_rows, cached_rows, shuffle_perm.reshape(1, row_total))


def encode_kernel(rows_ref, weight_ref, bias_ref, send_ref, latents_ref, sharp_ref, scales_ref):
    rows_total, width = rows_ref.shape
    batch_rows = rows_total // 2
    projected = lax.dot_general(
        rows_ref[...], weight_ref[...], NT, preferred_element_type=jnp.float32
    )
    rows_f = rows_ref[...].astype(jnp.float32)
    squares = jnp.sum(rows_f * rows_f, axis=1, keepdims=True)
    first = jnp.sum(squares[:batch_rows], axis=0, keepdims=True) / batch_rows
    second = jnp.sum(squares[batch_rows:], axis=0, keepdims=True) / batch_rows
    row = lax.broadcasted_iota(jnp.int32, (rows_total, 1), 0)
    scales = jnp.sqrt(width / jnp.where(row < batch_rows, first, second))
    scales_ref[...] = scales
    sharp = SHARP * (scales * projected + bias_ref[...])
    latents = jax.nn.softplus(sharp) / SHARP
    sharp_ref[...] = sharp
    latents_ref[...] = latents
    _, there = core_columns(width // 2)
    send_ref[...] = jnp.dot(
        latents.astype(jnp.bfloat16), weight_ref[:, there], preferred_element_type=jnp.float32
    ).astype(jnp.bfloat16)


def encode(rows, weight, enc_bias):
    rows_total, width = rows.shape
    count = weight.shape[0]
    f32 = jnp.float32
    return pl.pallas_call(
        encode_kernel,
        out_shape=(
            jax.ShapeDtypeStruct((rows_total, width // 2), jnp.bfloat16),
            jax.ShapeDtypeStruct((rows_total, count), f32),
            jax.ShapeDtypeStruct((rows_total, count), f32),
            jax.ShapeDtypeStruct((rows_total, 1), f32),
        ),
        in_specs=[whole()] * 3,
        out_specs=[whole()] * 4,
        compiler_params=pltpu.CompilerParams(vmem_limit_bytes=VMEM_BYTES),
        name="encode",
    )(rows, weight, enc_bias.reshape(1, count))


def keep_kernel(latents_ref, sharp_ref, weight_ref, norms_ref, mine_ref, gate_ref, pull_ref):
    rows_total = latents_ref.shape[0]
    half = weight_ref.shape[1] // 2
    latents = latents_ref[...]
    here, _ = core_columns(half)
    mine_ref[...] = jnp.dot(
        latents.astype(jnp.bfloat16), weight_ref[:, here], preferred_element_type=jnp.float32
    )
    gate_ref[...] = jax.nn.sigmoid(sharp_ref[...])
    counts = jnp.sum(latents, axis=0, keepdims=True)
    pull_ref[...] = SPARSITY / (rows_total // 2) * counts / norms_ref[...]


def keep(latents, sharp, weight, norms):
    rows_total, count = latents.shape
    width = weight.shape[1]
    f32 = jnp.float32
    return pl.pallas_call(
        keep_kernel,
        out_shape=(
            jax.ShapeDtypeStruct((rows_total, width // 2), f32),
            jax.ShapeDtypeStruct((rows_total, count), f32),
            jax.ShapeDtypeStruct((1, count), f32),
        ),
        in_specs=[whole()] * 4,
        out_specs=[whole()] * 3,
        compiler_params=pltpu.CompilerParams(vmem_limit_bytes=VMEM_BYTES),
        cost_estimate=pl.CostEstimate(
            flops=rows_total * count * width, bytes_accessed=count * width, transcendentals=0
        ),
        name="keep",
    )(latents, sharp, weight, norms)


def early_kernel(grad_ref, weight_ref, norms_ref, out_ref):
    here, _ = core_columns(weight_ref.shape[1] // 2)
    batch_rows = grad_ref.shape[0] // 2
    out_ref[...] = (
        lax.dot_general(
            grad_ref[...], weight_ref[:, here], NT, preferred_element_type=jnp.float32
        )
        + SPARSITY / batch_rows * norms_ref[...]
    )


def early(grad_mine, weight, norms):
    rows_total, half = grad_mine.shape
    count = weight.shape[0]
    return pl.pallas_call(
        early_kernel,
        out_shape=jax.ShapeDtypeStruct((rows_total, count), jnp.float32),
        in_specs=[whole()] * 3,
        out_specs=whole(),
        compiler_params=pltpu.CompilerParams(vmem_limit_bytes=VMEM_BYTES),
        cost_estimate=pl.CostEstimate(
            flops=2 * rows_total * count * half, bytes_accessed=count * half, transcendentals=0
        ),
        name="early",
    )(grad_mine, weight, norms)


def finish_kernel(
    tile,
    span,
    grad_ref,
    early_ref,
    rows_ref,
    weight_ref,
    latents_ref,
    gate_ref,
    scales_ref,
    pull_ref,
    weight_grad_hbm,
    bias_grad_hbm,
    dec_grad_hbm,
    staged_ref,
    bias_ref,
    dec_ref,
    sums_ref,
    left_ref,
    sems,
):
    rows_total, width = rows_ref.shape
    shares = dec_grad_hbm.shape[0]
    count = width // tile
    core = lax.axis_index("latent")
    _, there = core_columns(width // 2)
    grad_latents = early_ref[...] + lax.dot_general(
        grad_ref[:, there], weight_ref[:, there], NT, preferred_element_type=jnp.float32
    )
    grad_pre = grad_latents * gate_ref[...]
    bias_ref[...] = jnp.sum(grad_pre, axis=0, keepdims=True)
    bias_copy = pltpu.make_async_copy(bias_ref, bias_grad_hbm, sems.at[count])
    bias_copy.start()
    left = jnp.concatenate([grad_pre * scales_ref[...], latents_ref[...]], axis=0)
    left_ref[...] = left.T.astype(jnp.bfloat16)

    sums = jnp.sum(grad_ref[...].astype(jnp.float32), axis=0, keepdims=True)
    sums_ref[:, :width] = jnp.broadcast_to(sums, (8, width))
    sums_ref[:, width:] = jnp.zeros((8, span), jnp.float32)
    offset = lax.axis_index(("dp", "latent")) * shares
    lead = lax.rem(offset, 128)
    window = sums_ref[:, pl.ds(pl.multiple_of(offset - lead, 128), span)]
    window = pltpu.roll(window, lax.rem(span - lead, span), 1)
    dec_ref[...] = window[0, :shares]
    dec_copy = pltpu.make_async_copy(dec_ref, dec_grad_hbm, sems.at[count + 1])
    dec_copy.start()

    copies = [
        pltpu.make_async_copy(
            staged_ref.at[:, pl.ds(index * tile, tile)],
            weight_grad_hbm.at[:, pl.ds(index * tile, tile)],
            sems.at[index],
        )
        for index in range(count)
    ]

    @pl.loop(0, 1 + core // 2)
    def _(_):
        pull = pull_ref[...]
        for index in range(count):
            columns = slice(index * tile, (index + 1) * tile)
            right = jnp.concatenate([rows_ref[:, columns], grad_ref[:, columns]], axis=0)
            total = jnp.dot(left_ref[...], right, preferred_element_type=jnp.float32)
            total = total + pull * weight_ref[:, columns].astype(jnp.float32)
            staged_ref[:, columns] = total.astype(jnp.bfloat16)
            copies[index].start()

    for copy in copies:
        copy.wait()
    bias_copy.wait()
    dec_copy.wait()


def finish(grad_out, early_sum, rows, weight, latents, gate, scales, pull, shares):
    rows_total, width = rows.shape
    count = weight.shape[0]
    tile = 768
    span = (shares + 127 + 127) // 128 * 128
    f32 = jnp.float32
    return pl.pallas_call(
        functools.partial(finish_kernel, tile, span),
        out_shape=(
            jax.ShapeDtypeStruct((count, width), jnp.bfloat16),
            jax.ShapeDtypeStruct((1, count), f32),
            jax.ShapeDtypeStruct((shares,), f32),
        ),
        in_specs=[whole()] * 8,
        out_specs=[whole(pl.ANY)] * 3,
        scratch_shapes=[
            pltpu.VMEM((count, width), jnp.bfloat16),
            pltpu.VMEM((1, count), f32),
            pltpu.VMEM((shares,), f32),
            pltpu.VMEM((8, width + span), f32),
            pltpu.VMEM((count, 2 * rows_total), jnp.bfloat16),
            pltpu.SemaphoreType.DMA((width // tile + 2,)),
        ],
        compiler_params=pltpu.CompilerParams(vmem_limit_bytes=VMEM_BYTES),
        name="finish",
    )(grad_out, early_sum, rows, weight, latents, gate, scales, pull)


def per_device(cur_rows, cached_rows, shuffle_perm, weight, enc_bias, dec_bias):
    dp = lax.axis_size("dp")
    own, width = cur_rows.shape
    columns = cached_rows.shape[1]
    half = width // 2
    count = weight.shape[0]
    batch_rows = dp * own // 2
    core = lax.axis_index("latent")

    arrived = lax.all_to_all(pack(cur_rows, cached_rows, shuffle_perm, dp), "dp", 0, 0)
    gathered = arrived[:, :, :width].reshape(dp * own, width)
    next_batch = arrived[:, :, width:].transpose(1, 0, 2).reshape(own, dp * columns)

    weight_f = weight.astype(jnp.float32)
    norms = jnp.sqrt(jnp.sum(weight_f * weight_f, axis=1) + 1e-06).reshape(1, count)
    send, latents, sharp, scales = encode(gathered, weight, enc_bias)
    came = exchange(send, "latent", 1)
    mine, gate, pull = keep(latents, sharp, weight, norms)

    total = mine + came.astype(jnp.float32)
    corner = min(4, dp)
    sent = total.astype(jnp.bfloat16)
    for distance in range(1, corner):
        total = total + exchange(sent, "dp", distance).astype(jnp.float32)
    distance = corner
    while distance < dp:
        total = total + exchange(total.astype(jnp.bfloat16), "dp", distance).astype(jnp.float32)
        distance *= 2

    target = lax.dynamic_slice_in_dim(gathered, core * half, half, 1).astype(jnp.float32)
    bias = lax.dynamic_slice_in_dim(dec_bias, core * half, half, 0)
    error = total + bias[None, :] - target * scales
    grad_mine = (2.0 / batch_rows * error).astype(jnp.bfloat16)
    grad_other = exchange(grad_mine, "latent", 1)
    early_sum = early(grad_mine, weight, norms)
    low = jnp.where(core == 0, grad_mine, grad_other)
    high = jnp.where(core == 0, grad_other, grad_mine)
    grad_out = jnp.concatenate([low, high], axis=1)

    shares = width // (2 * dp)
    weight_grad, enc_bias_grad, dec_bias_grad = finish(
        grad_out,
        early_sum,
        gathered,
        weight,
        latents,
        gate,
        scales,
        pull.reshape(count, 1),
        shares,
    )
    return (weight_grad, enc_bias_grad.reshape(count), dec_bias_grad, next_batch)


def solution(mesh):
    return jax.shard_map(
        per_device,
        mesh=mesh,
        in_specs=(
            P(("group", "dp"), None),
            P("group", "dp"),
            P("group"),
            P(("group", "dp", "latent"), None),
            P(("group", "dp", "latent")),
            P("group"),
        ),
        out_specs=(
            P(("group", "dp", "latent"), None),
            P(("group", "dp", "latent")),
            P(("group", "dp", "latent")),
            P(("group", "dp"), None),
        ),
        check_vma=False,
    )
```

time: 39.9 us -> 41 us (1.028)
  Pallas kernels: 7.58 us -> 9.97 us
  waiting for transfers between devices: 15.5 us -> 14.8 us
  other arithmetic: 3.23 us -> 2.55 us
    pallas_call x1, Pallas kernels: 1.73 us -> 5.67 us  [pack(): pl.pallas_call(pack_kernel, out_shape=jax.ShapeDtypeStruct((dp, own, widt...]
    pallas_call x1 -> x3, Pallas kernels: 4.08 us -> 3.04 us  [the longest x1 2.33 us: finish(): pl.pallas_call(functools.partial(finish_kernel, tile, span), out_shape=(j...]
    ppermute x6, waiting for transfers between devices: 10.1 us -> 9.44 us  [exchange(): return lax.ppermute(value, axis, [(k, k ^ distance) for k in range(size)])]
    concatenate x1, other arithmetic: 0.67 us -> 0.01 us  [per_device(): grad_out = jnp.concatenate([low, high], axis=1)]
    pallas_call x1, Pallas kernels: 1.77 us -> 1.25 us  [encode(): pl.pallas_call(encode_kernel, out_shape=(jax.ShapeDtypeStruct((rows_total...]
  transfers between devices with their start and end apart: 7 -> 7, of which waited for: 7 -> 6; matrix products, arithmetic and copies ran while one was open for 8% -> 8% of each run, Pallas kernels for 0% -> 2%
where the time goes in v4:
time: 41 us; the launch traced here: 40.7 us
  waiting for transfers between devices  14.8 us (36%)
  starting transfers between devices  11.5 us (28%)
  Pallas kernels  9.97 us (24%)
  other arithmetic  2.55 us (6%)
  local copies, waits for them, and re-layouts  1.11 us (3%)
  between operations  0.77 us (2%)
    ppermute x6, waiting for transfers between devices, exchange(): return lax.ppermute(value, axis, [(k, k ^ distance) for k in range(size)])  9.44 us
    all_to_all x1, starting transfers between devices, per_device(): lax.all_to_all(pack(cur_rows, cached_rows, shuffle_perm, dp), 'dp', 0, 0)  7.26 us
    pallas_call x1, Pallas kernels, pack(): pl.pallas_call(pack_kernel, out_shape=jax.ShapeDtypeStruct((dp, own, widt...  5.67 us
    all_to_all x1, waiting for transfers between devices, per_device(): lax.all_to_all(pack(cur_rows, cached_rows, shuffle_perm, dp), 'dp', 0, 0)  5.38 us
    ppermute x6, starting transfers between devices, exchange(): return lax.ppermute(value, axis, [(k, k ^ distance) for k in range(size)])  4.2 us
    pallas_call x1, Pallas kernels, finish(): pl.pallas_call(functools.partial(finish_kernel, tile, span), out_shape=(j...  2.33 us
    reduce_sum x1, other arithmetic, per_device(): jnp.sum(weight_f * weight_f, axis=1) + 1e-06  2.21 us
    pallas_call x1, Pallas kernels, encode(): pl.pallas_call(encode_kernel, out_shape=(jax.ShapeDtypeStruct((rows_total...  1.25 us
  transfers between devices with their start and end apart: 7, of which 6 were waited for; matrix products, arithmetic and copies ran while one was open for 8% of the time, Pallas kernels for 2%

profile of v4, /device:TPU:0, one launch (start us, length us, event | category | flops | bytes accessed | tf_op | source)
XLA Modules:
  0.0 40.7 jit_solution(13558527628760328614)
XLA Ops:
  0.6 0.0 copy-start
  0.6 0.0 copy-start.1
  0.7 5.7 %pack.1 = bf16[8,2,5184]{2,1,0:T(2,128)(2,1)} custom-call(bf16[2,4608]{1,0:T(2,128)(2,1)} %cur_hbm.1, bf16[16,576]{1,0:T(8,128)(2,1)} %cached_hbm.1, s32[1,16]{1,0:T(1,128)} %bitcast.11), custom_call_target="tpu_custom_call" | custom-call | tf_op jit(solution)/shard_map/pack/pallas_call | solution.py:69
  6.3 7.3 %all-to-all-start = ((bf16[8,2,5184]{2,1,0:T(2,128)(2,1)}), bf16[8,2,5184]{2,1,0:T(2,128)(2,1)S(1)}, u32[]{:S(2)}, u32[]{:S(2)}) async-start(bf16[8,2,5184]{2,1,0:T(2,128)(2,1)} %pack.1), calls=%async_computation | async-start | bytes 335872 | tf_op jit(solution)/shard_map/all_to_all | solution.py:298
  13.6 2.2 %multiply_reduce_fusion = f32[256]{0:T(256)S(1)} fusion(bf16[256,4608]{1,0:T(8,128)(2,1)} %weight_ref.7), kind=kLoop, calls=%fused_computation | loop fusion | flops 3538688 | bytes 2360320 | tf_op jit(solution)/shard_map/reduce_sum | solution.py:303
  15.8 5.4 %all-to-all-done = bf16[8,2,5184]{2,1,0:T(2,128)(2,1)S(1)} async-done(((bf16[8,2,5184]{2,1,0:T(2,128)(2,1)}), bf16[8,2,5184]{2,1,0:T(2,128)(2,1)S(1)}, u32[]{:S(2)}, u32[]{:S(2)}) %all-to-all-start) | async-done | bytes 165920 | tf_op jit(solution)/shard_map/all_to_all | solution.py:298
  21.2 0.1 slice.8
  21.3 0.1 reshape.42.rows_ref
  21.4 0.0 copy-done
  21.4 0.0 copy-done.1
  21.4 0.0 copy-start.2
  21.4 1.3 %encode.1 = (bf16[16,2304]{1,0:T(8,128)(2,1)S(1)}, f32[16,256]{1,0:T(8,128)S(1)}, f32[16,256]{1,0:T(8,128)S(1)}, f32[16,1]{1,0:T(8,128)S(1)}) custom-call(bf16[16,4608]{1,0:T(8,128)(2,1)S(1)} %reshape.42.rows_ref, bf16[256,4608]{1,0:T(8,128)(2,1)S(1)} %copy-done, f32[1,256]{1,0:T(1,128)S(1)} %bitcast.9), custom_call_target="tpu_custom_call" | custom-call | tf_op jit(solution)/shard_map/encode/pallas_call | solution.py:112
  22.6 0.0 collective-permute-start
  22.7 0.3 keep.1
  23.0 1.0 %collective-permute-done = bf16[16,2304]{1,0:T(8,128)(2,1)S(1)} collective-permute-done((bf16[16,2304]{1,0:T(8,128)(2,1)S(1)}, bf16[16,2304]{1,0:T(8,128)(2,1)S(1)}, u32[]{:S(2)}, u32[]{:S(2)}) %collective-permute-start) | collective-permute-done | bytes 73760 | tf_op jit(solution)/shard_map/ppermute | solution.py:24
  24.0 0.9 %collective-permute-start.3 = (bf16[16,2304]{1,0:T(8,128)(2,1)S(1)}, bf16[16,2304]{1,0:T(8,128)(2,1)S(1)}, u32[]{:S(2)}, u32[]{:S(2)}) collective-permute-start(bf16[16,2304]{1,0:T(8,128)(2,1)S(1)} %fusion), channel_id=1, source_target_pairs={{0,6},{2,4},{4,2},{6,0},{8,14},{10,12},{12,10},{14,8},{1,7},{3,5},... | collective-permute-start | bytes 221192 | tf_op jit(solution)/shard_map/ppermute | solution.py:24
  24.8 1.6 %collective-permute-start.2 = (bf16[16,2304]{1,0:T(8,128)(2,1)S(1)}, bf16[16,2304]{1,0:T(8,128)(2,1)S(1)}, u32[]{:S(2)}, u32[]{:S(2)}) collective-permute-start(bf16[16,2304]{1,0:T(8,128)(2,1)S(1)} %fusion), channel_id=1, source_target_pairs={{0,4},{2,6},{4,0},{6,2},{8,12},{10,14},{12,8},{14,10},{1,5},{3,7},... | collective-permute-start | bytes 221192 | tf_op jit(solution)/shard_map/ppermute | solution.py:24
  26.4 1.1 %collective-permute-start.1 = (bf16[16,2304]{1,0:T(8,128)(2,1)S(1)}, bf16[16,2304]{1,0:T(8,128)(2,1)S(1)}, u32[]{:S(2)}, u32[]{:S(2)}) collective-permute-start(bf16[16,2304]{1,0:T(8,128)(2,1)S(1)} %fusion), channel_id=1, source_target_pairs={{0,2},{2,0},{4,6},{6,4},{8,10},{10,8},{12,14},{14,12},{1,3},{3,1},... | collective-permute-start | bytes 221192 | tf_op jit(solution)/shard_map/ppermute | solution.py:24
  27.5 2.5 %collective-permute-done.3 = bf16[16,2304]{1,0:T(8,128)(2,1)S(1)} collective-permute-done((bf16[16,2304]{1,0:T(8,128)(2,1)S(1)}, bf16[16,2304]{1,0:T(8,128)(2,1)S(1)}, u32[]{:S(2)}, u32[]{:S(2)}) %collective-permute-start.3) | collective-permute-done | bytes 73760 | tf_op jit(solution)/shard_map/ppermute | solution.py:24
  30.0 0.3 collective-permute-done.2
  30.3 0.6 %collective-permute-done.1 = bf16[16,2304]{1,0:T(8,128)(2,1)S(1)} collective-permute-done((bf16[16,2304]{1,0:T(8,128)(2,1)S(1)}, bf16[16,2304]{1,0:T(8,128)(2,1)S(1)}, u32[]{:S(2)}, u32[]{:S(2)}) %collective-permute-start.1) | collective-permute-done | bytes 73760 | tf_op jit(solution)/shard_map/ppermute | solution.py:24
  31.0 0.5 %collective-permute-start.4 = (bf16[16,2304]{1,0:T(8,128)(2,1)S(1)}, bf16[16,2304]{1,0:T(8,128)(2,1)S(1)}, u32[]{:S(2)}, u32[]{:S(2)}) collective-permute-start(bf16[16,2304]{1,0:T(8,128)(2,1)S(1)} %fusion.1), channel_id=1, source_target_pairs={{0,8},{2,10},{4,12},{6,14},{8,0},{10,2},{12,4},{14,6},{1,9},{3,11}... | collective-permute-start | bytes 221192 | tf_op jit(solution)/shard_map/ppermute | solution.py:24
  31.5 0.0 copy-done.2
  31.5 0.1 dynamic_slice.6
  31.6 0.1 reduce
  31.7 5.1 %collective-permute-done.4 = bf16[16,2304]{1,0:T(8,128)(2,1)S(1)} collective-permute-done((bf16[16,2304]{1,0:T(8,128)(2,1)S(1)}, bf16[16,2304]{1,0:T(8,128)(2,1)S(1)}, u32[]{:S(2)}, u32[]{:S(2)}) %collective-permute-start.4) | collective-permute-done | bytes 73760 | tf_op jit(solution)/shard_map/ppermute | solution.py:24
  36.8 0.1 multiply_convert_fusion.grad_ref
  36.9 0.1 collective-permute-start.5
  37.0 0.7 %reshape.46 = bf16[2,4608]{1,0:T(2,128)(2,1)} reshape(bf16[2,8,576]{2,1,0:T(8,128)(2,1)S(1)} %copy.11) | data formatting | bytes 36864 | tf_op jit(solution)/shard_map/reshape | solution.py:300
  37.7 0.1 copy.10.pull_ref
  37.8 0.4 %early.1.early_ref = f32[16,256]{1,0:T(8,128)S(1)} custom-call(bf16[16,2304]{1,0:T(8,128)(2,1)S(1)} %multiply_convert_fusion.grad_ref, bf16[256,4608]{1,0:T(8,128)(2,1)S(1)} %copy-done, f32[1,256]{1,0:T(1,128)S(1)} %bitcast.8), custom_call_target="tpu_custom_call" | custom-call | flops 18874368 | bytes 589824 | tf_op jit(solution)/shard_map/early/pallas_call | solution.py:175
  38.3 0.0 collective-permute-done.5
  38.3 2.3 %finish.1 = (bf16[256,4608]{1,0:T(8,128)(2,1)}, f32[1,256]{1,0:T(1,128)}, f32[288]{0:T(512)}) custom-call(bf16[16,4608]{1,0:T(8,128)(2,1)S(1)} %pad_maximum_fusion.grad_ref, f32[16,256]{1,0:T(8,128)S(1)} %early.1.early_ref, bf16[16,4608]{1,0:T(8,128)(2,1)S(1)} %reshape.42.rows_ref, bf16[256,4608]{1,0:T(8,128)(2,1)S(1)} %copy-done, ...), custom_call_target="tpu_custom_call" | custom-call | tf_op jit(solution)/shard_map/finish/pallas_call | solution.py:267
  (7 shorter events, 0.2 us)
Async XLA Ops:
  0.6 20.7 %copy-start = (bf16[256,4608]{1,0:T(8,128)(2,1)S(1)}, bf16[256,4608]{1,0:T(8,128)(2,1)}, u32[]{:S(2)}) copy-start(bf16[256,4608]{1,0:T(8,128)(2,1)} %weight_ref.7) | copy-start | bytes 7077892
  0.6 20.7 %copy-start.1 = (f32[256]{0:T(256)S(1)}, f32[256]{0:T(256)}, u32[]{:S(2)}) copy-start(f32[256]{0:T(256)} %param.10) | copy-start | bytes 3076
  6.3 14.9 %all-to-all-start = ((bf16[8,2,5184]{2,1,0:T(2,128)(2,1)}), bf16[8,2,5184]{2,1,0:T(2,128)(2,1)S(1)}, u32[]{:S(2)}, u32[]{:S(2)}) async-start(bf16[8,2,5184]{2,1,0:T(2,128)(2,1)} %pack.1), calls=%async_computation | async-start | bytes 335872 | tf_op jit(solution)/shard_map/all_to_all | solution.py:298
  21.4 10.1 %copy-start.2 = (f32[4608]{0:T(1024)S(1)}, f32[4608]{0:T(1024)}, u32[]{:S(2)}) copy-start(f32[4608]{0:T(1024)} %param.11) | copy-start | bytes 55300
  22.6 1.3 %collective-permute-start = (bf16[16,2304]{1,0:T(8,128)(2,1)S(1)}, bf16[16,2304]{1,0:T(8,128)(2,1)S(1)}, u32[]{:S(2)}, u32[]{:S(2)}) collective-permute-start(bf16[16,2304]{1,0:T(8,128)(2,1)S(1)} %get-tuple-element.17), channel_id=1, source_target_pairs={{0,1},{1,0},{2,3},{3,2},{4,5},{5,4},{6,7},{7,6},{8,9},{9,8},{10,11... | collective-permute-start | bytes 221192 | tf_op jit(solution)/shard_map/ppermute | solution.py:24
  24.0 6.1 %collective-permute-start.3 = (bf16[16,2304]{1,0:T(8,128)(2,1)S(1)}, bf16[16,2304]{1,0:T(8,128)(2,1)S(1)}, u32[]{:S(2)}, u32[]{:S(2)}) collective-permute-start(bf16[16,2304]{1,0:T(8,128)(2,1)S(1)} %fusion), channel_id=1, source_target_pairs={{0,6},{2,4},{4,2},{6,0},{8,14},{10,12},{12,10},{14,8},{1,7},{3,5},... | collective-permute-start | bytes 221192 | tf_op jit(solution)/shard_map/ppermute | solution.py:24
  24.8 5.5 %collective-permute-start.2 = (bf16[16,2304]{1,0:T(8,128)(2,1)S(1)}, bf16[16,2304]{1,0:T(8,128)(2,1)S(1)}, u32[]{:S(2)}, u32[]{:S(2)}) collective-permute-start(bf16[16,2304]{1,0:T(8,128)(2,1)S(1)} %fusion), channel_id=1, source_target_pairs={{0,4},{2,6},{4,0},{6,2},{8,12},{10,14},{12,8},{14,10},{1,5},{3,7},... | collective-permute-start | bytes 221192 | tf_op jit(solution)/shard_map/ppermute | solution.py:24
  26.4 4.5 %collective-permute-start.1 = (bf16[16,2304]{1,0:T(8,128)(2,1)S(1)}, bf16[16,2304]{1,0:T(8,128)(2,1)S(1)}, u32[]{:S(2)}, u32[]{:S(2)}) collective-permute-start(bf16[16,2304]{1,0:T(8,128)(2,1)S(1)} %fusion), channel_id=1, source_target_pairs={{0,2},{2,0},{4,6},{6,4},{8,10},{10,8},{12,14},{14,12},{1,3},{3,1},... | collective-permute-start | bytes 221192 | tf_op jit(solution)/shard_map/ppermute | solution.py:24
  31.0 5.8 %collective-permute-start.4 = (bf16[16,2304]{1,0:T(8,128)(2,1)S(1)}, bf16[16,2304]{1,0:T(8,128)(2,1)S(1)}, u32[]{:S(2)}, u32[]{:S(2)}) collective-permute-start(bf16[16,2304]{1,0:T(8,128)(2,1)S(1)} %fusion.1), channel_id=1, source_target_pairs={{0,8},{2,10},{4,12},{6,14},{8,0},{10,2},{12,4},{14,6},{1,9},{3,11}... | collective-permute-start | bytes 221192 | tf_op jit(solution)/shard_map/ppermute | solution.py:24
  36.9 1.4 %collective-permute-start.5 = (bf16[16,2304]{1,0:T(8,128)(2,1)S(1)}, bf16[16,2304]{1,0:T(8,128)(2,1)S(1)}, u32[]{:S(2)}, u32[]{:S(2)}) collective-permute-start(bf16[16,2304]{1,0:T(8,128)(2,1)S(1)} %multiply_convert_fusion.grad_ref), channel_id=1, source_target_pairs={{0,1},{1,0},{2,3},{3,2},{4,5},{5,4},{6,7},{7,6},{8,9},{9,8},{10,11... | collective-permute-start | bytes 221192 | tf_op jit(solution)/shard_map/ppermute | solution.py:24

commit v5 on v4

--- a/solution.py
+++ b/solution.py
@@ -31,36 +31,42 @@
     return here, there
 
 
-def pack_kernel(cur_hbm, cached_hbm, perm_hbm, out_hbm, cached_ref, perm_ref, ordered_ref, sems):
+def pack_kernel(
+    cur_hbm, cached_hbm, perm_hbm, out_hbm, cur_ref, cached_ref, perm_ref, staged_ref, sems
+):
     dp, own, _ = out_hbm.shape
     width = cur_hbm.shape[1]
     row_total, columns = cached_ref.shape
     fetches = [
-        pltpu.make_async_copy(cached_hbm, cached_ref, sems.at[0]),
-        pltpu.make_async_copy(perm_hbm, perm_ref, sems.at[1]),
+        pltpu.make_async_copy(source, target, sems.at[index])
+        for index, (source, target) in enumerate(
+            [(cur_hbm, cur_ref), (cached_hbm, cached_ref), (perm_hbm, perm_ref)]
+        )
     ]
     for fetch in fetches:
         fetch.start()
-    spreads = [
-        pltpu.make_async_copy(cur_hbm, out_hbm.at[peer, :, pl.ds(0, width)], sems.at[3 + peer])
-        for peer in range(dp)
-    ]
-    for spread in spreads:
-        spread.start()
-    for fetch in fetches:
-        fetch.wait()
+    rows_copy, next_copy = (
+        pltpu.make_async_copy(staged_ref.at[:, :, part], out_hbm.at[:, :, part], sem)
+        for part, sem in (
+            (pl.ds(0, width), sems.at[3]),
+            (pl.ds(width, columns), sems.at[4]),
+        )
+    )
+    fetches[0].wait()
+    cur = cur_ref[...]
+    for peer in range(dp):
+        staged_ref[peer, :, :width] = cur
+    rows_copy.start()
+    fetches[1].wait()
+    fetches[2].wait()
     slots = lax.broadcasted_iota(jnp.int32, (row_total, row_total), 0)
     selector = (jnp.broadcast_to(perm_ref[...], slots.shape) == slots).astype(jnp.bfloat16)
     ordered = jnp.dot(selector, cached_ref[...], preferred_element_type=jnp.float32)
     for peer in range(dp):
-        ordered_ref[peer] = ordered[peer * own : (peer + 1) * own].astype(jnp.bfloat16)
-    last = pltpu.make_async_copy(
-        ordered_ref, out_hbm.at[:, :, pl.ds(width, columns)], sems.at[2]
-    )
-    last.start()
-    for spread in spreads:
-        spread.wait()
-    last.wait()
+        staged_ref[peer, :, width:] = ordered[peer * own : (peer + 1) * own].astype(jnp.bfloat16)
+    next_copy.start()
+    rows_copy.wait()
+    next_copy.wait()
 
 
 def pack(cur_rows, cached_rows, shuffle_perm, dp):
@@ -72,10 +78,11 @@
         in_specs=[whole(pl.ANY)] * 3,
         out_specs=whole(pl.ANY),
         scratch_shapes=[
+            pltpu.VMEM((own, width), jnp.bfloat16),
             pltpu.VMEM((row_total, columns), jnp.bfloat16),
             pltpu.VMEM((1, row_total), jnp.int32),
-            pltpu.VMEM((dp, own, columns), jnp.bfloat16),
-            pltpu.SemaphoreType.DMA((3 + dp,)),
+            pltpu.VMEM((dp, own, width + columns), jnp.bfloat16),
+            pltpu.SemaphoreType.DMA((5,)),
         ],
         compiler_params=pltpu.CompilerParams(vmem_limit_bytes=PACK_BYTES),
         name="pack",

time: 41 us -> 37 us (0.902)
  Pallas kernels: 9.97 us -> 5.97 us
    pallas_call x1, Pallas kernels: 5.67 us -> 1.67 us  [pack(): pl.pallas_call(pack_kernel, out_shape=jax.ShapeDtypeStruct((dp, own, widt...]
  transfers between devices with their start and end apart: 7 -> 7, of which waited for: 6 -> 6; matrix products, arithmetic and copies ran while one was open for 8% -> 9% of each run, Pallas kernels for 2% -> 2%
where the time goes in v5:
time: 37 us; the launch traced here: 36.7 us
  waiting for transfers between devices  14.8 us (40%)
  starting transfers between devices  11.5 us (31%)
  Pallas kernels  5.97 us (16%)
  other arithmetic  2.55 us (7%)
  local copies, waits for them, and re-layouts  1.11 us (3%)
  between operations  0.77 us (2%)
    ppermute x6, waiting for transfers between devices, exchange(): return lax.ppermute(value, axis, [(k, k ^ distance) for k in range(size)])  9.44 us
    all_to_all x1, starting transfers between devices, per_device(): lax.all_to_all(pack(cur_rows, cached_rows, shuffle_perm, dp), 'dp', 0, 0)  7.26 us
    all_to_all x1, waiting for transfers between devices, per_device(): lax.all_to_all(pack(cur_rows, cached_rows, shuffle_perm, dp), 'dp', 0, 0)  5.38 us
    ppermute x6, starting transfers between devices, exchange(): return lax.ppermute(value, axis, [(k, k ^ distance) for k in range(size)])  4.2 us
    pallas_call x1, Pallas kernels, finish(): pl.pallas_call(functools.partial(finish_kernel, tile, span), out_shape=(j...  2.33 us
    reduce_sum x1, other arithmetic, per_device(): jnp.sum(weight_f * weight_f, axis=1) + 1e-06  2.21 us
    pallas_call x1, Pallas kernels, pack(): pl.pallas_call(pack_kernel, out_shape=jax.ShapeDtypeStruct((dp, own, widt...  1.67 us
    pallas_call x1, Pallas kernels, encode(): pl.pallas_call(encode_kernel, out_shape=(jax.ShapeDtypeStruct((rows_total...  1.25 us
  transfers between devices with their start and end apart: 7, of which 6 were waited for; matrix products, arithmetic and copies ran while one was open for 9% of the time, Pallas kernels for 2%

profile of v5, /device:TPU:0, one launch (start us, length us, event | category | flops | bytes accessed | tf_op | source)
XLA Modules:
  0.0 36.7 jit_solution(14762756716770765387)
XLA Ops:
  0.6 0.0 copy-start
  0.6 0.0 copy-start.1
  0.7 1.7 %pack.1 = bf16[8,2,5184]{2,1,0:T(2,128)(2,1)} custom-call(bf16[2,4608]{1,0:T(2,128)(2,1)} %cur_hbm.1, bf16[16,576]{1,0:T(8,128)(2,1)} %cached_hbm.1, s32[1,16]{1,0:T(1,128)} %bitcast.11), custom_call_target="tpu_custom_call" | custom-call | tf_op jit(solution)/shard_map/pack/pallas_call | solution.py:75
  2.3 7.3 %all-to-all-start = ((bf16[8,2,5184]{2,1,0:T(2,128)(2,1)}), bf16[8,2,5184]{2,1,0:T(2,128)(2,1)S(1)}, u32[]{:S(2)}, u32[]{:S(2)}) async-start(bf16[8,2,5184]{2,1,0:T(2,128)(2,1)} %pack.1), calls=%async_computation | async-start | bytes 335872 | tf_op jit(solution)/shard_map/all_to_all | solution.py:305
  9.6 2.2 %multiply_reduce_fusion = f32[256]{0:T(256)S(1)} fusion(bf16[256,4608]{1,0:T(8,128)(2,1)} %weight_ref.7), kind=kLoop, calls=%fused_computation | loop fusion | flops 3538688 | bytes 2360320 | tf_op jit(solution)/shard_map/reduce_sum | solution.py:310
  11.8 5.4 %all-to-all-done = bf16[8,2,5184]{2,1,0:T(2,128)(2,1)S(1)} async-done(((bf16[8,2,5184]{2,1,0:T(2,128)(2,1)}), bf16[8,2,5184]{2,1,0:T(2,128)(2,1)S(1)}, u32[]{:S(2)}, u32[]{:S(2)}) %all-to-all-start) | async-done | bytes 165920 | tf_op jit(solution)/shard_map/all_to_all | solution.py:305
  17.2 0.1 slice.8
  17.3 0.1 reshape.42.rows_ref
  17.4 0.0 copy-done
  17.4 0.0 copy-done.1
  17.4 0.0 copy-start.2
  17.4 1.3 %encode.1 = (bf16[16,2304]{1,0:T(8,128)(2,1)S(1)}, f32[16,256]{1,0:T(8,128)S(1)}, f32[16,256]{1,0:T(8,128)S(1)}, f32[16,1]{1,0:T(8,128)S(1)}) custom-call(bf16[16,4608]{1,0:T(8,128)(2,1)S(1)} %reshape.42.rows_ref, bf16[256,4608]{1,0:T(8,128)(2,1)S(1)} %copy-done, f32[1,256]{1,0:T(1,128)S(1)} %bitcast.9), custom_call_target="tpu_custom_call" | custom-call | tf_op jit(solution)/shard_map/encode/pallas_call | solution.py:119
  18.7 0.0 collective-permute-start
  18.7 0.3 keep.1
  19.0 1.0 %collective-permute-done = bf16[16,2304]{1,0:T(8,128)(2,1)S(1)} collective-permute-done((bf16[16,2304]{1,0:T(8,128)(2,1)S(1)}, bf16[16,2304]{1,0:T(8,128)(2,1)S(1)}, u32[]{:S(2)}, u32[]{:S(2)}) %collective-permute-start) | collective-permute-done | bytes 73760 | tf_op jit(solution)/shard_map/ppermute | solution.py:24
  20.0 0.9 %collective-permute-start.3 = (bf16[16,2304]{1,0:T(8,128)(2,1)S(1)}, bf16[16,2304]{1,0:T(8,128)(2,1)S(1)}, u32[]{:S(2)}, u32[]{:S(2)}) collective-permute-start(bf16[16,2304]{1,0:T(8,128)(2,1)S(1)} %fusion), channel_id=1, source_target_pairs={{0,6},{2,4},{4,2},{6,0},{8,14},{10,12},{12,10},{14,8},{1,7},{3,5},... | collective-permute-start | bytes 221192 | tf_op jit(solution)/shard_map/ppermute | solution.py:24
  20.8 1.6 %collective-permute-start.2 = (bf16[16,2304]{1,0:T(8,128)(2,1)S(1)}, bf16[16,2304]{1,0:T(8,128)(2,1)S(1)}, u32[]{:S(2)}, u32[]{:S(2)}) collective-permute-start(bf16[16,2304]{1,0:T(8,128)(2,1)S(1)} %fusion), channel_id=1, source_target_pairs={{0,4},{2,6},{4,0},{6,2},{8,12},{10,14},{12,8},{14,10},{1,5},{3,7},... | collective-permute-start | bytes 221192 | tf_op jit(solution)/shard_map/ppermute | solution.py:24
  22.4 1.1 %collective-permute-start.1 = (bf16[16,2304]{1,0:T(8,128)(2,1)S(1)}, bf16[16,2304]{1,0:T(8,128)(2,1)S(1)}, u32[]{:S(2)}, u32[]{:S(2)}) collective-permute-start(bf16[16,2304]{1,0:T(8,128)(2,1)S(1)} %fusion), channel_id=1, source_target_pairs={{0,2},{2,0},{4,6},{6,4},{8,10},{10,8},{12,14},{14,12},{1,3},{3,1},... | collective-permute-start | bytes 221192 | tf_op jit(solution)/shard_map/ppermute | solution.py:24
  23.5 2.5 %collective-permute-done.3 = bf16[16,2304]{1,0:T(8,128)(2,1)S(1)} collective-permute-done((bf16[16,2304]{1,0:T(8,128)(2,1)S(1)}, bf16[16,2304]{1,0:T(8,128)(2,1)S(1)}, u32[]{:S(2)}, u32[]{:S(2)}) %collective-permute-start.3) | collective-permute-done | bytes 73760 | tf_op jit(solution)/shard_map/ppermute | solution.py:24
  26.0 0.3 collective-permute-done.2
  26.3 0.6 %collective-permute-done.1 = bf16[16,2304]{1,0:T(8,128)(2,1)S(1)} collective-permute-done((bf16[16,2304]{1,0:T(8,128)(2,1)S(1)}, bf16[16,2304]{1,0:T(8,128)(2,1)S(1)}, u32[]{:S(2)}, u32[]{:S(2)}) %collective-permute-start.1) | collective-permute-done | bytes 73760 | tf_op jit(solution)/shard_map/ppermute | solution.py:24
  27.0 0.5 %collective-permute-start.4 = (bf16[16,2304]{1,0:T(8,128)(2,1)S(1)}, bf16[16,2304]{1,0:T(8,128)(2,1)S(1)}, u32[]{:S(2)}, u32[]{:S(2)}) collective-permute-start(bf16[16,2304]{1,0:T(8,128)(2,1)S(1)} %fusion.1), channel_id=1, source_target_pairs={{0,8},{2,10},{4,12},{6,14},{8,0},{10,2},{12,4},{14,6},{1,9},{3,11}... | collective-permute-start | bytes 221192 | tf_op jit(solution)/shard_map/ppermute | solution.py:24
  27.5 0.0 copy-done.2
  27.5 0.1 dynamic_slice.6
  27.6 0.1 reduce
  27.7 5.1 %collective-permute-done.4 = bf16[16,2304]{1,0:T(8,128)(2,1)S(1)} collective-permute-done((bf16[16,2304]{1,0:T(8,128)(2,1)S(1)}, bf16[16,2304]{1,0:T(8,128)(2,1)S(1)}, u32[]{:S(2)}, u32[]{:S(2)}) %collective-permute-start.4) | collective-permute-done | bytes 73760 | tf_op jit(solution)/shard_map/ppermute | solution.py:24
  32.8 0.1 multiply_convert_fusion.grad_ref
  32.9 0.1 collective-permute-start.5
  33.0 0.7 %reshape.46 = bf16[2,4608]{1,0:T(2,128)(2,1)} reshape(bf16[2,8,576]{2,1,0:T(8,128)(2,1)S(1)} %copy.11) | data formatting | bytes 36864 | tf_op jit(solution)/shard_map/reshape | solution.py:307
  33.7 0.1 copy.10.pull_ref
  33.8 0.4 %early.1.early_ref = f32[16,256]{1,0:T(8,128)S(1)} custom-call(bf16[16,2304]{1,0:T(8,128)(2,1)S(1)} %multiply_convert_fusion.grad_ref, bf16[256,4608]{1,0:T(8,128)(2,1)S(1)} %copy-done, f32[1,256]{1,0:T(1,128)S(1)} %bitcast.8), custom_call_target="tpu_custom_call" | custom-call | flops 18874368 | bytes 589824 | tf_op jit(solution)/shard_map/early/pallas_call | solution.py:182
  34.3 0.0 collective-permute-done.5
  34.4 2.3 %finish.1 = (bf16[256,4608]{1,0:T(8,128)(2,1)}, f32[1,256]{1,0:T(1,128)}, f32[288]{0:T(512)}) custom-call(bf16[16,4608]{1,0:T(8,128)(2,1)S(1)} %pad_maximum_fusion.grad_ref, f32[16,256]{1,0:T(8,128)S(1)} %early.1.early_ref, bf16[16,4608]{1,0:T(8,128)(2,1)S(1)} %reshape.42.rows_ref, bf16[256,4608]{1,0:T(8,128)(2,1)S(1)} %copy-done, ...), custom_call_target="tpu_custom_call" | custom-call | tf_op jit(solution)/shard_map/finish/pallas_call | solution.py:274
  (7 shorter events, 0.2 us)
Async XLA Ops:
  0.6 16.7 %copy-start = (bf16[256,4608]{1,0:T(8,128)(2,1)S(1)}, bf16[256,4608]{1,0:T(8,128)(2,1)}, u32[]{:S(2)}) copy-start(bf16[256,4608]{1,0:T(8,128)(2,1)} %weight_ref.7) | copy-start | bytes 7077892
  0.6 16.7 %copy-start.1 = (f32[256]{0:T(256)S(1)}, f32[256]{0:T(256)}, u32[]{:S(2)}) copy-start(f32[256]{0:T(256)} %param.10) | copy-start | bytes 3076
  2.3 14.9 %all-to-all-start = ((bf16[8,2,5184]{2,1,0:T(2,128)(2,1)}), bf16[8,2,5184]{2,1,0:T(2,128)(2,1)S(1)}, u32[]{:S(2)}, u32[]{:S(2)}) async-start(bf16[8,2,5184]{2,1,0:T(2,128)(2,1)} %pack.1), calls=%async_computation | async-start | bytes 335872 | tf_op jit(solution)/shard_map/all_to_all | solution.py:305
  17.4 10.1 %copy-start.2 = (f32[4608]{0:T(1024)S(1)}, f32[4608]{0:T(1024)}, u32[]{:S(2)}) copy-start(f32[4608]{0:T(1024)} %param.11) | copy-start | bytes 55300
  18.7 1.3 %collective-permute-start = (bf16[16,2304]{1,0:T(8,128)(2,1)S(1)}, bf16[16,2304]{1,0:T(8,128)(2,1)S(1)}, u32[]{:S(2)}, u32[]{:S(2)}) collective-permute-start(bf16[16,2304]{1,0:T(8,128)(2,1)S(1)} %get-tuple-element.17), channel_id=1, source_target_pairs={{0,1},{1,0},{2,3},{3,2},{4,5},{5,4},{6,7},{7,6},{8,9},{9,8},{10,11... | collective-permute-start | bytes 221192 | tf_op jit(solution)/shard_map/ppermute | solution.py:24
  20.0 6.1 %collective-permute-start.3 = (bf16[16,2304]{1,0:T(8,128)(2,1)S(1)}, bf16[16,2304]{1,0:T(8,128)(2,1)S(1)}, u32[]{:S(2)}, u32[]{:S(2)}) collective-permute-start(bf16[16,2304]{1,0:T(8,128)(2,1)S(1)} %fusion), channel_id=1, source_target_pairs={{0,6},{2,4},{4,2},{6,0},{8,14},{10,12},{12,10},{14,8},{1,7},{3,5},... | collective-permute-start | bytes 221192 | tf_op jit(solution)/shard_map/ppermute | solution.py:24
  20.8 5.5 %collective-permute-start.2 = (bf16[16,2304]{1,0:T(8,128)(2,1)S(1)}, bf16[16,2304]{1,0:T(8,128)(2,1)S(1)}, u32[]{:S(2)}, u32[]{:S(2)}) collective-permute-start(bf16[16,2304]{1,0:T(8,128)(2,1)S(1)} %fusion), channel_id=1, source_target_pairs={{0,4},{2,6},{4,0},{6,2},{8,12},{10,14},{12,8},{14,10},{1,5},{3,7},... | collective-permute-start | bytes 221192 | tf_op jit(solution)/shard_map/ppermute | solution.py:24
  22.4 4.5 %collective-permute-start.1 = (bf16[16,2304]{1,0:T(8,128)(2,1)S(1)}, bf16[16,2304]{1,0:T(8,128)(2,1)S(1)}, u32[]{:S(2)}, u32[]{:S(2)}) collective-permute-start(bf16[16,2304]{1,0:T(8,128)(2,1)S(1)} %fusion), channel_id=1, source_target_pairs={{0,2},{2,0},{4,6},{6,4},{8,10},{10,8},{12,14},{14,12},{1,3},{3,1},... | collective-permute-start | bytes 221192 | tf_op jit(solution)/shard_map/ppermute | solution.py:24
  27.0 5.8 %collective-permute-start.4 = (bf16[16,2304]{1,0:T(8,128)(2,1)S(1)}, bf16[16,2304]{1,0:T(8,128)(2,1)S(1)}, u32[]{:S(2)}, u32[]{:S(2)}) collective-permute-start(bf16[16,2304]{1,0:T(8,128)(2,1)S(1)} %fusion.1), channel_id=1, source_target_pairs={{0,8},{2,10},{4,12},{6,14},{8,0},{10,2},{12,4},{14,6},{1,9},{3,11}... | collective-permute-start | bytes 221192 | tf_op jit(solution)/shard_map/ppermute | solution.py:24
  32.9 1.4 %collective-permute-start.5 = (bf16[16,2304]{1,0:T(8,128)(2,1)S(1)}, bf16[16,2304]{1,0:T(8,128)(2,1)S(1)}, u32[]{:S(2)}, u32[]{:S(2)}) collective-permute-start(bf16[16,2304]{1,0:T(8,128)(2,1)S(1)} %multiply_convert_fusion.grad_ref), channel_id=1, source_target_pairs={{0,1},{1,0},{2,3},{3,2},{4,5},{5,4},{6,7},{7,6},{8,9},{9,8},{10,11... | collective-permute-start | bytes 221192 | tf_op jit(solution)/shard_map/ppermute | solution.py:24

commit v6 on v4

--- a/solution.py
+++ b/solution.py
@@ -10,7 +10,6 @@
 SPARSITY = 4.0
 SHARP = 4.0
 VMEM_BYTES = 16 * 1024 * 1024
-PACK_BYTES = 60 * 1024 * 1024
 NT = (((1,), (1,)), ((), ()))
 TN = (((0,), (0,)), ((), ()))
 
@@ -31,69 +30,90 @@
     return here, there
 
 
-def pack_kernel(cur_hbm, cached_hbm, perm_hbm, out_hbm, cached_ref, perm_ref, ordered_ref, sems):
-    dp, own, _ = out_hbm.shape
-    width = cur_hbm.shape[1]
+def flip_rows(value, distance):
+    count = value.shape[0]
+    row = lax.broadcasted_iota(jnp.int32, value.shape, 0)
+    bit = 1
+    while bit <= distance:
+        if distance & bit:
+            up = pltpu.roll(value, count - bit, 0)
+            down = pltpu.roll(value, bit, 0)
+            value = jnp.where(row & bit == 0, up, down)
+        bit *= 2
+    return value
+
+
+def order_kernel(own, cached_hbm, perm_hbm, out_ref, cached_ref, perm_ref, sems):
     row_total, columns = cached_ref.shape
+    dp = row_total // own
     fetches = [
         pltpu.make_async_copy(cached_hbm, cached_ref, sems.at[0]),
         pltpu.make_async_copy(perm_hbm, perm_ref, sems.at[1]),
     ]
     for fetch in fetches:
         fetch.start()
-    spreads = [
-        pltpu.make_async_copy(cur_hbm, out_hbm.at[peer, :, pl.ds(0, width)], sems.at[3 + peer])
-        for peer in range(dp)
-    ]
-    for spread in spreads:
-        spread.start()
+    row = lax.broadcasted_iota(jnp.int32, (row_total, row_total), 0)
+    rest = dp // 4
+    distance = row // (rest * own) + 4 * (row // own % rest)
+    wanted = (distance ^ lax.axis_index("dp")) * own + row % own
     for fetch in fetches:
         fetch.wait()
-    slots = lax.broadcasted_iota(jnp.int32, (row_total, row_total), 0)
-    selector = (jnp.broadcast_to(perm_ref[...], slots.shape) == slots).astype(jnp.bfloat16)
-    ordered = jnp.dot(selector, cached_ref[...], preferred_element_type=jnp.float32)
-    for peer in range(dp):
-        ordered_ref[peer] = ordered[peer * own : (peer + 1) * own].astype(jnp.bfloat16)
-    last = pltpu.make_async_copy(
-        ordered_ref, out_hbm.at[:, :, pl.ds(width, columns)], sems.at[2]
-    )
-    last.start()
-    for spread in spreads:
-        spread.wait()
-    last.wait()
-
-
-def pack(cur_rows, cached_rows, shuffle_perm, dp):
-    own, width = cur_rows.shape
+    selector = (jnp.broadcast_to(perm_ref[...], row.shape) == wanted).astype(jnp.bfloat16)
+    out_ref[...] = jnp.dot(
+        selector, cached_ref[...], preferred_element_type=jnp.float32
+    ).astype(jnp.bfloat16)
+
+
+def order(cached_rows, shuffle_perm, own):
     row_total, columns = cached_rows.shape
     return pl.pallas_call(
-        pack_kernel,
-        out_shape=jax.ShapeDtypeStruct((dp, own, width + columns), jnp.bfloat16),
-        in_specs=[whole(pl.ANY)] * 3,
-        out_specs=whole(pl.ANY),
+        functools.partial(order_kernel, own),
+        out_shape=jax.ShapeDtypeStruct((row_total, columns), jnp.bfloat16),
+        in_specs=[whole(pl.ANY)] * 2,
+        out_specs=whole(),
         scratch_shapes=[
             pltpu.VMEM((row_total, columns), jnp.bfloat16),
             pltpu.VMEM((1, row_total), jnp.int32),
-            pltpu.VMEM((dp, own, columns), jnp.bfloat16),
-            pltpu.SemaphoreType.DMA((3 + dp,)),
+            pltpu.SemaphoreType.DMA((2,)),
         ],
-        compiler_params=pltpu.CompilerParams(vmem_limit_bytes=PACK_BYTES),
-        name="pack",
-    )(cur_rows, cached_rows, shuffle_perm.reshape(1, row_total))
-
-
-def encode_kernel(rows_ref, weight_ref, bias_ref, send_ref, latents_ref, sharp_ref, scales_ref):
-    rows_total, width = rows_ref.shape
+        compiler_params=pltpu.CompilerParams(vmem_limit_bytes=VMEM_BYTES),
+        cost_estimate=pl.CostEstimate(flops=4000000, bytes_accessed=2000000, transcendentals=0),
+        name="order",
+    )(cached_rows, shuffle_perm.reshape(1, row_total))
+
+
+def encode_kernel(
+    own,
+    first_ref,
+    second_ref,
+    third_ref,
+    fourth_ref,
+    weight_ref,
+    bias_ref,
+    send_ref,
+    rows_ref,
+    latents_ref,
+    sharp_ref,
+    scales_ref,
+    rows_f_ref,
+):
+    rows_total, width = rows_f_ref.shape
     batch_rows = rows_total // 2
-    projected = lax.dot_general(
-        rows_ref[...], weight_ref[...], NT, preferred_element_type=jnp.float32
-    )
-    rows_f = rows_ref[...].astype(jnp.float32)
+    part = rows_total // 4
+    for index, ref in enumerate((first_ref, second_ref, third_ref, fourth_ref)):
+        value = ref[...].astype(jnp.float32)
+        rows_f_ref[index * part : (index + 1) * part] = value[:, :width]
+    rows_f = rows_f_ref[...]
+    rows = rows_f.astype(jnp.bfloat16)
+    rows_ref[...] = rows
+    projected = lax.dot_general(rows, weight_ref[...], NT, preferred_element_type=jnp.float32)
     squares = jnp.sum(rows_f * rows_f, axis=1, keepdims=True)
-    first = jnp.sum(squares[:batch_rows], axis=0, keepdims=True) / batch_rows
-    second = jnp.sum(squares[batch_rows:], axis=0, keepdims=True) / batch_rows
     row = lax.broadcasted_iota(jnp.int32, (rows_total, 1), 0)
-    scales = jnp.sqrt(width / jnp.where(row < batch_rows, first, second))
+    rest = part // own
+    near = row // own % rest < rest // 2
+    here = jnp.sum(jnp.where(near, squares, 0.0), axis=0, keepdims=True) / batch_rows
+    far = jnp.sum(jnp.where(near, 0.0, squares), axis=0, keepdims=True) / batch_rows
+    scales = jnp.sqrt(width / jnp.where(near, here, far))
     scales_ref[...] = scales
     sharp = SHARP * (scales * projected + bias_ref[...])
     latents = jax.nn.softplus(sharp) / SHARP
@@ -105,23 +125,25 @@
     ).astype(jnp.bfloat16)
 
 
-def encode(rows, weight, enc_bias):
-    rows_total, width = rows.shape
-    count = weight.shape[0]
+def encode(parts, weight, enc_bias, own):
+    count, width = weight.shape
+    rows_total = 4 * parts[0].shape[0]
     f32 = jnp.float32
     return pl.pallas_call(
-        encode_kernel,
+        functools.partial(encode_kernel, own),
         out_shape=(
             jax.ShapeDtypeStruct((rows_total, width // 2), jnp.bfloat16),
+            jax.ShapeDtypeStruct((rows_total, width), jnp.bfloat16),
             jax.ShapeDtypeStruct((rows_total, count), f32),
             jax.ShapeDtypeStruct((rows_total, count), f32),
             jax.ShapeDtypeStruct((rows_total, 1), f32),
         ),
-        in_specs=[whole()] * 3,
-        out_specs=[whole()] * 4,
+        in_specs=[whole()] * 6,
+        out_specs=[whole()] * 5,
+        scratch_shapes=[pltpu.VMEM((rows_total, width), f32)],
         compiler_params=pltpu.CompilerParams(vmem_limit_bytes=VMEM_BYTES),
         name="encode",
-    )(rows, weight, enc_bias.reshape(1, count))
+    )(*parts, weight, enc_bias.reshape(1, count))
 
 
 def keep_kernel(latents_ref, sharp_ref, weight_ref, norms_ref, mine_ref, gate_ref, pull_ref):
@@ -156,6 +178,49 @@
         ),
         name="keep",
     )(latents, sharp, weight, norms)
+
+
+def merge_kernel(distances, total_ref, *refs):
+    total = total_ref[...]
+    for distance, ref in zip(distances, refs):
+        total = total + flip_rows(ref[...].astype(jnp.float32), distance)
+    sum_ref, sent_ref = refs[len(distances) :]
+    sum_ref[...] = total
+    sent_ref[...] = total.astype(jnp.bfloat16)
+
+
+def merge(total, arrived, distances):
+    return pl.pallas_call(
+        functools.partial(merge_kernel, distances),
+        out_shape=(
+            jax.ShapeDtypeStruct(total.shape, jnp.float32),
+            jax.ShapeDtypeStruct(total.shape, jnp.bfloat16),
+        ),
+        in_specs=[whole()] * (1 + len(arrived)),
+        out_specs=[whole()] * 2,
+        compiler_params=pltpu.CompilerParams(vmem_limit_bytes=VMEM_BYTES),
+        name="merge",
+    )(total, *arrived)
+
+
+def settle_kernel(distance, total_ref, arrived_ref, rows_ref, scales_ref, bias_ref, grad_ref):
+    rows_total, width = rows_ref.shape
+    here, _ = core_columns(width // 2)
+    total = total_ref[...] + flip_rows(arrived_ref[...].astype(jnp.float32), distance)
+    target = rows_ref[:, here].astype(jnp.float32) * scales_ref[...]
+    error = total + bias_ref[:, here] - target
+    grad_ref[...] = (2.0 / (rows_total // 2) * error).astype(jnp.bfloat16)
+
+
+def settle(total, arrived, rows, scales, dec_bias, distance):
+    return pl.pallas_call(
+        functools.partial(settle_kernel, distance),
+        out_shape=jax.ShapeDtypeStruct(total.shape, jnp.bfloat16),
+        in_specs=[whole()] * 5,
+        out_specs=whole(),
+        compiler_params=pltpu.CompilerParams(vmem_limit_bytes=VMEM_BYTES),
+        name="settle",
+    )(total, arrived, rows, scales, dec_bias.reshape(1, -1))
 
 
 def early_kernel(grad_ref, weight_ref, norms_ref, out_ref):
@@ -288,42 +353,67 @@
 
 def per_device(cur_rows, cached_rows, shuffle_perm, weight, enc_bias, dec_bias):
     dp = lax.axis_size("dp")
+    rest = dp // 4
     own, width = cur_rows.shape
     columns = cached_rows.shape[1]
-    half = width // 2
     count = weight.shape[0]
-    batch_rows = dp * own // 2
+    place = lax.axis_index("dp")
     core = lax.axis_index("latent")
 
-    arrived = lax.all_to_all(pack(cur_rows, cached_rows, shuffle_perm, dp), "dp", 0, 0)
-    gathered = arrived[:, :, :width].reshape(dp * own, width)
-    next_batch = arrived[:, :, width:].transpose(1, 0, 2).reshape(own, dp * columns)
+    near = cur_rows
+    distance = 4
+    while distance < dp:
+        near = jnp.concatenate([near, exchange(near, "dp", distance)], axis=0)
+        distance *= 2
+    ordered = order(cached_rows, shuffle_perm, own).reshape(4, rest * own, columns)
+    parts = [near] + [
+        exchange(jnp.concatenate([near, ordered[low]], axis=1), "dp", low) for low in range(1, 4)
+    ]
 
     weight_f = weight.astype(jnp.float32)
     norms = jnp.sqrt(jnp.sum(weight_f * weight_f, axis=1) + 1e-06).reshape(1, count)
-    send, latents, sharp, scales = encode(gathered, weight, enc_bias)
+    send, gathered, latents, sharp, scales = encode(parts, weight, enc_bias, own)
     came = exchange(send, "latent", 1)
     mine, gate, pull = keep(latents, sharp, weight, norms)
 
     total = mine + came.astype(jnp.float32)
-    corner = min(4, dp)
     sent = total.astype(jnp.bfloat16)
-    for distance in range(1, corner):
-        total = total + exchange(sent, "dp", distance).astype(jnp.float32)
-    distance = corner
+    lows = (1, 2, 3)
+    total, sent = merge(
+        total,
+        [exchange(sent, "dp", low) for low in lows],
+        tuple(low * rest * own for low in lows),
+    )
+
+    riders = jnp.stack([ordered[0]] + [part[:, width:] for part in parts[1:]])
+    riders = riders.reshape(4, rest, own, columns).transpose(1, 0, 2, 3)
+    riders, sent = lax.optimization_barrier((riders, sent))
+    distance = 4
     while distance < dp:
-        total = total + exchange(total.astype(jnp.bfloat16), "dp", distance).astype(jnp.float32)
+        arrived = exchange(sent, "dp", distance)
+        split = riders.reshape((-1, 2) + riders.shape[1:])
+        riders = jnp.concatenate([split[:, 0], exchange(split[:, 1], "dp", distance)], axis=1)
+        row_distance = distance // 4 * own
+        if 2 * distance < dp:
+            total, sent = merge(total, [arrived], (row_distance,))
+        else:
+            grad_mine = settle(total, arrived, gathered, scales, dec_bias, row_distance)
         distance *= 2
 
-    target = lax.dynamic_slice_in_dim(gathered, core * half, half, 1).astype(jnp.float32)
-    bias = lax.dynamic_slice_in_dim(dec_bias, core * half, half, 0)
-    error = total + bias[None, :] - target * scales
-    grad_mine = (2.0 / batch_rows * error).astype(jnp.bfloat16)
+    riders = riders[0]
+    bit = 1
+    while bit < dp:
+        pairs = riders.reshape(dp // (2 * bit), 2, bit * own * columns)
+        pairs = jnp.where(place & bit == 0, pairs, pairs[:, ::-1])
+        riders = pairs.reshape(dp, own, columns)
+        bit *= 2
+    next_batch = riders.transpose(1, 0, 2).reshape(own, dp * columns)
+
     grad_other = exchange(grad_mine, "latent", 1)
     early_sum = early(grad_mine, weight, norms)
-    low = jnp.where(core == 0, grad_mine, grad_other)
-    high = jnp.where(core == 0, grad_other, grad_mine)
-    grad_out = jnp.concatenate([low, high], axis=1)
+    low_half = jnp.where(core == 0, grad_mine, grad_other)
+    high_half = jnp.where(core == 0, grad_other, grad_mine)
+    grad_out = jnp.concatenate([low_half, high_half], axis=1)
 
     shares = width // (2 * dp)
     weight_grad, enc_bias_grad, dec_bias_grad = finish(

time: 41 us -> 37 us (0.902)
  waiting for transfers between devices: 14.8 us -> 9.03 us
  Pallas kernels: 9.97 us -> 4.62 us
  starting transfers between devices: 11.5 us -> 14.4 us
  local copies, waits for them, and re-layouts: 1.11 us -> 3.76 us
  other arithmetic: 2.55 us -> 3.99 us
    ppermute x6 -> x11, starting transfers between devices: 4.2 us -> 14.4 us  [exchange(): return lax.ppermute(value, axis, [(k, k ^ distance) for k in range(size)])]
    all_to_all x1 -> x0, starting transfers between devices: 7.26 us -> none  [per_device(): lax.all_to_all(pack(cur_rows, cached_rows, shuffle_perm, dp), 'dp', 0, 0)]
    all_to_all x1 -> x0, waiting for transfers between devices: 5.38 us -> none  [per_device(): lax.all_to_all(pack(cur_rows, cached_rows, shuffle_perm, dp), 'dp', 0, 0)]
    pallas_call x2 -> x4, Pallas kernels: 6.92 us -> 1.59 us  [the longest x1 1.26 us: encode(): pl.pallas_call(functools.partial(encode_kernel, own), out_shape=(jax.Shap...]
    rev x0 -> x3, local copies, waits for them, and re-layouts: none -> 1.81 us  [per_device(): pairs = jnp.where(place & bit == 0, pairs, pairs[:, ::-1])]
    concatenate x1 -> x4, other arithmetic: 0.01 us -> 1.59 us  [the longest x1 0.78 us: per_device(): jnp.concatenate([near, ordered[low]], axis=1)]
    unnamed x6 -> x10, local copies, waits for them, and re-layouts: 0.02 us -> 0.74 us
    ppermute x6 -> x11, waiting for transfers between devices: 9.44 us -> 9.03 us  [exchange(): return lax.ppermute(value, axis, [(k, k ^ distance) for k in range(size)])]
  transfers between devices with their start and end apart: 7 -> 11, of which waited for: 6 -> 9; matrix products, arithmetic and copies ran while one was open for 8% -> 17% of each run, Pallas kernels for 2% -> 2%
where the time goes in v6:
time: 37 us; the launch traced here: 36.6 us
  starting transfers between devices  14.4 us (39%)
  waiting for transfers between devices  9.03 us (24%)
  Pallas kernels  4.62 us (12%)
  other arithmetic  3.99 us (11%)
  local copies, waits for them, and re-layouts  3.76 us (10%)
  between operations  0.87 us (2%)
    ppermute x11, starting transfers between devices, exchange(): return lax.ppermute(value, axis, [(k, k ^ distance) for k in range(size)])  14.4 us
    ppermute x11, waiting for transfers between devices, exchange(): return lax.ppermute(value, axis, [(k, k ^ distance) for k in range(size)])  9.03 us
    pallas_call x1, Pallas kernels, finish(): pl.pallas_call(functools.partial(finish_kernel, tile, span), out_shape=(j...  2.33 us
    reduce_sum x1, other arithmetic, per_device(): jnp.sum(weight_f * weight_f, axis=1) + 1e-06  2.21 us
    rev x3, local copies, waits for them, and re-layouts, per_device(): pairs = jnp.where(place & bit == 0, pairs, pairs[:, ::-1])  1.81 us
    pallas_call x1, Pallas kernels, encode(): pl.pallas_call(functools.partial(encode_kernel, own), out_shape=(jax.Shap...  1.26 us
    concatenate x1, other arithmetic, per_device(): jnp.concatenate([near, ordered[low]], axis=1)  0.78 us
    concatenate x1, other arithmetic, per_device(): near = jnp.concatenate([near, exchange(near, 'dp', distance)], axis=0)  0.76 us
  transfers between devices with their start and end apart: 11, of which 9 were waited for; matrix products, arithmetic and copies ran while one was open for 17% of the time, Pallas kernels for 2%

profile of v6, /device:TPU:0, one launch (start us, length us, event | category | flops | bytes accessed | tf_op | source)
XLA Modules:
  0.0 36.6 jit_solution(17700133631825910048)
XLA Ops:
  0.6 0.0 copy-start
  0.6 0.0 copy-start.3
  0.7 0.0 copy-start.2
  0.7 4.1 %collective-permute-start = (bf16[2,4608]{1,0:T(2,128)(2,1)}, bf16[2,4608]{1,0:T(2,128)(2,1)S(1)}, u32[]{:S(2)}, u32[]{:S(2)}) collective-permute-start(bf16[2,4608]{1,0:T(2,128)(2,1)} %param.6), channel_id=1, source_target_pairs={{0,8},{2,10},{4,12},{6,14},{8,0},{10,2},{12,4},{14,6},{1,9},{3,11}... | collective-permute-start | bytes 55304 | tf_op jit(solution)/shard_map/ppermute | solution.py:23
  4.8 2.2 %multiply_reduce_fusion = f32[256]{0:T(256)S(1)} fusion(bf16[256,4608]{1,0:T(8,128)(2,1)} %weight_ref.7), kind=kLoop, calls=%fused_computation | loop fusion | flops 3538688 | bytes 2360320 | tf_op jit(solution)/shard_map/reduce_sum | solution.py:374
  7.0 0.0 copy-done.3
  7.0 0.0 copy-start.1
  7.0 0.7 %copy-done.1 = bf16[16,576]{1,0:T(8,128)(2,1)S(1)} copy-done((bf16[16,576]{1,0:T(8,128)(2,1)S(1)}, bf16[16,576]{1,0:T(8,128)(2,1)}, u32[]{:S(2)}) %copy-start.1) | copy-done | bytes 18456
  7.7 0.2 order.1
  7.9 0.0 collective-permute-done
  7.9 0.8 %pad_maximum_fusion.4 = (bf16[4,5184]{1,0:T(4,128)(2,1)S(1)}, bf16[4,5184]{1,0:T(4,128)(2,1)S(1)}, bf16[4,5184]{1,0:T(4,128)(2,1)S(1)}) fusion(bf16[4,576]{1,0:T(4,128)(2,1)S(1)} %get-tuple-element.44, bf16[2,4608]{1,0:T(2,128)(2,1)S(1)} %collective-permute-done, bf16[2,4608]{1,0:T(2,128)(2,1)} %param.6, bf16[4,576]{1,0:T(4,128)(2,1)S(1)} %get-tuple-element.45, ...), kind=kLoop, calls=%fused_computation.8 | loop fusion | flops 248832 | bytes 175104 | tf_op jit(solution)/shard_map/concatenate | solution.py:370
  8.7 2.6 %collective-permute-start.3 = (bf16[4,5184]{1,0:T(4,128)(2,1)S(1)}, bf16[4,5184]{1,0:T(4,128)(2,1)S(1)}, u32[]{:S(2)}, u32[]{:S(2)}) collective-permute-start(bf16[4,5184]{1,0:T(4,128)(2,1)S(1)} %get-tuple-element.38), channel_id=1, source_target_pairs={{0,6},{2,4},{4,2},{6,0},{8,14},{10,12},{12,10},{14,8},{1,7},{3,5},... | collective-permute-start | bytes 124424 | tf_op jit(solution)/shard_map/ppermute | solution.py:23
  11.3 0.4 %collective-permute-start.2 = (bf16[4,5184]{1,0:T(4,128)(2,1)S(1)}, bf16[4,5184]{1,0:T(4,128)(2,1)S(1)}, u32[]{:S(2)}, u32[]{:S(2)}) collective-permute-start(bf16[4,5184]{1,0:T(4,128)(2,1)S(1)} %get-tuple-element.39), channel_id=1, source_target_pairs={{0,4},{2,6},{4,0},{6,2},{8,12},{10,14},{12,8},{14,10},{1,5},{3,7},... | collective-permute-start | bytes 124424 | tf_op jit(solution)/shard_map/ppermute | solution.py:23
  11.7 0.5 %collective-permute-start.1 = (bf16[4,5184]{1,0:T(4,128)(2,1)S(1)}, bf16[4,5184]{1,0:T(4,128)(2,1)S(1)}, u32[]{:S(2)}, u32[]{:S(2)}) collective-permute-start(bf16[4,5184]{1,0:T(4,128)(2,1)S(1)} %get-tuple-element.40), channel_id=1, source_target_pairs={{0,2},{2,0},{4,6},{6,4},{8,10},{10,8},{12,14},{14,12},{1,3},{3,1},... | collective-permute-start | bytes 124424 | tf_op jit(solution)/shard_map/ppermute | solution.py:23
  12.3 0.8 %pad_maximum_fusion.5.first_ref = bf16[4,4608]{1,0:T(4,128)(2,1)S(1)} fusion(bf16[2,4608]{1,0:T(2,128)(2,1)S(1)} %collective-permute-done, bf16[2,4608]{1,0:T(2,128)(2,1)} %param.6), kind=kLoop, calls=%fused_computation.9 | loop fusion | flops 73728 | bytes 73728 | tf_op jit(solution)/shard_map/concatenate | solution.py:366
  13.0 1.1 %collective-permute-done.3.fourth_ref = bf16[4,5184]{1,0:T(4,128)(2,1)S(1)} collective-permute-done((bf16[4,5184]{1,0:T(4,128)(2,1)S(1)}, bf16[4,5184]{1,0:T(4,128)(2,1)S(1)}, u32[]{:S(2)}, u32[]{:S(2)}) %collective-permute-start.3) | collective-permute-done | bytes 41504 | tf_op jit(solution)/shard_map/ppermute | solution.py:23
  14.1 1.2 %collective-permute-done.2.third_ref = bf16[4,5184]{1,0:T(4,128)(2,1)S(1)} collective-permute-done((bf16[4,5184]{1,0:T(4,128)(2,1)S(1)}, bf16[4,5184]{1,0:T(4,128)(2,1)S(1)}, u32[]{:S(2)}, u32[]{:S(2)}) %collective-permute-start.2) | collective-permute-done | bytes 41504 | tf_op jit(solution)/shard_map/ppermute | solution.py:23
  15.3 0.4 %collective-permute-done.1.second_ref = bf16[4,5184]{1,0:T(4,128)(2,1)S(1)} collective-permute-done((bf16[4,5184]{1,0:T(4,128)(2,1)S(1)}, bf16[4,5184]{1,0:T(4,128)(2,1)S(1)}, u32[]{:S(2)}, u32[]{:S(2)}) %collective-permute-start.1) | collective-permute-done | bytes 41504 | tf_op jit(solution)/shard_map/ppermute | solution.py:23
  15.7 0.0 copy-done
  15.7 0.0 copy-done.2
  15.7 0.0 copy-start.4
  15.7 1.3 %encode.1 = (bf16[16,2304]{1,0:T(8,128)(2,1)S(1)}, bf16[16,4608]{1,0:T(8,128)(2,1)S(1)}, f32[16,256]{1,0:T(8,128)S(1)}, f32[16,256]{1,0:T(8,128)S(1)}, f32[16,1]{1,0:T(8,128)S(1)}) custom-call(bf16[4,4608]{1,0:T(4,128)(2,1)S(1)} %pad_maximum_fusion.5.first_ref, bf16[4,5184]{1,0:T(4,128)(2,1)S(1)} %collective-permute-done.1.second_ref, ...), custom_call_target="tpu_custom_call" | custom-call | tf_op jit(solution)/shard_map/encode/pallas_call | solution.py:132
  17.0 0.0 collective-permute-start.4
  17.2 0.3 keep.1
  17.4 0.8 %collective-permute-done.4 = bf16[16,2304]{1,0:T(8,128)(2,1)S(1)} collective-permute-done((bf16[16,2304]{1,0:T(8,128)(2,1)S(1)}, bf16[16,2304]{1,0:T(8,128)(2,1)S(1)}, u32[]{:S(2)}, u32[]{:S(2)}) %collective-permute-start.4) | collective-permute-done | bytes 73760 | tf_op jit(solution)/shard_map/ppermute | solution.py:23
  18.3 1.6 %collective-permute-start.7 = (bf16[16,2304]{1,0:T(8,128)(2,1)S(1)}, bf16[16,2304]{1,0:T(8,128)(2,1)S(1)}, u32[]{:S(2)}, u32[]{:S(2)}) collective-permute-start(bf16[16,2304]{1,0:T(8,128)(2,1)S(1)} %get-tuple-element.34), channel_id=1, source_target_pairs={{0,6},{2,4},{4,2},{6,0},{8,14},{10,12},{12,10},{14,8},{1,7},{3,5},... | collective-permute-start | bytes 221192 | tf_op jit(solution)/shard_map/ppermute | solution.py:23
  19.9 0.4 %collective-permute-start.6 = (bf16[16,2304]{1,0:T(8,128)(2,1)S(1)}, bf16[16,2304]{1,0:T(8,128)(2,1)S(1)}, u32[]{:S(2)}, u32[]{:S(2)}) collective-permute-start(bf16[16,2304]{1,0:T(8,128)(2,1)S(1)} %get-tuple-element.34), channel_id=1, source_target_pairs={{0,4},{2,6},{4,0},{6,2},{8,12},{10,14},{12,8},{14,10},{1,5},{3,7},... | collective-permute-start | bytes 221192 | tf_op jit(solution)/shard_map/ppermute | solution.py:23
  20.4 1.5 %collective-permute-start.5 = (bf16[16,2304]{1,0:T(8,128)(2,1)S(1)}, bf16[16,2304]{1,0:T(8,128)(2,1)S(1)}, u32[]{:S(2)}, u32[]{:S(2)}) collective-permute-start(bf16[16,2304]{1,0:T(8,128)(2,1)S(1)} %get-tuple-element.34), channel_id=1, source_target_pairs={{0,2},{2,0},{4,6},{6,4},{8,10},{10,8},{12,14},{14,12},{1,3},{3,1},... | collective-permute-start | bytes 221192 | tf_op jit(solution)/shard_map/ppermute | solution.py:23
  21.9 2.1 %collective-permute-done.7.refs_2_ = bf16[16,2304]{1,0:T(8,128)(2,1)S(1)} collective-permute-done((bf16[16,2304]{1,0:T(8,128)(2,1)S(1)}, bf16[16,2304]{1,0:T(8,128)(2,1)S(1)}, u32[]{:S(2)}, u32[]{:S(2)}) %collective-permute-start.7) | collective-permute-done | bytes 73760 | tf_op jit(solution)/shard_map/ppermute | solution.py:23
  24.0 0.3 collective-permute-done.6.refs_1_
  24.3 0.9 %collective-permute-done.5.refs_0_ = bf16[16,2304]{1,0:T(8,128)(2,1)S(1)} collective-permute-done((bf16[16,2304]{1,0:T(8,128)(2,1)S(1)}, bf16[16,2304]{1,0:T(8,128)(2,1)S(1)}, u32[]{:S(2)}, u32[]{:S(2)}) %collective-permute-start.5) | collective-permute-done | bytes 73760 | tf_op jit(solution)/shard_map/ppermute | solution.py:23
  25.2 0.1 merge.1
  25.3 1.8 %collective-permute-start.10 = (bf16[1,4,2,576]{3,2,1,0:T(2,128)(2,1)S(1)}, bf16[1,4,2,576]{3,2,1,0:T(2,128)(2,1)S(1)}, u32[]{:S(2)}, u32[]{:S(2)}) collective-permute-start(bf16[1,4,2,576]{3,2,1,0:T(2,128)(2,1)S(1)} %get-tuple-element.42), channel_id=1, source_target_pairs={{0,8},{2,10},{4,12},{6,14},{8,0},{10,2},{12,4},{14,6},{1,9},{3,11}... | collective-permute-start | bytes 27656 | tf_op jit(solution)/shard_map/ppermute | solution.py:23
  27.1 0.0 copy-done.4
  27.1 0.1 copy.13.pull_ref
  27.2 1.3 %collective-permute-start.8 = (bf16[16,2304]{1,0:T(8,128)(2,1)S(1)}, bf16[16,2304]{1,0:T(8,128)(2,1)S(1)}, u32[]{:S(2)}, u32[]{:S(2)}) collective-permute-start(bf16[16,2304]{1,0:T(8,128)(2,1)S(1)} %get-tuple-element.25), channel_id=1, source_target_pairs={{0,8},{2,10},{4,12},{6,14},{8,0},{10,2},{12,4},{14,6},{1,9},{3,11}... | collective-permute-start | bytes 221192 | tf_op jit(solution)/shard_map/ppermute | solution.py:23
  28.5 1.4 %collective-permute-done.10 = bf16[1,4,2,576]{3,2,1,0:T(2,128)(2,1)S(1)} collective-permute-done((bf16[1,4,2,576]{3,2,1,0:T(2,128)(2,1)S(1)}, bf16[1,4,2,576]{3,2,1,0:T(2,128)(2,1)S(1)}, u32[]{:S(2)}, u32[]{:S(2)}) %collective-permute-start.10) | collective-permute-done | bytes 9248 | tf_op jit(solution)/shard_map/ppermute | solution.py:23
  30.0 0.1 reshape_squeeze.3
  30.1 0.3 rev.9
  30.4 0.5 %rev.10 = bf16[2,2,2304]{2,1,0:T(2,128)(2,1)S(1)} reverse(bf16[2,2,2304]{2,1,0:T(2,128)(2,1)S(1)} %reshape_reshape.6), dimensions={1} | reverse | bytes 36864 | tf_op jit(solution)/shard_map/rev | solution.py:407
  31.0 0.9 %rev.11 = bf16[1,2,4608]{2,1,0:T(2,128)(2,1)S(1)} reverse(bf16[1,2,4608]{2,1,0:T(2,128)(2,1)S(1)} %reshape_reshape.7), dimensions={1} | reverse | bytes 36864 | tf_op jit(solution)/shard_map/rev | solution.py:407
  32.0 0.8 %collective-permute-done.8.arrived_ref = bf16[16,2304]{1,0:T(8,128)(2,1)S(1)} collective-permute-done((bf16[16,2304]{1,0:T(8,128)(2,1)S(1)}, bf16[16,2304]{1,0:T(8,128)(2,1)S(1)}, u32[]{:S(2)}, u32[]{:S(2)}) %collective-permute-start.8) | collective-permute-done | bytes 73760 | tf_op jit(solution)/shard_map/ppermute | solution.py:23
  32.8 0.1 settle.1.grad_ref
  32.9 0.1 collective-permute-start.9
  33.0 0.1 reshape.69
  33.1 0.7 %reshape.70 = bf16[2,4608]{1,0:T(2,128)(2,1)} reshape(bf16[2,8,576]{2,1,0:T(8,128)(2,1)S(1)} %copy.15) | data formatting | bytes 36864 | tf_op jit(solution)/shard_map/reshape | solution.py:410
  33.8 0.4 %early.1.early_ref = f32[16,256]{1,0:T(8,128)S(1)} custom-call(bf16[16,2304]{1,0:T(8,128)(2,1)S(1)} %settle.1.grad_ref, bf16[256,4608]{1,0:T(8,128)(2,1)S(1)} %copy-done, f32[1,256]{1,0:T(1,128)S(1)} %bitcast.19), custom_call_target="tpu_custom_call" | custom-call | flops 18874368 | bytes 589824 | tf_op jit(solution)/shard_map/early/pallas_call | solution.py:240
  34.2 0.0 collective-permute-done.9
  34.3 2.3 %finish.1 = (bf16[256,4608]{1,0:T(8,128)(2,1)}, f32[1,256]{1,0:T(1,128)}, f32[288]{0:T(512)}) custom-call(bf16[16,4608]{1,0:T(8,128)(2,1)S(1)} %pad_maximum_fusion.grad_ref, f32[16,256]{1,0:T(8,128)S(1)} %early.1.early_ref, bf16[16,4608]{1,0:T(8,128)(2,1)S(1)} %get-tuple-element.26.rows_ref, bf16[256,4608]{1,0:T(8,128)(2,1)S(1)} %copy-done, ...), custom_call_target="tpu_custom_call" | custom-call | tf_op jit(solution)/shard_map/finish/pallas_call | solution.py:332
  (22 shorter events, 0.4 us)
Async XLA Ops:
  0.6 15.1 %copy-start = (bf16[256,4608]{1,0:T(8,128)(2,1)S(1)}, bf16[256,4608]{1,0:T(8,128)(2,1)}, u32[]{:S(2)}) copy-start(bf16[256,4608]{1,0:T(8,128)(2,1)} %weight_ref.7) | copy-start | bytes 7077892
  0.6 6.3 %copy-start.3 = (s32[16]{0:T(128)S(1)}, s32[16]{0:T(128)}, u32[]{:S(2)}) copy-start(s32[16]{0:T(128)} %param.8) | copy-start | bytes 196
  0.7 15.1 %copy-start.2 = (f32[256]{0:T(256)S(1)}, f32[256]{0:T(256)}, u32[]{:S(2)}) copy-start(f32[256]{0:T(256)} %param.10) | copy-start | bytes 3076
  0.7 7.2 %collective-permute-start = (bf16[2,4608]{1,0:T(2,128)(2,1)}, bf16[2,4608]{1,0:T(2,128)(2,1)S(1)}, u32[]{:S(2)}, u32[]{:S(2)}) collective-permute-start(bf16[2,4608]{1,0:T(2,128)(2,1)} %param.6), channel_id=1, source_target_pairs={{0,8},{2,10},{4,12},{6,14},{8,0},{10,2},{12,4},{14,6},{1,9},{3,11}... | collective-permute-start | bytes 55304 | tf_op jit(solution)/shard_map/ppermute | solution.py:23
  7.0 0.7 %copy-start.1 = (bf16[16,576]{1,0:T(8,128)(2,1)S(1)}, bf16[16,576]{1,0:T(8,128)(2,1)}, u32[]{:S(2)}) copy-start(bf16[16,576]{1,0:T(8,128)(2,1)} %cached_hbm.1) | copy-start | bytes 55300
  8.7 5.4 %collective-permute-start.3 = (bf16[4,5184]{1,0:T(4,128)(2,1)S(1)}, bf16[4,5184]{1,0:T(4,128)(2,1)S(1)}, u32[]{:S(2)}, u32[]{:S(2)}) collective-permute-start(bf16[4,5184]{1,0:T(4,128)(2,1)S(1)} %get-tuple-element.38), channel_id=1, source_target_pairs={{0,6},{2,4},{4,2},{6,0},{8,14},{10,12},{12,10},{14,8},{1,7},{3,5},... | collective-permute-start | bytes 124424 | tf_op jit(solution)/shard_map/ppermute | solution.py:23
  11.3 4.0 %collective-permute-start.2 = (bf16[4,5184]{1,0:T(4,128)(2,1)S(1)}, bf16[4,5184]{1,0:T(4,128)(2,1)S(1)}, u32[]{:S(2)}, u32[]{:S(2)}) collective-permute-start(bf16[4,5184]{1,0:T(4,128)(2,1)S(1)} %get-tuple-element.39), channel_id=1, source_target_pairs={{0,4},{2,6},{4,0},{6,2},{8,12},{10,14},{12,8},{14,10},{1,5},{3,7},... | collective-permute-start | bytes 124424 | tf_op jit(solution)/shard_map/ppermute | solution.py:23
  11.7 4.0 %collective-permute-start.1 = (bf16[4,5184]{1,0:T(4,128)(2,1)S(1)}, bf16[4,5184]{1,0:T(4,128)(2,1)S(1)}, u32[]{:S(2)}, u32[]{:S(2)}) collective-permute-start(bf16[4,5184]{1,0:T(4,128)(2,1)S(1)} %get-tuple-element.40), channel_id=1, source_target_pairs={{0,2},{2,0},{4,6},{6,4},{8,10},{10,8},{12,14},{14,12},{1,3},{3,1},... | collective-permute-start | bytes 124424 | tf_op jit(solution)/shard_map/ppermute | solution.py:23
  15.7 11.3 %copy-start.4 = (f32[4608]{0:T(1024)S(1)}, f32[4608]{0:T(1024)}, u32[]{:S(2)}) copy-start(f32[4608]{0:T(1024)} %param.11) | copy-start | bytes 55300
  17.0 1.3 %collective-permute-start.4 = (bf16[16,2304]{1,0:T(8,128)(2,1)S(1)}, bf16[16,2304]{1,0:T(8,128)(2,1)S(1)}, u32[]{:S(2)}, u32[]{:S(2)}) collective-permute-start(bf16[16,2304]{1,0:T(8,128)(2,1)S(1)} %get-tuple-element.22), channel_id=1, source_target_pairs={{0,1},{1,0},{2,3},{3,2},{4,5},{5,4},{6,7},{7,6},{8,9},{9,8},{10,11... | collective-permute-start | bytes 221192 | tf_op jit(solution)/shard_map/ppermute | solution.py:23
  18.3 5.7 %collective-permute-start.7 = (bf16[16,2304]{1,0:T(8,128)(2,1)S(1)}, bf16[16,2304]{1,0:T(8,128)(2,1)S(1)}, u32[]{:S(2)}, u32[]{:S(2)}) collective-permute-start(bf16[16,2304]{1,0:T(8,128)(2,1)S(1)} %get-tuple-element.34), channel_id=1, source_target_pairs={{0,6},{2,4},{4,2},{6,0},{8,14},{10,12},{12,10},{14,8},{1,7},{3,5},... | collective-permute-start | bytes 221192 | tf_op jit(solution)/shard_map/ppermute | solution.py:23
  19.9 4.4 %collective-permute-start.6 = (bf16[16,2304]{1,0:T(8,128)(2,1)S(1)}, bf16[16,2304]{1,0:T(8,128)(2,1)S(1)}, u32[]{:S(2)}, u32[]{:S(2)}) collective-permute-start(bf16[16,2304]{1,0:T(8,128)(2,1)S(1)} %get-tuple-element.34), channel_id=1, source_target_pairs={{0,4},{2,6},{4,0},{6,2},{8,12},{10,14},{12,8},{14,10},{1,5},{3,7},... | collective-permute-start | bytes 221192 | tf_op jit(solution)/shard_map/ppermute | solution.py:23
  20.4 4.8 %collective-permute-start.5 = (bf16[16,2304]{1,0:T(8,128)(2,1)S(1)}, bf16[16,2304]{1,0:T(8,128)(2,1)S(1)}, u32[]{:S(2)}, u32[]{:S(2)}) collective-permute-start(bf16[16,2304]{1,0:T(8,128)(2,1)S(1)} %get-tuple-element.34), channel_id=1, source_target_pairs={{0,2},{2,0},{4,6},{6,4},{8,10},{10,8},{12,14},{14,12},{1,3},{3,1},... | collective-permute-start | bytes 221192 | tf_op jit(solution)/shard_map/ppermute | solution.py:23
  25.3 4.6 %collective-permute-start.10 = (bf16[1,4,2,576]{3,2,1,0:T(2,128)(2,1)S(1)}, bf16[1,4,2,576]{3,2,1,0:T(2,128)(2,1)S(1)}, u32[]{:S(2)}, u32[]{:S(2)}) collective-permute-start(bf16[1,4,2,576]{3,2,1,0:T(2,128)(2,1)S(1)} %get-tuple-element.42), channel_id=1, source_target_pairs={{0,8},{2,10},{4,12},{6,14},{8,0},{10,2},{12,4},{14,6},{1,9},{3,11}... | collective-permute-start | bytes 27656 | tf_op jit(solution)/shard_map/ppermute | solution.py:23
  27.2 5.5 %collective-permute-start.8 = (bf16[16,2304]{1,0:T(8,128)(2,1)S(1)}, bf16[16,2304]{1,0:T(8,128)(2,1)S(1)}, u32[]{:S(2)}, u32[]{:S(2)}) collective-permute-start(bf16[16,2304]{1,0:T(8,128)(2,1)S(1)} %get-tuple-element.25), channel_id=1, source_target_pairs={{0,8},{2,10},{4,12},{6,14},{8,0},{10,2},{12,4},{14,6},{1,9},{3,11}... | collective-permute-start | bytes 221192 | tf_op jit(solution)/shard_map/ppermute | solution.py:23
  32.9 1.4 %collective-permute-start.9 = (bf16[16,2304]{1,0:T(8,128)(2,1)S(1)}, bf16[16,2304]{1,0:T(8,128)(2,1)S(1)}, u32[]{:S(2)}, u32[]{:S(2)}) collective-permute-start(bf16[16,2304]{1,0:T(8,128)(2,1)S(1)} %settle.1.grad_ref), channel_id=1, source_target_pairs={{0,1},{1,0},{2,3},{3,2},{4,5},{5,4},{6,7},{7,6},{8,9},{9,8},{10,11... | collective-permute-start | bytes 221192 | tf_op jit(solution)/shard_map/ppermute | solution.py:23

commit v7 on v6

--- a/solution.py
+++ b/solution.py
@@ -43,12 +43,26 @@
     return value
 
 
-def order_kernel(own, cached_hbm, perm_hbm, out_ref, cached_ref, perm_ref, sems):
+def order_kernel(
+    cur_hbm,
+    cached_hbm,
+    perm_hbm,
+    weight_hbm,
+    out_ref,
+    cur_ref,
+    weight_ref,
+    cached_ref,
+    perm_ref,
+    sems,
+):
     row_total, columns = cached_ref.shape
+    own = cur_ref.shape[0]
     dp = row_total // own
     fetches = [
         pltpu.make_async_copy(cached_hbm, cached_ref, sems.at[0]),
         pltpu.make_async_copy(perm_hbm, perm_ref, sems.at[1]),
+        pltpu.make_async_copy(cur_hbm, cur_ref, sems.at[2]),
+        pltpu.make_async_copy(weight_hbm, weight_ref, sems.at[3]),
     ]
     for fetch in fetches:
         fetch.start()
@@ -56,30 +70,41 @@
     rest = dp // 4
     distance = row // (rest * own) + 4 * (row // own % rest)
     wanted = (distance ^ lax.axis_index("dp")) * own + row % own
-    for fetch in fetches:
+    for fetch in fetches[:2]:
         fetch.wait()
     selector = (jnp.broadcast_to(perm_ref[...], row.shape) == wanted).astype(jnp.bfloat16)
     out_ref[...] = jnp.dot(
         selector, cached_ref[...], preferred_element_type=jnp.float32
     ).astype(jnp.bfloat16)
-
-
-def order(cached_rows, shuffle_perm, own):
+    for fetch in fetches[2:]:
+        fetch.wait()
+
+
+def order(cur_rows, cached_rows, shuffle_perm, weight):
     row_total, columns = cached_rows.shape
     return pl.pallas_call(
-        functools.partial(order_kernel, own),
-        out_shape=jax.ShapeDtypeStruct((row_total, columns), jnp.bfloat16),
-        in_specs=[whole(pl.ANY)] * 2,
-        out_specs=whole(),
+        order_kernel,
+        out_shape=(
+            jax.ShapeDtypeStruct((row_total, columns), jnp.bfloat16),
+            jax.ShapeDtypeStruct(cur_rows.shape, jnp.bfloat16),
+            jax.ShapeDtypeStruct(weight.shape, jnp.bfloat16),
+        ),
+        in_specs=[whole(pl.ANY)] * 4,
+        out_specs=[whole()] * 3,
         scratch_shapes=[
             pltpu.VMEM((row_total, columns), jnp.bfloat16),
             pltpu.VMEM((1, row_total), jnp.int32),
-            pltpu.SemaphoreType.DMA((2,)),
+            pltpu.SemaphoreType.DMA((4,)),
         ],
         compiler_params=pltpu.CompilerParams(vmem_limit_bytes=VMEM_BYTES),
         cost_estimate=pl.CostEstimate(flops=4000000, bytes_accessed=2000000, transcendentals=0),
         name="order",
-    )(cached_rows, shuffle_perm.reshape(1, row_total))
+    )(
+        *(
+            pltpu.with_memory_space_constraint(value, pltpu.MemorySpace.HBM)
+            for value in (cur_rows, cached_rows, shuffle_perm.reshape(1, row_total), weight)
+        )
+    )
 
 
 def encode_kernel(
@@ -146,67 +171,104 @@
     )(*parts, weight, enc_bias.reshape(1, count))
 
 
-def keep_kernel(latents_ref, sharp_ref, weight_ref, norms_ref, mine_ref, gate_ref, pull_ref):
-    rows_total = latents_ref.shape[0]
+def keep_kernel(rides, latents_ref, sharp_ref, weight_ref, *refs):
     half = weight_ref.shape[1] // 2
     latents = latents_ref[...]
+    if rides:
+        *refs, leaving_ref, staying_ref, packed_ref = refs
+    *sources, mine_ref, gate_ref, norms_ref, pull_ref = refs
     here, _ = core_columns(half)
     mine_ref[...] = jnp.dot(
         latents.astype(jnp.bfloat16), weight_ref[:, here], preferred_element_type=jnp.float32
     )
     gate_ref[...] = jax.nn.sigmoid(sharp_ref[...])
+    weight_f = weight_ref[...].astype(jnp.float32)
+    squares = jnp.sum(weight_f * weight_f, axis=1, keepdims=True)
+    squares = jnp.broadcast_to(squares, (squares.shape[0], 128)).T
+    norms = jnp.sqrt(squares[:1] + 1e-06)
+    norms_ref[...] = norms
     counts = jnp.sum(latents, axis=0, keepdims=True)
-    pull_ref[...] = SPARSITY / (rows_total // 2) * counts / norms_ref[...]
-
-
-def keep(latents, sharp, weight, norms):
+    pull = SPARSITY / (latents.shape[0] // 2) * counts / norms
+    pull_ref[...] = jnp.broadcast_to(pull, squares.shape).T[:, :1]
+    if rides:
+        own = staying_ref.shape[1]
+        shares = packed_ref.shape[1]
+        below = len(sources) * own
+        for index, ref in enumerate(sources):
+            start = ref.shape[1] - 2 * shares
+            value = ref[:, start:].astype(jnp.float32)
+            staying_ref[index] = value[:own]
+            rows = slice(index * own, (index + 1) * own)
+            packed_ref[rows] = value[own:, :shares]
+            rows = slice(below + index * own, below + (index + 1) * own)
+            packed_ref[rows] = value[own:, shares:]
+        leaving_ref[...] = packed_ref[...].astype(jnp.bfloat16)
+
+
+def keep(latents, sharp, weight, sources, own, shares):
     rows_total, count = latents.shape
     width = weight.shape[1]
     f32 = jnp.float32
-    return pl.pallas_call(
-        keep_kernel,
-        out_shape=(
-            jax.ShapeDtypeStruct((rows_total, width // 2), f32),
-            jax.ShapeDtypeStruct((rows_total, count), f32),
-            jax.ShapeDtypeStruct((1, count), f32),
-        ),
-        in_specs=[whole()] * 4,
-        out_specs=[whole()] * 3,
+    out_shape = [
+        jax.ShapeDtypeStruct((rows_total, width // 2), f32),
+        jax.ShapeDtypeStruct((rows_total, count), f32),
+        jax.ShapeDtypeStruct((1, count), f32),
+        jax.ShapeDtypeStruct((count, 1), f32),
+    ]
+    scratch = []
+    if sources:
+        out_shape += [
+            jax.ShapeDtypeStruct((rows_total, shares), jnp.bfloat16),
+            jax.ShapeDtypeStruct((len(sources), own, 2 * shares), f32),
+        ]
+        scratch = [pltpu.VMEM((rows_total, shares), f32)]
+    return pl.pallas_call(
+        functools.partial(keep_kernel, bool(sources)),
+        out_shape=out_shape,
+        in_specs=[whole()] * (3 + len(sources)),
+        out_specs=[whole()] * len(out_shape),
+        scratch_shapes=scratch,
         compiler_params=pltpu.CompilerParams(vmem_limit_bytes=VMEM_BYTES),
         cost_estimate=pl.CostEstimate(
             flops=rows_total * count * width, bytes_accessed=count * width, transcendentals=0
         ),
         name="keep",
-    )(latents, sharp, weight, norms)
+    )(latents, sharp, weight, *sources)
 
 
 def merge_kernel(distances, total_ref, *refs):
     total = total_ref[...]
     for distance, ref in zip(distances, refs):
         total = total + flip_rows(ref[...].astype(jnp.float32), distance)
-    sum_ref, sent_ref = refs[len(distances) :]
+    *riders, sum_ref, sent_ref = refs[len(distances) :]
     sum_ref[...] = total
-    sent_ref[...] = total.astype(jnp.bfloat16)
-
-
-def merge(total, arrived, distances):
+    half = total.shape[1]
+    sent_ref[:, :half] = total.astype(jnp.bfloat16)
+    for rider in riders:
+        sent_ref[:, half:] = rider[...]
+
+
+def merge(total, arrived, distances, riders=()):
+    rows_total, half = total.shape
+    wide = half + sum(rider.shape[1] for rider in riders)
     return pl.pallas_call(
         functools.partial(merge_kernel, distances),
         out_shape=(
             jax.ShapeDtypeStruct(total.shape, jnp.float32),
-            jax.ShapeDtypeStruct(total.shape, jnp.bfloat16),
-        ),
-        in_specs=[whole()] * (1 + len(arrived)),
+            jax.ShapeDtypeStruct((rows_total, wide), jnp.bfloat16),
+        ),
+        in_specs=[whole()] * (1 + len(arrived) + len(riders)),
         out_specs=[whole()] * 2,
         compiler_params=pltpu.CompilerParams(vmem_limit_bytes=VMEM_BYTES),
         name="merge",
-    )(total, *arrived)
+    )(total, *arrived, *riders)
 
 
 def settle_kernel(distance, total_ref, arrived_ref, rows_ref, scales_ref, bias_ref, grad_ref):
     rows_total, width = rows_ref.shape
     here, _ = core_columns(width // 2)
-    total = total_ref[...] + flip_rows(arrived_ref[...].astype(jnp.float32), distance)
+    arrived = arrived_ref[:, : width // 2].astype(jnp.float32)
+    total = total_ref[...] + flip_rows(arrived, distance)
     target = rows_ref[:, here].astype(jnp.float32) * scales_ref[...]
     error = total + bias_ref[:, here] - target
     grad_ref[...] = (2.0 / (rows_total // 2) * error).astype(jnp.bfloat16)
@@ -253,6 +315,7 @@
 def finish_kernel(
     tile,
     span,
+    rides,
     grad_ref,
     early_ref,
     rows_ref,
@@ -261,16 +324,16 @@
     gate_ref,
     scales_ref,
     pull_ref,
-    weight_grad_hbm,
-    bias_grad_hbm,
-    dec_grad_hbm,
-    staged_ref,
-    bias_ref,
-    dec_ref,
-    sums_ref,
-    left_ref,
-    sems,
+    *refs,
 ):
+    if rides:
+        arrived_ref, staying_ref, weight_grad_hbm, bias_grad_hbm, dec_grad_hbm, next_hbm = refs[:6]
+        staged_ref, bias_ref, dec_ref, sums_ref, left_ref, sems, blocks_ref, line_ref, next_ref = (
+            refs[6:]
+        )
+    else:
+        weight_grad_hbm, bias_grad_hbm, dec_grad_hbm = refs[:3]
+        staged_ref, bias_ref, dec_ref, sums_ref, left_ref, sems = refs[3:]
     rows_total, width = rows_ref.shape
     shares = dec_grad_hbm.shape[0]
     count = width // tile
@@ -297,6 +360,22 @@
     dec_copy = pltpu.make_async_copy(dec_ref, dec_grad_hbm, sems.at[count + 1])
     dec_copy.start()
 
+    if rides:
+        near, own, columns = staying_ref.shape
+        came = arrived_ref[:, width // 2 :].astype(jnp.float32)
+        for index in range(near):
+            blocks_ref[index] = staying_ref[index]
+            rows = slice(index * own, (index + 1) * own)
+            blocks_ref[near + index, :, :shares] = came[rows]
+            rows = slice((near + index) * own, (near + index + 1) * own)
+            blocks_ref[near + index, :, shares:] = came[rows]
+        place = lax.axis_index("dp")
+        for source in range(2 * near):
+            line_ref[:, source * columns : (source + 1) * columns] = blocks_ref[place ^ source]
+        next_ref[...] = line_ref[...].astype(jnp.bfloat16)
+        next_copy = pltpu.make_async_copy(next_ref, next_hbm, sems.at[count + 2])
+        next_copy.start()
+
     copies = [
         pltpu.make_async_copy(
             staged_ref.at[:, pl.ds(index * tile, tile)],
@@ -321,34 +400,63 @@
         copy.wait()
     bias_copy.wait()
     dec_copy.wait()
-
-
-def finish(grad_out, early_sum, rows, weight, latents, gate, scales, pull, shares):
+    if rides:
+        next_copy.wait()
+
+
+def finish(grad_out, early_sum, rows, weight, latents, gate, scales, pull, shares, riders):
     rows_total, width = rows.shape
     count = weight.shape[0]
     tile = 768
     span = (shares + 127 + 127) // 128 * 128
     f32 = jnp.float32
-    return pl.pallas_call(
-        functools.partial(finish_kernel, tile, span),
-        out_shape=(
-            jax.ShapeDtypeStruct((count, width), jnp.bfloat16),
-            jax.ShapeDtypeStruct((1, count), f32),
-            jax.ShapeDtypeStruct((shares,), f32),
-        ),
-        in_specs=[whole()] * 8,
-        out_specs=[whole(pl.ANY)] * 3,
-        scratch_shapes=[
-            pltpu.VMEM((count, width), jnp.bfloat16),
-            pltpu.VMEM((1, count), f32),
-            pltpu.VMEM((shares,), f32),
-            pltpu.VMEM((8, width + span), f32),
-            pltpu.VMEM((count, 2 * rows_total), jnp.bfloat16),
-            pltpu.SemaphoreType.DMA((width // tile + 2,)),
-        ],
+    out_shape = [
+        jax.ShapeDtypeStruct((count, width), jnp.bfloat16),
+        jax.ShapeDtypeStruct((1, count), f32),
+        jax.ShapeDtypeStruct((shares,), f32),
+    ]
+    scratch = [
+        pltpu.VMEM((count, width), jnp.bfloat16),
+        pltpu.VMEM((1, count), f32),
+        pltpu.VMEM((shares,), f32),
+        pltpu.VMEM((8, width + span), f32),
+        pltpu.VMEM((count, 2 * rows_total), jnp.bfloat16),
+        pltpu.SemaphoreType.DMA((width // tile + 3,)),
+    ]
+    if riders:
+        near, own, columns = riders[1].shape
+        out_shape.append(jax.ShapeDtypeStruct((own, width), jnp.bfloat16))
+        scratch += [
+            pltpu.VMEM((2 * near, own, columns), f32),
+            pltpu.VMEM((own, width), f32),
+            pltpu.VMEM((own, width), jnp.bfloat16),
+        ]
+    return pl.pallas_call(
+        functools.partial(finish_kernel, tile, span, bool(riders)),
+        out_shape=out_shape,
+        in_specs=[whole()] * (8 + len(riders)),
+        out_specs=[whole(pl.ANY)] * len(out_shape),
+        scratch_shapes=scratch,
         compiler_params=pltpu.CompilerParams(vmem_limit_bytes=VMEM_BYTES),
         name="finish",
-    )(grad_out, early_sum, rows, weight, latents, gate, scales, pull)
+    )(grad_out, early_sum, rows, weight, latents, gate, scales, pull, *riders)
+
+
+def shuffle_rest(riders, dp, own, columns):
+    place = lax.axis_index("dp")
+    distance = 4
+    while distance < dp:
+        split = riders.reshape((-1, 2) + riders.shape[1:])
+        riders = jnp.concatenate([split[:, 0], exchange(split[:, 1], "dp", distance)], axis=1)
+        distance *= 2
+    riders = riders[0]
+    bit = 1
+    while bit < dp:
+        pairs = riders.reshape(dp // (2 * bit), 2, bit * own * columns)
+        pairs = jnp.where(place & bit == 0, pairs, pairs[:, ::-1])
+        riders = pairs.reshape(dp, own, columns)
+        bit *= 2
+    return riders.transpose(1, 0, 2).reshape(own, dp * columns)
 
 
 def per_device(cur_rows, cached_rows, shuffle_perm, weight, enc_bias, dec_bias):
@@ -357,24 +465,26 @@
     own, width = cur_rows.shape
     columns = cached_rows.shape[1]
     count = weight.shape[0]
-    place = lax.axis_index("dp")
+    shares = width // (2 * dp)
     core = lax.axis_index("latent")
 
-    near = cur_rows
-    distance = 4
+    came = exchange(cur_rows, "dp", 4)
+    ordered, cur_copy, weight = order(cur_rows, cached_rows, shuffle_perm, weight)
+    near = jnp.concatenate([cur_copy, came], axis=0)
+    distance = 8
     while distance < dp:
         near = jnp.concatenate([near, exchange(near, "dp", distance)], axis=0)
         distance *= 2
-    ordered = order(cached_rows, shuffle_perm, own).reshape(4, rest * own, columns)
+    ordered = ordered.reshape(4, rest * own, columns)
     parts = [near] + [
         exchange(jnp.concatenate([near, ordered[low]], axis=1), "dp", low) for low in range(1, 4)
     ]
 
-    weight_f = weight.astype(jnp.float32)
-    norms = jnp.sqrt(jnp.sum(weight_f * weight_f, axis=1) + 1e-06).reshape(1, count)
     send, gathered, latents, sharp, scales = encode(parts, weight, enc_bias, own)
     came = exchange(send, "latent", 1)
-    mine, gate, pull = keep(latents, sharp, weight, norms)
+    rides = rest == 2
+    sources = [ordered[0]] + parts[1:] if rides else []
+    mine, gate, norms, pull, *riders = keep(latents, sharp, weight, sources, own, shares)
 
     total = mine + came.astype(jnp.float32)
     sent = total.astype(jnp.bfloat16)
@@ -383,16 +493,11 @@
         total,
         [exchange(sent, "dp", low) for low in lows],
         tuple(low * rest * own for low in lows),
-    )
-
-    riders = jnp.stack([ordered[0]] + [part[:, width:] for part in parts[1:]])
-    riders = riders.reshape(4, rest, own, columns).transpose(1, 0, 2, 3)
-    riders, sent = lax.optimization_barrier((riders, sent))
+        riders[:1],
+    )
     distance = 4
     while distance < dp:
         arrived = exchange(sent, "dp", distance)
-        split = riders.reshape((-1, 2) + riders.shape[1:])
-        riders = jnp.concatenate([split[:, 0], exchange(split[:, 1], "dp", distance)], axis=1)
         row_distance = distance // 4 * own
         if 2 * distance < dp:
             total, sent = merge(total, [arrived], (row_distance,))
@@ -400,23 +505,12 @@
             grad_mine = settle(total, arrived, gathered, scales, dec_bias, row_distance)
         distance *= 2
 
-    riders = riders[0]
-    bit = 1
-    while bit < dp:
-        pairs = riders.reshape(dp // (2 * bit), 2, bit * own * columns)
-        pairs = jnp.where(place & bit == 0, pairs, pairs[:, ::-1])
-        riders = pairs.reshape(dp, own, columns)
-        bit *= 2
-    next_batch = riders.transpose(1, 0, 2).reshape(own, dp * columns)
-
     grad_other = exchange(grad_mine, "latent", 1)
     early_sum = early(grad_mine, weight, norms)
     low_half = jnp.where(core == 0, grad_mine, grad_other)
     high_half = jnp.where(core == 0, grad_other, grad_mine)
     grad_out = jnp.concatenate([low_half, high_half], axis=1)
-
-    shares = width // (2 * dp)
-    weight_grad, enc_bias_grad, dec_bias_grad = finish(
+    weight_grad, enc_bias_grad, dec_bias_grad, *shuffled = finish(
         grad_out,
         early_sum,
         gathered,
@@ -424,9 +518,16 @@
         latents,
         gate,
         scales,
-        pull.reshape(count, 1),
+        pull,
         shares,
-    )
+        (arrived, riders[1]) if rides else (),
+    )
+    if rides:
+        next_batch = shuffled[0]
+    else:
+        riders = jnp.stack([ordered[0]] + [part[:, width:] for part in parts[1:]])
+        riders = riders.reshape(4, rest, own, columns).transpose(1, 0, 2, 3)
+        next_batch = shuffle_rest(riders, dp, own, columns)
     return (weight_grad, enc_bias_grad.reshape(count), dec_bias_grad, next_batch)
 
 

time: 37 us -> 34.8 us (0.941)
  waiting for transfers between devices: 9.03 us -> 13.2 us
  other arithmetic: 3.99 us -> 0.15 us
  local copies, waits for them, and re-layouts: 3.76 us -> 0.03 us
  Pallas kernels: 4.62 us -> 6.63 us
  starting transfers between devices: 14.4 us -> 13.9 us
    ppermute x11 -> x10, waiting for transfers between devices: 9.03 us -> 13.2 us  [exchange(): return lax.ppermute(value, axis, [(k, k ^ distance) for k in range(size)])]
    reduce_sum x1 -> x0, other arithmetic: 2.21 us -> none  [per_device(): jnp.sum(weight_f * weight_f, axis=1) + 1e-06]
    pallas_call x3, Pallas kernels: 2.78 us -> 4.77 us  [the longest x1 2.32 us: finish(): pl.pallas_call(functools.partial(finish_kernel, tile, span, bool(riders))...]
    rev x3 -> x0, local copies, waits for them, and re-layouts: 1.81 us -> none  [per_device(): pairs = jnp.where(place & bit == 0, pairs, pairs[:, ::-1])]
    reshape x3 -> x0, local copies, waits for them, and re-layouts: 0.93 us -> none  [the longest x1 0.7 us: per_device(): next_batch = riders.transpose(1, 0, 2).reshape(own, dp * columns)]
    concatenate x2 -> x1, other arithmetic: 0.8 us -> 0.04 us  [per_device(): near = jnp.concatenate([cur_copy, came], axis=0)]
    unnamed x10 -> x4, local copies, waits for them, and re-layouts: 0.74 us -> 0.01 us
    concatenate x1, other arithmetic: 0.78 us -> 0.06 us  [per_device(): jnp.concatenate([near, ordered[low]], axis=1)]
  transfers between devices with their start and end apart: 11 -> 10, of which waited for: 9 -> 10; matrix products, arithmetic and copies ran while one was open for 17% -> 0% of each run, Pallas kernels for 2% -> 8%
where the time goes in v7:
time: 34.8 us; the launch traced here: 34.7 us
  starting transfers between devices  13.9 us (40%)
  waiting for transfers between devices  13.2 us (38%)
  Pallas kernels  6.63 us (19%)
  between operations  0.72 us (2%)
    ppermute x10, starting transfers between devices, exchange(): return lax.ppermute(value, axis, [(k, k ^ distance) for k in range(size)])  13.9 us
    ppermute x10, waiting for transfers between devices, exchange(): return lax.ppermute(value, axis, [(k, k ^ distance) for k in range(size)])  13.2 us
    pallas_call x1, Pallas kernels, finish(): pl.pallas_call(functools.partial(finish_kernel, tile, span, bool(riders))...  2.32 us
    pallas_call x1, Pallas kernels, order(): pl.pallas_call(order_kernel, out_shape=(jax.ShapeDtypeStruct((row_total,...  1.75 us
    pallas_call x1, Pallas kernels, encode(): pl.pallas_call(functools.partial(encode_kernel, own), out_shape=(jax.Shap...  1.26 us
    pallas_call x1, Pallas kernels, keep(): pl.pallas_call(functools.partial(keep_kernel, bool(sources)), out_shape=o...  0.7 us
  transfers between devices with their start and end apart: 10, of which 10 were waited for; matrix products, arithmetic and copies ran while one was open for 0% of the time, Pallas kernels for 8%

profile of v7, /device:TPU:0, one launch (start us, length us, event | category | flops | bytes accessed | tf_op | source)
XLA Modules:
  0.0 34.7 jit_solution(11867103759431826665)
XLA Ops:
  0.6 0.0 copy-start
  0.6 4.1 %collective-permute-start = (bf16[2,4608]{1,0:T(2,128)(2,1)}, bf16[2,4608]{1,0:T(2,128)(2,1)S(1)}, u32[]{:S(2)}, u32[]{:S(2)}) collective-permute-start(bf16[2,4608]{1,0:T(2,128)(2,1)} %cur_hbm.1), channel_id=1, source_target_pairs={{0,8},{2,10},{4,12},{6,14},{8,0},{10,2},{12,4},{14,6},{1,9},{3,11}... | collective-permute-start | bytes 55304 | tf_op jit(solution)/shard_map/ppermute | solution.py:23
  4.7 1.8 %order.1 = (bf16[16,576]{1,0:T(8,128)(2,1)S(1)}, bf16[2,4608]{1,0:T(2,128)(2,1)S(1)}, bf16[256,4608]{1,0:T(8,128)(2,1)S(1)}) custom-call(bf16[2,4608]{1,0:T(2,128)(2,1)} %cur_hbm.1, bf16[16,576]{1,0:T(8,128)(2,1)} %cached_hbm.1, s32[1,16]{1,0:T(1,128)} %bitcast.4, bf16[256,4608]{1,0:T(8,128)(2,1)} %weight_hbm.1), custom_call_target="tpu_custom_call" | custom-call | flops 4000000 | bytes 2000000 | tf_op jit(solution)/shard_map/order/pallas_call | solution.py:85
  6.5 0.2 collective-permute-done
  6.7 0.1 pad_maximum_fusion.4
  6.8 2.9 %collective-permute-start.3 = (bf16[4,5184]{1,0:T(4,128)(2,1)S(1)}, bf16[4,5184]{1,0:T(4,128)(2,1)S(1)}, u32[]{:S(2)}, u32[]{:S(2)}) collective-permute-start(bf16[4,5184]{1,0:T(4,128)(2,1)S(1)} %get-tuple-element.48), channel_id=1, source_target_pairs={{0,6},{2,4},{4,2},{6,0},{8,14},{10,12},{12,10},{14,8},{1,7},{3,5},... | collective-permute-start | bytes 124424 | tf_op jit(solution)/shard_map/ppermute | solution.py:23
  9.7 0.5 %collective-permute-start.2 = (bf16[4,5184]{1,0:T(4,128)(2,1)S(1)}, bf16[4,5184]{1,0:T(4,128)(2,1)S(1)}, u32[]{:S(2)}, u32[]{:S(2)}) collective-permute-start(bf16[4,5184]{1,0:T(4,128)(2,1)S(1)} %get-tuple-element.49), channel_id=1, source_target_pairs={{0,4},{2,6},{4,0},{6,2},{8,12},{10,14},{12,8},{14,10},{1,5},{3,7},... | collective-permute-start | bytes 124424 | tf_op jit(solution)/shard_map/ppermute | solution.py:23
  10.2 0.1 collective-permute-start.1
  10.4 1.7 %collective-permute-done.3.fourth_ref.refs_3_ = bf16[4,5184]{1,0:T(4,128)(2,1)S(1)} collective-permute-done((bf16[4,5184]{1,0:T(4,128)(2,1)S(1)}, bf16[4,5184]{1,0:T(4,128)(2,1)S(1)}, u32[]{:S(2)}, u32[]{:S(2)}) %collective-permute-start.3) | collective-permute-done | bytes 41504 | tf_op jit(solution)/shard_map/ppermute | solution.py:23
  12.0 1.7 %collective-permute-done.2.third_ref.refs_2_ = bf16[4,5184]{1,0:T(4,128)(2,1)S(1)} collective-permute-done((bf16[4,5184]{1,0:T(4,128)(2,1)S(1)}, bf16[4,5184]{1,0:T(4,128)(2,1)S(1)}, u32[]{:S(2)}, u32[]{:S(2)}) %collective-permute-start.2) | collective-permute-done | bytes 41504 | tf_op jit(solution)/shard_map/ppermute | solution.py:23
  13.7 0.5 %collective-permute-done.1.second_ref.refs_1_ = bf16[4,5184]{1,0:T(4,128)(2,1)S(1)} collective-permute-done((bf16[4,5184]{1,0:T(4,128)(2,1)S(1)}, bf16[4,5184]{1,0:T(4,128)(2,1)S(1)}, u32[]{:S(2)}, u32[]{:S(2)}) %collective-permute-start.1) | collective-permute-done | bytes 41504 | tf_op jit(solution)/shard_map/ppermute | solution.py:23
  14.2 0.0 copy-done
  14.2 0.0 copy-start.1
  14.2 1.3 %encode.1 = (bf16[16,2304]{1,0:T(8,128)(2,1)S(1)}, bf16[16,4608]{1,0:T(8,128)(2,1)S(1)}, f32[16,256]{1,0:T(8,128)S(1)}, f32[16,256]{1,0:T(8,128)S(1)}, f32[16,1]{1,0:T(8,128)S(1)}) custom-call(bf16[4,4608]{1,0:T(4,128)(2,1)S(1)} %pad_maximum_fusion.5.first_ref, bf16[4,5184]{1,0:T(4,128)(2,1)S(1)} %collective-permute-done.1.second_ref.refs_1_, ...), custom_call_target="tpu_custom_call" | custom-call | tf_op jit(solution)/shard_map/encode/pallas_call | solution.py:157
  15.5 0.0 collective-permute-start.4
  15.5 0.7 %keep.1 = (f32[16,2304]{1,0:T(8,128)S(1)}, f32[16,256]{1,0:T(8,128)S(1)}, f32[1,256]{1,0:T(1,128)S(1)}, f32[256,1]{1,0:T(8,128)S(1)}, bf16[16,288]{1,0:T(8,128)(2,1)S(1)}, /*index=5*/f32[4,2,576]{2,1,0:T(2,128)S(1)}) custom-call(f32[16,256]{1,0:T(8,128)S(1)} %get-tuple-element.27.latents_ref, f32[16,256]{1,0:T(8,128)S(1)} %get-tuple-element.28.sharp_ref, ...), custom_call_target="tpu_custom_call" | custom-call | flops 18874368 | bytes 1179648 | tf_op jit(solution)/shard_map/keep/pallas_call | solution.py:225
  16.2 0.6 %collective-permute-done.4 = bf16[16,2304]{1,0:T(8,128)(2,1)S(1)} collective-permute-done((bf16[16,2304]{1,0:T(8,128)(2,1)S(1)}, bf16[16,2304]{1,0:T(8,128)(2,1)S(1)}, u32[]{:S(2)}, u32[]{:S(2)}) %collective-permute-start.4) | collective-permute-done | bytes 73760 | tf_op jit(solution)/shard_map/ppermute | solution.py:23
  16.8 1.5 %collective-permute-start.7 = (bf16[16,2304]{1,0:T(8,128)(2,1)S(1)}, bf16[16,2304]{1,0:T(8,128)(2,1)S(1)}, u32[]{:S(2)}, u32[]{:S(2)}) collective-permute-start(bf16[16,2304]{1,0:T(8,128)(2,1)S(1)} %get-tuple-element.44), channel_id=1, source_target_pairs={{0,6},{2,4},{4,2},{6,0},{8,14},{10,12},{12,10},{14,8},{1,7},{3,5},... | collective-permute-start | bytes 221192 | tf_op jit(solution)/shard_map/ppermute | solution.py:23
  18.3 0.1 collective-permute-start.6
  18.4 1.9 %collective-permute-start.5 = (bf16[16,2304]{1,0:T(8,128)(2,1)S(1)}, bf16[16,2304]{1,0:T(8,128)(2,1)S(1)}, u32[]{:S(2)}, u32[]{:S(2)}) collective-permute-start(bf16[16,2304]{1,0:T(8,128)(2,1)S(1)} %get-tuple-element.44), channel_id=1, source_target_pairs={{0,2},{2,0},{4,6},{6,4},{8,10},{10,8},{12,14},{14,12},{1,3},{3,1},... | collective-permute-start | bytes 221192 | tf_op jit(solution)/shard_map/ppermute | solution.py:23
  20.3 2.2 %collective-permute-done.7.refs_2_ = bf16[16,2304]{1,0:T(8,128)(2,1)S(1)} collective-permute-done((bf16[16,2304]{1,0:T(8,128)(2,1)S(1)}, bf16[16,2304]{1,0:T(8,128)(2,1)S(1)}, u32[]{:S(2)}, u32[]{:S(2)}) %collective-permute-start.7) | collective-permute-done | bytes 73760 | tf_op jit(solution)/shard_map/ppermute | solution.py:23
  22.6 0.1 collective-permute-done.6.refs_1_
  22.7 1.0 %collective-permute-done.5.refs_0_ = bf16[16,2304]{1,0:T(8,128)(2,1)S(1)} collective-permute-done((bf16[16,2304]{1,0:T(8,128)(2,1)S(1)}, bf16[16,2304]{1,0:T(8,128)(2,1)S(1)}, u32[]{:S(2)}, u32[]{:S(2)}) %collective-permute-start.5) | collective-permute-done | bytes 73760 | tf_op jit(solution)/shard_map/ppermute | solution.py:23
  23.6 0.1 merge.1
  23.7 2.6 %collective-permute-start.8 = (bf16[16,2592]{1,0:T(8,128)(2,1)S(1)}, bf16[16,2592]{1,0:T(8,128)(2,1)S(1)}, u32[]{:S(2)}, u32[]{:S(2)}) collective-permute-start(bf16[16,2592]{1,0:T(8,128)(2,1)S(1)} %get-tuple-element.33), channel_id=1, source_target_pairs={{0,8},{2,10},{4,12},{6,14},{8,0},{10,2},{12,4},{14,6},{1,9},{3,11}... | collective-permute-start | bytes 248840 | tf_op jit(solution)/shard_map/ppermute | solution.py:23
  26.3 0.0 copy-done.1
  26.3 4.5 %collective-permute-done.8.arrived_ref.refs_0_ = bf16[16,2592]{1,0:T(8,128)(2,1)S(1)} collective-permute-done((bf16[16,2592]{1,0:T(8,128)(2,1)S(1)}, bf16[16,2592]{1,0:T(8,128)(2,1)S(1)}, u32[]{:S(2)}, u32[]{:S(2)}) %collective-permute-start.8) | collective-permute-done | bytes 82976 | tf_op jit(solution)/shard_map/ppermute | solution.py:23
  30.9 0.1 settle.1.grad_ref
  31.0 0.1 collective-permute-start.9
  31.0 0.4 %early.1.early_ref = f32[16,256]{1,0:T(8,128)S(1)} custom-call(bf16[16,2304]{1,0:T(8,128)(2,1)S(1)} %settle.1.grad_ref, bf16[256,4608]{1,0:T(8,128)(2,1)S(1)} %get-tuple-element.26.weight_ref, f32[1,256]{1,0:T(1,128)S(1)} %get-tuple-element.36.norms_ref), custom_call_target="tpu_custom_call" | custom-call | flops 18874368 | bytes 589824 | tf_op jit(solution)/shard_map/early/pallas_call | solution.py:302
  31.5 0.8 %collective-permute-done.9 = bf16[16,2304]{1,0:T(8,128)(2,1)S(1)} collective-permute-done((bf16[16,2304]{1,0:T(8,128)(2,1)S(1)}, bf16[16,2304]{1,0:T(8,128)(2,1)S(1)}, u32[]{:S(2)}, u32[]{:S(2)}) %collective-permute-start.9) | collective-permute-done | bytes 73760 | tf_op jit(solution)/shard_map/ppermute | solution.py:23
  32.3 2.3 %finish.1 = (bf16[256,4608]{1,0:T(8,128)(2,1)}, f32[1,256]{1,0:T(1,128)}, f32[288]{0:T(512)}, bf16[2,4608]{1,0:T(2,128)(2,1)}) custom-call(bf16[16,4608]{1,0:T(8,128)(2,1)S(1)} %pad_maximum_fusion.grad_ref, f32[16,256]{1,0:T(8,128)S(1)} %early.1.early_ref, bf16[16,4608]{1,0:T(8,128)(2,1)S(1)} %get-tuple-element.34.rows_ref, ...), custom_call_target="tpu_custom_call" | custom-call | tf_op jit(solution)/shard_map/finish/pallas_call | solution.py:434
  (6 shorter events, 0.1 us)
Async XLA Ops:
  0.6 13.6 %copy-start = (f32[256]{0:T(256)S(1)}, f32[256]{0:T(256)}, u32[]{:S(2)}) copy-start(f32[256]{0:T(256)} %param.10) | copy-start | bytes 3076
  0.6 6.1 %collective-permute-start = (bf16[2,4608]{1,0:T(2,128)(2,1)}, bf16[2,4608]{1,0:T(2,128)(2,1)S(1)}, u32[]{:S(2)}, u32[]{:S(2)}) collective-permute-start(bf16[2,4608]{1,0:T(2,128)(2,1)} %cur_hbm.1), channel_id=1, source_target_pairs={{0,8},{2,10},{4,12},{6,14},{8,0},{10,2},{12,4},{14,6},{1,9},{3,11}... | collective-permute-start | bytes 55304 | tf_op jit(solution)/shard_map/ppermute | solution.py:23
  6.8 5.3 %collective-permute-start.3 = (bf16[4,5184]{1,0:T(4,128)(2,1)S(1)}, bf16[4,5184]{1,0:T(4,128)(2,1)S(1)}, u32[]{:S(2)}, u32[]{:S(2)}) collective-permute-start(bf16[4,5184]{1,0:T(4,128)(2,1)S(1)} %get-tuple-element.48), channel_id=1, source_target_pairs={{0,6},{2,4},{4,2},{6,0},{8,14},{10,12},{12,10},{14,8},{1,7},{3,5},... | collective-permute-start | bytes 124424 | tf_op jit(solution)/shard_map/ppermute | solution.py:23
  9.7 4.0 %collective-permute-start.2 = (bf16[4,5184]{1,0:T(4,128)(2,1)S(1)}, bf16[4,5184]{1,0:T(4,128)(2,1)S(1)}, u32[]{:S(2)}, u32[]{:S(2)}) collective-permute-start(bf16[4,5184]{1,0:T(4,128)(2,1)S(1)} %get-tuple-element.49), channel_id=1, source_target_pairs={{0,4},{2,6},{4,0},{6,2},{8,12},{10,14},{12,8},{14,10},{1,5},{3,7},... | collective-permute-start | bytes 124424 | tf_op jit(solution)/shard_map/ppermute | solution.py:23
  10.2 4.0 %collective-permute-start.1 = (bf16[4,5184]{1,0:T(4,128)(2,1)S(1)}, bf16[4,5184]{1,0:T(4,128)(2,1)S(1)}, u32[]{:S(2)}, u32[]{:S(2)}) collective-permute-start(bf16[4,5184]{1,0:T(4,128)(2,1)S(1)} %get-tuple-element.50), channel_id=1, source_target_pairs={{0,2},{2,0},{4,6},{6,4},{8,10},{10,8},{12,14},{14,12},{1,3},{3,1},... | collective-permute-start | bytes 124424 | tf_op jit(solution)/shard_map/ppermute | solution.py:23
  14.2 12.1 %copy-start.1 = (f32[4608]{0:T(1024)S(1)}, f32[4608]{0:T(1024)}, u32[]{:S(2)}) copy-start(f32[4608]{0:T(1024)} %param.11) | copy-start | bytes 55300
  15.5 1.3 %collective-permute-start.4 = (bf16[16,2304]{1,0:T(8,128)(2,1)S(1)}, bf16[16,2304]{1,0:T(8,128)(2,1)S(1)}, u32[]{:S(2)}, u32[]{:S(2)}) collective-permute-start(bf16[16,2304]{1,0:T(8,128)(2,1)S(1)} %get-tuple-element.30), channel_id=1, source_target_pairs={{0,1},{1,0},{2,3},{3,2},{4,5},{5,4},{6,7},{7,6},{8,9},{9,8},{10,11... | collective-permute-start | bytes 221192 | tf_op jit(solution)/shard_map/ppermute | solution.py:23
  16.8 5.8 %collective-permute-start.7 = (bf16[16,2304]{1,0:T(8,128)(2,1)S(1)}, bf16[16,2304]{1,0:T(8,128)(2,1)S(1)}, u32[]{:S(2)}, u32[]{:S(2)}) collective-permute-start(bf16[16,2304]{1,0:T(8,128)(2,1)S(1)} %get-tuple-element.44), channel_id=1, source_target_pairs={{0,6},{2,4},{4,2},{6,0},{8,14},{10,12},{12,10},{14,8},{1,7},{3,5},... | collective-permute-start | bytes 221192 | tf_op jit(solution)/shard_map/ppermute | solution.py:23
  18.3 4.4 %collective-permute-start.6 = (bf16[16,2304]{1,0:T(8,128)(2,1)S(1)}, bf16[16,2304]{1,0:T(8,128)(2,1)S(1)}, u32[]{:S(2)}, u32[]{:S(2)}) collective-permute-start(bf16[16,2304]{1,0:T(8,128)(2,1)S(1)} %get-tuple-element.44), channel_id=1, source_target_pairs={{0,4},{2,6},{4,0},{6,2},{8,12},{10,14},{12,8},{14,10},{1,5},{3,7},... | collective-permute-start | bytes 221192 | tf_op jit(solution)/shard_map/ppermute | solution.py:23
  18.4 5.2 %collective-permute-start.5 = (bf16[16,2304]{1,0:T(8,128)(2,1)S(1)}, bf16[16,2304]{1,0:T(8,128)(2,1)S(1)}, u32[]{:S(2)}, u32[]{:S(2)}) collective-permute-start(bf16[16,2304]{1,0:T(8,128)(2,1)S(1)} %get-tuple-element.44), channel_id=1, source_target_pairs={{0,2},{2,0},{4,6},{6,4},{8,10},{10,8},{12,14},{14,12},{1,3},{3,1},... | collective-permute-start | bytes 221192 | tf_op jit(solution)/shard_map/ppermute | solution.py:23
  23.7 7.1 %collective-permute-start.8 = (bf16[16,2592]{1,0:T(8,128)(2,1)S(1)}, bf16[16,2592]{1,0:T(8,128)(2,1)S(1)}, u32[]{:S(2)}, u32[]{:S(2)}) collective-permute-start(bf16[16,2592]{1,0:T(8,128)(2,1)S(1)} %get-tuple-element.33), channel_id=1, source_target_pairs={{0,8},{2,10},{4,12},{6,14},{8,0},{10,2},{12,4},{14,6},{1,9},{3,11}... | collective-permute-start | bytes 248840 | tf_op jit(solution)/shard_map/ppermute | solution.py:23
  31.0 1.3 %collective-permute-start.9 = (bf16[16,2304]{1,0:T(8,128)(2,1)S(1)}, bf16[16,2304]{1,0:T(8,128)(2,1)S(1)}, u32[]{:S(2)}, u32[]{:S(2)}) collective-permute-start(bf16[16,2304]{1,0:T(8,128)(2,1)S(1)} %settle.1.grad_ref), channel_id=1, source_target_pairs={{0,1},{1,0},{2,3},{3,2},{4,5},{5,4},{6,7},{7,6},{8,9},{9,8},{10,11... | collective-permute-start | bytes 221192 | tf_op jit(solution)/shard_map/ppermute | solution.py:23

commit v8 on v7

--- a/solution.py
+++ b/solution.py
@@ -44,6 +44,7 @@
 
 
 def order_kernel(
+    turn,
     cur_hbm,
     cached_hbm,
     perm_hbm,
@@ -68,7 +69,8 @@
         fetch.start()
     row = lax.broadcasted_iota(jnp.int32, (row_total, row_total), 0)
     rest = dp // 4
-    distance = row // (rest * own) + 4 * (row // own % rest)
+    low, high = row // (rest * own), row // own % rest
+    distance = (low ^ (turn * high)) + 4 * high
     wanted = (distance ^ lax.axis_index("dp")) * own + row % own
     for fetch in fetches[:2]:
         fetch.wait()
@@ -80,10 +82,10 @@
         fetch.wait()
 
 
-def order(cur_rows, cached_rows, shuffle_perm, weight):
+def order(cur_rows, cached_rows, shuffle_perm, weight, turn):
     row_total, columns = cached_rows.shape
     return pl.pallas_call(
-        order_kernel,
+        functools.partial(order_kernel, turn),
         out_shape=(
             jax.ShapeDtypeStruct((row_total, columns), jnp.bfloat16),
             jax.ShapeDtypeStruct(cur_rows.shape, jnp.bfloat16),
@@ -121,6 +123,7 @@
     sharp_ref,
     scales_ref,
     rows_f_ref,
+    scaled_ref,
 ):
     rows_total, width = rows_f_ref.shape
     batch_rows = rows_total // 2
@@ -140,14 +143,20 @@
     far = jnp.sum(jnp.where(near, 0.0, squares), axis=0, keepdims=True) / batch_rows
     scales = jnp.sqrt(width / jnp.where(near, here, far))
     scales_ref[...] = scales
-    sharp = SHARP * (scales * projected + bias_ref[...])
-    latents = jax.nn.softplus(sharp) / SHARP
-    sharp_ref[...] = sharp
-    latents_ref[...] = latents
-    _, there = core_columns(width // 2)
-    send_ref[...] = jnp.dot(
-        latents.astype(jnp.bfloat16), weight_ref[:, there], preferred_element_type=jnp.float32
-    ).astype(jnp.bfloat16)
+    scaled_ref[...] = scales * projected
+
+    @pl.loop(0, 1 + lax.axis_index("latent") // 2)
+    def _(_):
+        sharp = SHARP * (scaled_ref[...] + bias_ref[...])
+        latents = jax.nn.softplus(sharp) / SHARP
+        sharp_ref[...] = sharp
+        latents_ref[...] = latents
+        _, there = core_columns(width // 2)
+        send_ref[...] = jnp.dot(
+            latents.astype(jnp.bfloat16),
+            weight_ref[:, there],
+            preferred_element_type=jnp.float32,
+        ).astype(jnp.bfloat16)
 
 
 def encode(parts, weight, enc_bias, own):
@@ -165,7 +174,7 @@
         ),
         in_specs=[whole()] * 6,
         out_specs=[whole()] * 5,
-        scratch_shapes=[pltpu.VMEM((rows_total, width), f32)],
+        scratch_shapes=[pltpu.VMEM((rows_total, width), f32), pltpu.VMEM((rows_total, count), f32)],
         compiler_params=pltpu.CompilerParams(vmem_limit_bytes=VMEM_BYTES),
         name="encode",
     )(*parts, weight, enc_bias.reshape(1, count))
@@ -316,7 +325,9 @@
     tile,
     span,
     rides,
-    grad_ref,
+    turn,
+    mine_ref,
+    other_ref,
     early_ref,
     rows_ref,
     weight_ref,
@@ -328,20 +339,20 @@
 ):
     if rides:
         arrived_ref, staying_ref, weight_grad_hbm, bias_grad_hbm, dec_grad_hbm, next_hbm = refs[:6]
-        staged_ref, bias_ref, dec_ref, sums_ref, left_ref, sems, blocks_ref, line_ref, next_ref = (
-            refs[6:]
-        )
+        *refs, blocks_ref, line_ref, next_ref = refs[6:]
     else:
-        weight_grad_hbm, bias_grad_hbm, dec_grad_hbm = refs[:3]
-        staged_ref, bias_ref, dec_ref, sums_ref, left_ref, sems = refs[3:]
+        weight_grad_hbm, bias_grad_hbm, dec_grad_hbm, *refs = refs
+    grad_ref, staged_ref, bias_ref, dec_ref, sums_ref, left_ref, sems = refs
     rows_total, width = rows_ref.shape
     shares = dec_grad_hbm.shape[0]
     count = width // tile
     core = lax.axis_index("latent")
-    _, there = core_columns(width // 2)
+    here, there = core_columns(width // 2)
     grad_latents = early_ref[...] + lax.dot_general(
-        grad_ref[:, there], weight_ref[:, there], NT, preferred_element_type=jnp.float32
-    )
+        other_ref[...], weight_ref[:, there], NT, preferred_element_type=jnp.float32
+    )
+    grad_ref[:, here] = mine_ref[...]
+    grad_ref[:, there] = other_ref[...]
     grad_pre = grad_latents * gate_ref[...]
     bias_ref[...] = jnp.sum(grad_pre, axis=0, keepdims=True)
     bias_copy = pltpu.make_async_copy(bias_ref, bias_grad_hbm, sems.at[count])
@@ -371,7 +382,9 @@
             blocks_ref[near + index, :, shares:] = came[rows]
         place = lax.axis_index("dp")
         for source in range(2 * near):
-            line_ref[:, source * columns : (source + 1) * columns] = blocks_ref[place ^ source]
+            away = place ^ source
+            away = away ^ (turn * (away // near))
+            line_ref[:, source * columns : (source + 1) * columns] = blocks_ref[away]
         next_ref[...] = line_ref[...].astype(jnp.bfloat16)
         next_copy = pltpu.make_async_copy(next_ref, next_hbm, sems.at[count + 2])
         next_copy.start()
@@ -404,7 +417,7 @@
         next_copy.wait()
 
 
-def finish(grad_out, early_sum, rows, weight, latents, gate, scales, pull, shares, riders):
+def finish(mine, other, early_sum, rows, weight, latents, gate, scales, pull, shares, riders, turn):
     rows_total, width = rows.shape
     count = weight.shape[0]
     tile = 768
@@ -416,6 +429,7 @@
         jax.ShapeDtypeStruct((shares,), f32),
     ]
     scratch = [
+        pltpu.VMEM((rows_total, width), jnp.bfloat16),
         pltpu.VMEM((count, width), jnp.bfloat16),
         pltpu.VMEM((1, count), f32),
         pltpu.VMEM((shares,), f32),
@@ -432,14 +446,14 @@
             pltpu.VMEM((own, width), jnp.bfloat16),
         ]
     return pl.pallas_call(
-        functools.partial(finish_kernel, tile, span, bool(riders)),
+        functools.partial(finish_kernel, tile, span, bool(riders), turn),
         out_shape=out_shape,
-        in_specs=[whole()] * (8 + len(riders)),
+        in_specs=[whole()] * (9 + len(riders)),
         out_specs=[whole(pl.ANY)] * len(out_shape),
         scratch_shapes=scratch,
         compiler_params=pltpu.CompilerParams(vmem_limit_bytes=VMEM_BYTES),
         name="finish",
-    )(grad_out, early_sum, rows, weight, latents, gate, scales, pull, *riders)
+    )(mine, other, early_sum, rows, weight, latents, gate, scales, pull, *riders)
 
 
 def shuffle_rest(riders, dp, own, columns):
@@ -466,10 +480,12 @@
     columns = cached_rows.shape[1]
     count = weight.shape[0]
     shares = width // (2 * dp)
-    core = lax.axis_index("latent")
+
+    rides = rest == 2
+    turn = 2 if rides else 0
 
     came = exchange(cur_rows, "dp", 4)
-    ordered, cur_copy, weight = order(cur_rows, cached_rows, shuffle_perm, weight)
+    ordered, cur_copy, weight = order(cur_rows, cached_rows, shuffle_perm, weight, turn)
     near = jnp.concatenate([cur_copy, came], axis=0)
     distance = 8
     while distance < dp:
@@ -482,7 +498,6 @@
 
     send, gathered, latents, sharp, scales = encode(parts, weight, enc_bias, own)
     came = exchange(send, "latent", 1)
-    rides = rest == 2
     sources = [ordered[0]] + parts[1:] if rides else []
     mine, gate, norms, pull, *riders = keep(latents, sharp, weight, sources, own, shares)
 
@@ -497,8 +512,8 @@
     )
     distance = 4
     while distance < dp:
-        arrived = exchange(sent, "dp", distance)
-        row_distance = distance // 4 * own
+        arrived = exchange(sent, "dp", distance + turn)
+        row_distance = distance // 4 * own + turn * rest * own
         if 2 * distance < dp:
             total, sent = merge(total, [arrived], (row_distance,))
         else:
@@ -507,11 +522,9 @@
 
     grad_other = exchange(grad_mine, "latent", 1)
     early_sum = early(grad_mine, weight, norms)
-    low_half = jnp.where(core == 0, grad_mine, grad_other)
-    high_half = jnp.where(core == 0, grad_other, grad_mine)
-    grad_out = jnp.concatenate([low_half, high_half], axis=1)
     weight_grad, enc_bias_grad, dec_bias_grad, *shuffled = finish(
-        grad_out,
+        grad_mine,
+        grad_other,
         early_sum,
         gathered,
         weight,
@@ -521,6 +534,7 @@
         pull,
         shares,
         (arrived, riders[1]) if rides else (),
+        turn,
     )
     if rides:
         next_batch = shuffled[0]

time: 34.8 us -> 33.8 us (0.971)
  waiting for transfers between devices: 13.2 us -> 11.4 us
  starting transfers between devices: 13.9 us -> 15 us
    ppermute x10, waiting for transfers between devices: 13.2 us -> 11.4 us  [exchange(): return lax.ppermute(value, axis, [(k, k ^ distance) for k in range(size)])]
    ppermute x10, starting transfers between devices: 13.9 us -> 15 us  [exchange(): return lax.ppermute(value, axis, [(k, k ^ distance) for k in range(size)])]
  transfers between devices with their start and end apart: 10 -> 10, of which waited for: 10 -> 10; matrix products, arithmetic and copies ran while one was open for 0% -> 0% of each run, Pallas kernels for 8% -> 9%
where the time goes in v8:
time: 33.8 us; the launch traced here: 33.6 us
  starting transfers between devices  15 us (44%)
  waiting for transfers between devices  11.4 us (34%)
  Pallas kernels  6.36 us (19%)
  between operations  0.71 us (2%)
    ppermute x10, starting transfers between devices, exchange(): return lax.ppermute(value, axis, [(k, k ^ distance) for k in range(size)])  15 us
    ppermute x10, waiting for transfers between devices, exchange(): return lax.ppermute(value, axis, [(k, k ^ distance) for k in range(size)])  11.4 us
    pallas_call x1, Pallas kernels, finish(): pl.pallas_call(functools.partial(finish_kernel, tile, span, bool(riders),...  2.31 us
    pallas_call x1, Pallas kernels, order(): pl.pallas_call(functools.partial(order_kernel, turn), out_shape=(jax.Shap...  1.75 us
    pallas_call x1, Pallas kernels, encode(): pl.pallas_call(functools.partial(encode_kernel, own), out_shape=(jax.Shap...  1 us
    pallas_call x1, Pallas kernels, keep(): pl.pallas_call(functools.partial(keep_kernel, bool(sources)), out_shape=o...  0.7 us
  transfers between devices with their start and end apart: 10, of which 10 were waited for; matrix products, arithmetic and copies ran while one was open for 0% of the time, Pallas kernels for 9%

profile of v8, /device:TPU:0, one launch (start us, length us, event | category | flops | bytes accessed | tf_op | source)
XLA Modules:
  0.0 33.6 jit_solution(14563291727676383151)
XLA Ops:
  0.6 0.0 copy-start
  0.6 4.1 %collective-permute-start = (bf16[2,4608]{1,0:T(2,128)(2,1)}, bf16[2,4608]{1,0:T(2,128)(2,1)S(1)}, u32[]{:S(2)}, u32[]{:S(2)}) collective-permute-start(bf16[2,4608]{1,0:T(2,128)(2,1)} %cur_hbm.1), channel_id=1, source_target_pairs={{0,8},{2,10},{4,12},{6,14},{8,0},{10,2},{12,4},{14,6},{1,9},{3,11}... | collective-permute-start | bytes 55304 | tf_op jit(solution)/shard_map/ppermute | solution.py:23
  4.7 1.8 %order.1 = (bf16[16,576]{1,0:T(8,128)(2,1)S(1)}, bf16[2,4608]{1,0:T(2,128)(2,1)S(1)}, bf16[256,4608]{1,0:T(8,128)(2,1)S(1)}) custom-call(bf16[2,4608]{1,0:T(2,128)(2,1)} %cur_hbm.1, bf16[16,576]{1,0:T(8,128)(2,1)} %cached_hbm.1, s32[1,16]{1,0:T(1,128)} %bitcast.4, bf16[256,4608]{1,0:T(8,128)(2,1)} %weight_hbm.1), custom_call_target="tpu_custom_call" | custom-call | flops 4000000 | bytes 2000000 | tf_op jit(solution)/shard_map/order/pallas_call | solution.py:87
  6.5 0.2 collective-permute-done
  6.7 0.1 pad_maximum_fusion.3
  6.8 2.9 %collective-permute-start.3 = (bf16[4,5184]{1,0:T(4,128)(2,1)S(1)}, bf16[4,5184]{1,0:T(4,128)(2,1)S(1)}, u32[]{:S(2)}, u32[]{:S(2)}) collective-permute-start(bf16[4,5184]{1,0:T(4,128)(2,1)S(1)} %get-tuple-element.46), channel_id=1, source_target_pairs={{0,6},{2,4},{4,2},{6,0},{8,14},{10,12},{12,10},{14,8},{1,7},{3,5},... | collective-permute-start | bytes 124424 | tf_op jit(solution)/shard_map/ppermute | solution.py:23
  9.7 0.5 %collective-permute-start.2 = (bf16[4,5184]{1,0:T(4,128)(2,1)S(1)}, bf16[4,5184]{1,0:T(4,128)(2,1)S(1)}, u32[]{:S(2)}, u32[]{:S(2)}) collective-permute-start(bf16[4,5184]{1,0:T(4,128)(2,1)S(1)} %get-tuple-element.47), channel_id=1, source_target_pairs={{0,4},{2,6},{4,0},{6,2},{8,12},{10,14},{12,8},{14,10},{1,5},{3,7},... | collective-permute-start | bytes 124424 | tf_op jit(solution)/shard_map/ppermute | solution.py:23
  10.2 0.1 collective-permute-start.1
  10.4 1.7 %collective-permute-done.3.fourth_ref.refs_3_ = bf16[4,5184]{1,0:T(4,128)(2,1)S(1)} collective-permute-done((bf16[4,5184]{1,0:T(4,128)(2,1)S(1)}, bf16[4,5184]{1,0:T(4,128)(2,1)S(1)}, u32[]{:S(2)}, u32[]{:S(2)}) %collective-permute-start.3) | collective-permute-done | bytes 41504 | tf_op jit(solution)/shard_map/ppermute | solution.py:23
  12.0 1.7 %collective-permute-done.2.third_ref.refs_2_ = bf16[4,5184]{1,0:T(4,128)(2,1)S(1)} collective-permute-done((bf16[4,5184]{1,0:T(4,128)(2,1)S(1)}, bf16[4,5184]{1,0:T(4,128)(2,1)S(1)}, u32[]{:S(2)}, u32[]{:S(2)}) %collective-permute-start.2) | collective-permute-done | bytes 41504 | tf_op jit(solution)/shard_map/ppermute | solution.py:23
  13.7 0.5 %collective-permute-done.1.second_ref.refs_1_ = bf16[4,5184]{1,0:T(4,128)(2,1)S(1)} collective-permute-done((bf16[4,5184]{1,0:T(4,128)(2,1)S(1)}, bf16[4,5184]{1,0:T(4,128)(2,1)S(1)}, u32[]{:S(2)}, u32[]{:S(2)}) %collective-permute-start.1) | collective-permute-done | bytes 41504 | tf_op jit(solution)/shard_map/ppermute | solution.py:23
  14.2 0.0 copy-done
  14.2 0.0 copy-start.1
  14.2 1.0 %encode.1 = (bf16[16,2304]{1,0:T(8,128)(2,1)S(1)}, bf16[16,4608]{1,0:T(8,128)(2,1)S(1)}, f32[16,256]{1,0:T(8,128)S(1)}, f32[16,256]{1,0:T(8,128)S(1)}, f32[16,1]{1,0:T(8,128)S(1)}) custom-call(bf16[4,4608]{1,0:T(4,128)(2,1)S(1)} %pad_maximum_fusion.4.first_ref, bf16[4,5184]{1,0:T(4,128)(2,1)S(1)} %collective-permute-done.1.second_ref.refs_1_, ...), custom_call_target="tpu_custom_call" | custom-call | tf_op jit(solution)/shard_map/encode/pallas_call | solution.py:166
  15.2 0.1 collective-permute-start.4
  15.3 0.7 %keep.1 = (f32[16,2304]{1,0:T(8,128)S(1)}, f32[16,256]{1,0:T(8,128)S(1)}, f32[1,256]{1,0:T(1,128)S(1)}, f32[256,1]{1,0:T(8,128)S(1)}, bf16[16,288]{1,0:T(8,128)(2,1)S(1)}, /*index=5*/f32[4,2,576]{2,1,0:T(2,128)S(1)}) custom-call(f32[16,256]{1,0:T(8,128)S(1)} %get-tuple-element.27.latents_ref, f32[16,256]{1,0:T(8,128)S(1)} %get-tuple-element.28.sharp_ref, ...), custom_call_target="tpu_custom_call" | custom-call | flops 18874368 | bytes 1179648 | tf_op jit(solution)/shard_map/keep/pallas_call | solution.py:234
  16.0 0.5 %collective-permute-done.4 = bf16[16,2304]{1,0:T(8,128)(2,1)S(1)} collective-permute-done((bf16[16,2304]{1,0:T(8,128)(2,1)S(1)}, bf16[16,2304]{1,0:T(8,128)(2,1)S(1)}, u32[]{:S(2)}, u32[]{:S(2)}) %collective-permute-start.4) | collective-permute-done | bytes 73760 | tf_op jit(solution)/shard_map/ppermute | solution.py:23
  16.5 1.5 %collective-permute-start.7 = (bf16[16,2304]{1,0:T(8,128)(2,1)S(1)}, bf16[16,2304]{1,0:T(8,128)(2,1)S(1)}, u32[]{:S(2)}, u32[]{:S(2)}) collective-permute-start(bf16[16,2304]{1,0:T(8,128)(2,1)S(1)} %get-tuple-element.44), channel_id=1, source_target_pairs={{0,6},{2,4},{4,2},{6,0},{8,14},{10,12},{12,10},{14,8},{1,7},{3,5},... | collective-permute-start | bytes 221192 | tf_op jit(solution)/shard_map/ppermute | solution.py:23
  18.1 0.1 collective-permute-start.6
  18.2 1.9 %collective-permute-start.5 = (bf16[16,2304]{1,0:T(8,128)(2,1)S(1)}, bf16[16,2304]{1,0:T(8,128)(2,1)S(1)}, u32[]{:S(2)}, u32[]{:S(2)}) collective-permute-start(bf16[16,2304]{1,0:T(8,128)(2,1)S(1)} %get-tuple-element.44), channel_id=1, source_target_pairs={{0,2},{2,0},{4,6},{6,4},{8,10},{10,8},{12,14},{14,12},{1,3},{3,1},... | collective-permute-start | bytes 221192 | tf_op jit(solution)/shard_map/ppermute | solution.py:23
  20.1 2.2 %collective-permute-done.7.refs_2_ = bf16[16,2304]{1,0:T(8,128)(2,1)S(1)} collective-permute-done((bf16[16,2304]{1,0:T(8,128)(2,1)S(1)}, bf16[16,2304]{1,0:T(8,128)(2,1)S(1)}, u32[]{:S(2)}, u32[]{:S(2)}) %collective-permute-start.7) | collective-permute-done | bytes 73760 | tf_op jit(solution)/shard_map/ppermute | solution.py:23
  22.3 0.1 collective-permute-done.6.refs_1_
  22.4 1.0 %collective-permute-done.5.refs_0_ = bf16[16,2304]{1,0:T(8,128)(2,1)S(1)} collective-permute-done((bf16[16,2304]{1,0:T(8,128)(2,1)S(1)}, bf16[16,2304]{1,0:T(8,128)(2,1)S(1)}, u32[]{:S(2)}, u32[]{:S(2)}) %collective-permute-start.5) | collective-permute-done | bytes 73760 | tf_op jit(solution)/shard_map/ppermute | solution.py:23
  23.4 0.1 merge.1
  23.5 3.7 %collective-permute-start.8 = (bf16[16,2592]{1,0:T(8,128)(2,1)S(1)}, bf16[16,2592]{1,0:T(8,128)(2,1)S(1)}, u32[]{:S(2)}, u32[]{:S(2)}) collective-permute-start(bf16[16,2592]{1,0:T(8,128)(2,1)S(1)} %get-tuple-element.33), channel_id=1, source_target_pairs={{0,12},{2,14},{4,8},{6,10},{8,4},{10,6},{12,0},{14,2},{1,13},{3,15... | collective-permute-start | bytes 248840 | tf_op jit(solution)/shard_map/ppermute | solution.py:23
  27.2 0.0 copy-done.1
  27.2 2.7 %collective-permute-done.8.arrived_ref.refs_0_ = bf16[16,2592]{1,0:T(8,128)(2,1)S(1)} collective-permute-done((bf16[16,2592]{1,0:T(8,128)(2,1)S(1)}, bf16[16,2592]{1,0:T(8,128)(2,1)S(1)}, u32[]{:S(2)}, u32[]{:S(2)}) %collective-permute-start.8) | collective-permute-done | bytes 82976 | tf_op jit(solution)/shard_map/ppermute | solution.py:23
  29.9 0.1 settle.1.grad_ref.mine_ref
  30.0 0.1 collective-permute-start.9
  30.1 0.4 %early.1.early_ref = f32[16,256]{1,0:T(8,128)S(1)} custom-call(bf16[16,2304]{1,0:T(8,128)(2,1)S(1)} %settle.1.grad_ref.mine_ref, bf16[256,4608]{1,0:T(8,128)(2,1)S(1)} %get-tuple-element.26.weight_ref, f32[1,256]{1,0:T(1,128)S(1)} %get-tuple-element.36.norms_ref), custom_call_target="tpu_custom_call" | custom-call | flops 18874368 | bytes 589824 | tf_op jit(solution)/shard_map/early/pallas_call | solution.py:311
  30.5 0.8 %collective-permute-done.9.other_ref = bf16[16,2304]{1,0:T(8,128)(2,1)S(1)} collective-permute-done((bf16[16,2304]{1,0:T(8,128)(2,1)S(1)}, bf16[16,2304]{1,0:T(8,128)(2,1)S(1)}, u32[]{:S(2)}, u32[]{:S(2)}) %collective-permute-start.9) | collective-permute-done | bytes 73760 | tf_op jit(solution)/shard_map/ppermute | solution.py:23
  31.3 2.3 %finish.1 = (bf16[256,4608]{1,0:T(8,128)(2,1)}, f32[1,256]{1,0:T(1,128)}, f32[288]{0:T(512)}, bf16[2,4608]{1,0:T(2,128)(2,1)}) custom-call(bf16[16,2304]{1,0:T(8,128)(2,1)S(1)} %settle.1.grad_ref.mine_ref, bf16[16,2304]{1,0:T(8,128)(2,1)S(1)} %collective-permute-done.9.other_ref, f32[16,256]{1,0:T(8,128)S(1)} %early.1.early_ref, ...), custom_call_target="tpu_custom_call" | custom-call | tf_op jit(solution)/shard_map/finish/pallas_call | solution.py:448
  (4 shorter events, 0.1 us)
Async XLA Ops:
  0.6 13.6 %copy-start = (f32[256]{0:T(256)S(1)}, f32[256]{0:T(256)}, u32[]{:S(2)}) copy-start(f32[256]{0:T(256)} %param.10) | copy-start | bytes 3076
  0.6 6.1 %collective-permute-start = (bf16[2,4608]{1,0:T(2,128)(2,1)}, bf16[2,4608]{1,0:T(2,128)(2,1)S(1)}, u32[]{:S(2)}, u32[]{:S(2)}) collective-permute-start(bf16[2,4608]{1,0:T(2,128)(2,1)} %cur_hbm.1), channel_id=1, source_target_pairs={{0,8},{2,10},{4,12},{6,14},{8,0},{10,2},{12,4},{14,6},{1,9},{3,11}... | collective-permute-start | bytes 55304 | tf_op jit(solution)/shard_map/ppermute | solution.py:23
  6.8 5.3 %collective-permute-start.3 = (bf16[4,5184]{1,0:T(4,128)(2,1)S(1)}, bf16[4,5184]{1,0:T(4,128)(2,1)S(1)}, u32[]{:S(2)}, u32[]{:S(2)}) collective-permute-start(bf16[4,5184]{1,0:T(4,128)(2,1)S(1)} %get-tuple-element.46), channel_id=1, source_target_pairs={{0,6},{2,4},{4,2},{6,0},{8,14},{10,12},{12,10},{14,8},{1,7},{3,5},... | collective-permute-start | bytes 124424 | tf_op jit(solution)/shard_map/ppermute | solution.py:23
  9.7 4.0 %collective-permute-start.2 = (bf16[4,5184]{1,0:T(4,128)(2,1)S(1)}, bf16[4,5184]{1,0:T(4,128)(2,1)S(1)}, u32[]{:S(2)}, u32[]{:S(2)}) collective-permute-start(bf16[4,5184]{1,0:T(4,128)(2,1)S(1)} %get-tuple-element.47), channel_id=1, source_target_pairs={{0,4},{2,6},{4,0},{6,2},{8,12},{10,14},{12,8},{14,10},{1,5},{3,7},... | collective-permute-start | bytes 124424 | tf_op jit(solution)/shard_map/ppermute | solution.py:23
  10.2 4.0 %collective-permute-start.1 = (bf16[4,5184]{1,0:T(4,128)(2,1)S(1)}, bf16[4,5184]{1,0:T(4,128)(2,1)S(1)}, u32[]{:S(2)}, u32[]{:S(2)}) collective-permute-start(bf16[4,5184]{1,0:T(4,128)(2,1)S(1)} %get-tuple-element.48), channel_id=1, source_target_pairs={{0,2},{2,0},{4,6},{6,4},{8,10},{10,8},{12,14},{14,12},{1,3},{3,1},... | collective-permute-start | bytes 124424 | tf_op jit(solution)/shard_map/ppermute | solution.py:23
  14.2 13.0 %copy-start.1 = (f32[4608]{0:T(1024)S(1)}, f32[4608]{0:T(1024)}, u32[]{:S(2)}) copy-start(f32[4608]{0:T(1024)} %param.11) | copy-start | bytes 55300
  15.2 1.3 %collective-permute-start.4 = (bf16[16,2304]{1,0:T(8,128)(2,1)S(1)}, bf16[16,2304]{1,0:T(8,128)(2,1)S(1)}, u32[]{:S(2)}, u32[]{:S(2)}) collective-permute-start(bf16[16,2304]{1,0:T(8,128)(2,1)S(1)} %get-tuple-element.30), channel_id=1, source_target_pairs={{0,1},{1,0},{2,3},{3,2},{4,5},{5,4},{6,7},{7,6},{8,9},{9,8},{10,11... | collective-permute-start | bytes 221192 | tf_op jit(solution)/shard_map/ppermute | solution.py:23
  16.5 5.8 %collective-permute-start.7 = (bf16[16,2304]{1,0:T(8,128)(2,1)S(1)}, bf16[16,2304]{1,0:T(8,128)(2,1)S(1)}, u32[]{:S(2)}, u32[]{:S(2)}) collective-permute-start(bf16[16,2304]{1,0:T(8,128)(2,1)S(1)} %get-tuple-element.44), channel_id=1, source_target_pairs={{0,6},{2,4},{4,2},{6,0},{8,14},{10,12},{12,10},{14,8},{1,7},{3,5},... | collective-permute-start | bytes 221192 | tf_op jit(solution)/shard_map/ppermute | solution.py:23
  18.1 4.4 %collective-permute-start.6 = (bf16[16,2304]{1,0:T(8,128)(2,1)S(1)}, bf16[16,2304]{1,0:T(8,128)(2,1)S(1)}, u32[]{:S(2)}, u32[]{:S(2)}) collective-permute-start(bf16[16,2304]{1,0:T(8,128)(2,1)S(1)} %get-tuple-element.44), channel_id=1, source_target_pairs={{0,4},{2,6},{4,0},{6,2},{8,12},{10,14},{12,8},{14,10},{1,5},{3,7},... | collective-permute-start | bytes 221192 | tf_op jit(solution)/shard_map/ppermute | solution.py:23
  18.2 5.2 %collective-permute-start.5 = (bf16[16,2304]{1,0:T(8,128)(2,1)S(1)}, bf16[16,2304]{1,0:T(8,128)(2,1)S(1)}, u32[]{:S(2)}, u32[]{:S(2)}) collective-permute-start(bf16[16,2304]{1,0:T(8,128)(2,1)S(1)} %get-tuple-element.44), channel_id=1, source_target_pairs={{0,2},{2,0},{4,6},{6,4},{8,10},{10,8},{12,14},{14,12},{1,3},{3,1},... | collective-permute-start | bytes 221192 | tf_op jit(solution)/shard_map/ppermute | solution.py:23
  23.5 6.4 %collective-permute-start.8 = (bf16[16,2592]{1,0:T(8,128)(2,1)S(1)}, bf16[16,2592]{1,0:T(8,128)(2,1)S(1)}, u32[]{:S(2)}, u32[]{:S(2)}) collective-permute-start(bf16[16,2592]{1,0:T(8,128)(2,1)S(1)} %get-tuple-element.33), channel_id=1, source_target_pairs={{0,12},{2,14},{4,8},{6,10},{8,4},{10,6},{12,0},{14,2},{1,13},{3,15... | collective-permute-start | bytes 248840 | tf_op jit(solution)/shard_map/ppermute | solution.py:23
  30.0 1.3 %collective-permute-start.9 = (bf16[16,2304]{1,0:T(8,128)(2,1)S(1)}, bf16[16,2304]{1,0:T(8,128)(2,1)S(1)}, u32[]{:S(2)}, u32[]{:S(2)}) collective-permute-start(bf16[16,2304]{1,0:T(8,128)(2,1)S(1)} %settle.1.grad_ref.mine_ref), channel_id=1, source_target_pairs={{0,1},{1,0},{2,3},{3,2},{4,5},{5,4},{6,7},{7,6},{8,9},{9,8},{10,11... | collective-permute-start | bytes 221192 | tf_op jit(solution)/shard_map/ppermute | solution.py:23

commit v9 on v8

--- a/solution.py
+++ b/solution.py
@@ -492,9 +492,20 @@
         near = jnp.concatenate([near, exchange(near, "dp", distance)], axis=0)
         distance *= 2
     ordered = ordered.reshape(4, rest * own, columns)
-    parts = [near] + [
-        exchange(jnp.concatenate([near, ordered[low]], axis=1), "dp", low) for low in range(1, 4)
+    messages = [None] + [
+        jnp.concatenate([near, ordered[low]], axis=1) for low in range(1, 4)
     ]
+    roles = (1, 3)
+    core = lax.axis_index("latent")
+    pairs = [(2 * k + c, 2 * (k ^ roles[c]) + c) for k in range(dp) for c in range(2)]
+    parts = [near, None, None, None]
+    parts[2] = exchange(messages[2], "dp", 2)
+    fetched = lax.ppermute(
+        jnp.where(core == 0, messages[roles[0]], messages[roles[1]]), ("dp", "latent"), pairs
+    )
+    handed = exchange(fetched, "latent", 1)
+    parts[roles[0]] = jnp.where(core == 0, fetched, handed)
+    parts[roles[1]] = jnp.where(core == 0, handed, fetched)
 
     send, gathered, latents, sharp, scales = encode(parts, weight, enc_bias, own)
     came = exchange(send, "latent", 1)

time: 33.8 us -> 32.7 us (0.967)
  waiting for transfers between devices: 11.4 us -> 10.3 us
    ppermute x10 -> x9, starting transfers between devices: 15 us -> 13 us  [exchange(): return lax.ppermute(value, axis, [(k, k ^ distance) for k in range(size)])]
    ppermute x0 -> x1, starting transfers between devices: none -> 1.96 us  [per_device(): lax.ppermute(jnp.where(core == 0, messages[roles[0]], messages[roles[1]])...]
    ppermute x10 -> x9, waiting for transfers between devices: 11.4 us -> 9.72 us  [exchange(): return lax.ppermute(value, axis, [(k, k ^ distance) for k in range(size)])]
    ppermute x0 -> x1, waiting for transfers between devices: none -> 0.61 us  [per_device(): lax.ppermute(jnp.where(core == 0, messages[roles[0]], messages[roles[1]])...]
where the time goes in v9:
time: 32.7 us; the launch traced here: 32.5 us
  starting transfers between devices  14.9 us (46%)
  waiting for transfers between devices  10.3 us (31%)
  Pallas kernels  6.36 us (19%)
  between operations  0.72 us (2%)
    ppermute x9, starting transfers between devices, exchange(): return lax.ppermute(value, axis, [(k, k ^ distance) for k in range(size)])  13 us
    ppermute x9, waiting for transfers between devices, exchange(): return lax.ppermute(value, axis, [(k, k ^ distance) for k in range(size)])  9.72 us
    pallas_call x1, Pallas kernels, finish(): pl.pallas_call(functools.partial(finish_kernel, tile, span, bool(riders),...  2.3 us
    ppermute x1, starting transfers between devices, per_device(): lax.ppermute(jnp.where(core == 0, messages[roles[0]], messages[roles[1]])...  1.96 us
    pallas_call x1, Pallas kernels, order(): pl.pallas_call(functools.partial(order_kernel, turn), out_shape=(jax.Shap...  1.75 us
    pallas_call x1, Pallas kernels, encode(): pl.pallas_call(functools.partial(encode_kernel, own), out_shape=(jax.Shap...  1 us
    pallas_call x1, Pallas kernels, keep(): pl.pallas_call(functools.partial(keep_kernel, bool(sources)), out_shape=o...  0.7 us
  transfers between devices with their start and end apart: 10, of which 10 were waited for; matrix products, arithmetic and copies ran while one was open for 0% of the time, Pallas kernels for 9%

profile of v9, /device:TPU:0, one launch (start us, length us, event | category | flops | bytes accessed | tf_op | source)
XLA Modules:
  0.0 32.5 jit_solution(9549320605654980964)
XLA Ops:
  0.6 0.0 copy-start
  0.6 4.1 %collective-permute-start = (bf16[2,4608]{1,0:T(2,128)(2,1)}, bf16[2,4608]{1,0:T(2,128)(2,1)S(1)}, u32[]{:S(2)}, u32[]{:S(2)}) collective-permute-start(bf16[2,4608]{1,0:T(2,128)(2,1)} %cur_hbm.1), channel_id=1, source_target_pairs={{0,8},{2,10},{4,12},{6,14},{8,0},{10,2},{12,4},{14,6},{1,9},{3,11}... | collective-permute-start | bytes 55304 | tf_op jit(solution)/shard_map/ppermute | solution.py:23
  4.7 1.8 %order.1 = (bf16[16,576]{1,0:T(8,128)(2,1)S(1)}, bf16[2,4608]{1,0:T(2,128)(2,1)S(1)}, bf16[256,4608]{1,0:T(8,128)(2,1)S(1)}) custom-call(bf16[2,4608]{1,0:T(2,128)(2,1)} %cur_hbm.1, bf16[16,576]{1,0:T(8,128)(2,1)} %cached_hbm.1, s32[1,16]{1,0:T(1,128)} %bitcast.4, bf16[256,4608]{1,0:T(8,128)(2,1)} %weight_hbm.1), custom_call_target="tpu_custom_call" | custom-call | flops 4000000 | bytes 2000000 | tf_op jit(solution)/shard_map/order/pallas_call | solution.py:87
  6.5 0.2 collective-permute-done
  6.7 0.1 pad_maximum_fusion.1
  6.8 2.0 %collective-permute-start.1 = (bf16[4,5184]{1,0:T(4,128)(2,1)S(1)}, bf16[4,5184]{1,0:T(4,128)(2,1)S(1)}, u32[]{:S(2)}, u32[]{:S(2)}) collective-permute-start(bf16[4,5184]{1,0:T(4,128)(2,1)S(1)} %get-tuple-element.49), channel_id=1, source_target_pairs={{0,2},{1,7},{2,0},{3,5},{4,6},{5,3},{6,4},{7,1},{8,10},{9,15},{10,... | collective-permute-start | bytes 124424 | tf_op jit(solution)/shard_map/ppermute | solution.py:503
  8.7 1.5 %collective-permute-start.3 = (bf16[4,5184]{1,0:T(4,128)(2,1)S(1)}, bf16[4,5184]{1,0:T(4,128)(2,1)S(1)}, u32[]{:S(2)}, u32[]{:S(2)}) collective-permute-start(bf16[4,5184]{1,0:T(4,128)(2,1)S(1)} %get-tuple-element.48), channel_id=1, source_target_pairs={{0,4},{2,6},{4,0},{6,2},{8,12},{10,14},{12,8},{14,10},{1,5},{3,7},... | collective-permute-start | bytes 124424 | tf_op jit(solution)/shard_map/ppermute | solution.py:23
  10.2 0.6 %collective-permute-done.1 = bf16[4,5184]{1,0:T(4,128)(2,1)S(1)} collective-permute-done((bf16[4,5184]{1,0:T(4,128)(2,1)S(1)}, bf16[4,5184]{1,0:T(4,128)(2,1)S(1)}, u32[]{:S(2)}, u32[]{:S(2)}) %collective-permute-start.1) | collective-permute-done | bytes 41504 | tf_op jit(solution)/shard_map/ppermute | solution.py:503
  10.8 0.0 collective-permute-start.2
  10.9 1.2 %collective-permute-done.2 = bf16[4,5184]{1,0:T(4,128)(2,1)S(1)} collective-permute-done((bf16[4,5184]{1,0:T(4,128)(2,1)S(1)}, bf16[4,5184]{1,0:T(4,128)(2,1)S(1)}, u32[]{:S(2)}, u32[]{:S(2)}) %collective-permute-start.2) | collective-permute-done | bytes 41504 | tf_op jit(solution)/shard_map/ppermute | solution.py:23
  12.1 0.6 %collective-permute-done.3.third_ref.refs_2_ = bf16[4,5184]{1,0:T(4,128)(2,1)S(1)} collective-permute-done((bf16[4,5184]{1,0:T(4,128)(2,1)S(1)}, bf16[4,5184]{1,0:T(4,128)(2,1)S(1)}, u32[]{:S(2)}, u32[]{:S(2)}) %collective-permute-start.3) | collective-permute-done | bytes 41504 | tf_op jit(solution)/shard_map/ppermute | solution.py:23
  12.7 0.0 copy-done
  12.7 0.0 copy-start.1
  12.7 1.0 %encode.1 = (bf16[16,2304]{1,0:T(8,128)(2,1)S(1)}, bf16[16,4608]{1,0:T(8,128)(2,1)S(1)}, f32[16,256]{1,0:T(8,128)S(1)}, f32[16,256]{1,0:T(8,128)S(1)}, f32[16,1]{1,0:T(8,128)S(1)}) custom-call(bf16[4,4608]{1,0:T(4,128)(2,1)S(1)} %pad_maximum_fusion.2.first_ref, bf16[4,5184]{1,0:T(4,128)(2,1)S(1)} %get-tuple-element.47.second_ref.refs_1_, ...), custom_call_target="tpu_custom_call" | custom-call | tf_op jit(solution)/shard_map/encode/pallas_call | solution.py:166
  13.7 0.1 collective-permute-start.4
  13.8 0.7 %keep.1 = (f32[16,2304]{1,0:T(8,128)S(1)}, f32[16,256]{1,0:T(8,128)S(1)}, f32[1,256]{1,0:T(1,128)S(1)}, f32[256,1]{1,0:T(8,128)S(1)}, bf16[16,288]{1,0:T(8,128)(2,1)S(1)}, /*index=5*/f32[4,2,576]{2,1,0:T(2,128)S(1)}) custom-call(f32[16,256]{1,0:T(8,128)S(1)} %get-tuple-element.27.latents_ref, f32[16,256]{1,0:T(8,128)S(1)} %get-tuple-element.28.sharp_ref, ...), custom_call_target="tpu_custom_call" | custom-call | flops 18874368 | bytes 1179648 | tf_op jit(solution)/shard_map/keep/pallas_call | solution.py:234
  14.5 0.5 %collective-permute-done.4 = bf16[16,2304]{1,0:T(8,128)(2,1)S(1)} collective-permute-done((bf16[16,2304]{1,0:T(8,128)(2,1)S(1)}, bf16[16,2304]{1,0:T(8,128)(2,1)S(1)}, u32[]{:S(2)}, u32[]{:S(2)}) %collective-permute-start.4) | collective-permute-done | bytes 73760 | tf_op jit(solution)/shard_map/ppermute | solution.py:23
  15.1 2.3 %collective-permute-start.7 = (bf16[16,2304]{1,0:T(8,128)(2,1)S(1)}, bf16[16,2304]{1,0:T(8,128)(2,1)S(1)}, u32[]{:S(2)}, u32[]{:S(2)}) collective-permute-start(bf16[16,2304]{1,0:T(8,128)(2,1)S(1)} %get-tuple-element.44), channel_id=1, source_target_pairs={{0,6},{2,4},{4,2},{6,0},{8,14},{10,12},{12,10},{14,8},{1,7},{3,5},... | collective-permute-start | bytes 221192 | tf_op jit(solution)/shard_map/ppermute | solution.py:23
  17.4 0.5 %collective-permute-start.6 = (bf16[16,2304]{1,0:T(8,128)(2,1)S(1)}, bf16[16,2304]{1,0:T(8,128)(2,1)S(1)}, u32[]{:S(2)}, u32[]{:S(2)}) collective-permute-start(bf16[16,2304]{1,0:T(8,128)(2,1)S(1)} %get-tuple-element.44), channel_id=1, source_target_pairs={{0,4},{2,6},{4,0},{6,2},{8,12},{10,14},{12,8},{14,10},{1,5},{3,7},... | collective-permute-start | bytes 221192 | tf_op jit(solution)/shard_map/ppermute | solution.py:23
  17.9 0.7 %collective-permute-start.5 = (bf16[16,2304]{1,0:T(8,128)(2,1)S(1)}, bf16[16,2304]{1,0:T(8,128)(2,1)S(1)}, u32[]{:S(2)}, u32[]{:S(2)}) collective-permute-start(bf16[16,2304]{1,0:T(8,128)(2,1)S(1)} %get-tuple-element.44), channel_id=1, source_target_pairs={{0,2},{2,0},{4,6},{6,4},{8,10},{10,8},{12,14},{14,12},{1,3},{3,1},... | collective-permute-start | bytes 221192 | tf_op jit(solution)/shard_map/ppermute | solution.py:23
  18.6 2.2 %collective-permute-done.7.refs_2_ = bf16[16,2304]{1,0:T(8,128)(2,1)S(1)} collective-permute-done((bf16[16,2304]{1,0:T(8,128)(2,1)S(1)}, bf16[16,2304]{1,0:T(8,128)(2,1)S(1)}, u32[]{:S(2)}, u32[]{:S(2)}) %collective-permute-start.7) | collective-permute-done | bytes 73760 | tf_op jit(solution)/shard_map/ppermute | solution.py:23
  20.9 0.9 %collective-permute-done.6.refs_1_ = bf16[16,2304]{1,0:T(8,128)(2,1)S(1)} collective-permute-done((bf16[16,2304]{1,0:T(8,128)(2,1)S(1)}, bf16[16,2304]{1,0:T(8,128)(2,1)S(1)}, u32[]{:S(2)}, u32[]{:S(2)}) %collective-permute-start.6) | collective-permute-done | bytes 73760 | tf_op jit(solution)/shard_map/ppermute | solution.py:23
  21.8 0.4 %collective-permute-done.5.refs_0_ = bf16[16,2304]{1,0:T(8,128)(2,1)S(1)} collective-permute-done((bf16[16,2304]{1,0:T(8,128)(2,1)S(1)}, bf16[16,2304]{1,0:T(8,128)(2,1)S(1)}, u32[]{:S(2)}, u32[]{:S(2)}) %collective-permute-start.5) | collective-permute-done | bytes 73760 | tf_op jit(solution)/shard_map/ppermute | solution.py:23
  22.3 0.1 merge.1
  22.3 3.7 %collective-permute-start.8 = (bf16[16,2592]{1,0:T(8,128)(2,1)S(1)}, bf16[16,2592]{1,0:T(8,128)(2,1)S(1)}, u32[]{:S(2)}, u32[]{:S(2)}) collective-permute-start(bf16[16,2592]{1,0:T(8,128)(2,1)S(1)} %get-tuple-element.33), channel_id=1, source_target_pairs={{0,12},{2,14},{4,8},{6,10},{8,4},{10,6},{12,0},{14,2},{1,13},{3,15... | collective-permute-start | bytes 248840 | tf_op jit(solution)/shard_map/ppermute | solution.py:23
  26.0 0.0 copy-done.1
  26.0 2.8 %collective-permute-done.8.arrived_ref.refs_0_ = bf16[16,2592]{1,0:T(8,128)(2,1)S(1)} collective-permute-done((bf16[16,2592]{1,0:T(8,128)(2,1)S(1)}, bf16[16,2592]{1,0:T(8,128)(2,1)S(1)}, u32[]{:S(2)}, u32[]{:S(2)}) %collective-permute-start.8) | collective-permute-done | bytes 82976 | tf_op jit(solution)/shard_map/ppermute | solution.py:23
  28.8 0.1 settle.1.grad_ref.mine_ref
  28.9 0.1 collective-permute-start.9
  29.0 0.4 %early.1.early_ref = f32[16,256]{1,0:T(8,128)S(1)} custom-call(bf16[16,2304]{1,0:T(8,128)(2,1)S(1)} %settle.1.grad_ref.mine_ref, bf16[256,4608]{1,0:T(8,128)(2,1)S(1)} %get-tuple-element.26.weight_ref, f32[1,256]{1,0:T(1,128)S(1)} %get-tuple-element.36.norms_ref), custom_call_target="tpu_custom_call" | custom-call | flops 18874368 | bytes 589824 | tf_op jit(solution)/shard_map/early/pallas_call | solution.py:311
  29.4 0.8 %collective-permute-done.9.other_ref = bf16[16,2304]{1,0:T(8,128)(2,1)S(1)} collective-permute-done((bf16[16,2304]{1,0:T(8,128)(2,1)S(1)}, bf16[16,2304]{1,0:T(8,128)(2,1)S(1)}, u32[]{:S(2)}, u32[]{:S(2)}) %collective-permute-start.9) | collective-permute-done | bytes 73760 | tf_op jit(solution)/shard_map/ppermute | solution.py:23
  30.2 2.3 %finish.1 = (bf16[256,4608]{1,0:T(8,128)(2,1)}, f32[1,256]{1,0:T(1,128)}, f32[288]{0:T(512)}, bf16[2,4608]{1,0:T(2,128)(2,1)}) custom-call(bf16[16,2304]{1,0:T(8,128)(2,1)S(1)} %settle.1.grad_ref.mine_ref, bf16[16,2304]{1,0:T(8,128)(2,1)S(1)} %collective-permute-done.9.other_ref, f32[16,256]{1,0:T(8,128)S(1)} %early.1.early_ref, ...), custom_call_target="tpu_custom_call" | custom-call | tf_op jit(solution)/shard_map/finish/pallas_call | solution.py:448
  (5 shorter events, 0.1 us)
Async XLA Ops:
  0.6 12.1 %copy-start = (f32[256]{0:T(256)S(1)}, f32[256]{0:T(256)}, u32[]{:S(2)}) copy-start(f32[256]{0:T(256)} %param.10) | copy-start | bytes 3076
  0.6 6.1 %collective-permute-start = (bf16[2,4608]{1,0:T(2,128)(2,1)}, bf16[2,4608]{1,0:T(2,128)(2,1)S(1)}, u32[]{:S(2)}, u32[]{:S(2)}) collective-permute-start(bf16[2,4608]{1,0:T(2,128)(2,1)} %cur_hbm.1), channel_id=1, source_target_pairs={{0,8},{2,10},{4,12},{6,14},{8,0},{10,2},{12,4},{14,6},{1,9},{3,11}... | collective-permute-start | bytes 55304 | tf_op jit(solution)/shard_map/ppermute | solution.py:23
  6.8 4.1 %collective-permute-start.1 = (bf16[4,5184]{1,0:T(4,128)(2,1)S(1)}, bf16[4,5184]{1,0:T(4,128)(2,1)S(1)}, u32[]{:S(2)}, u32[]{:S(2)}) collective-permute-start(bf16[4,5184]{1,0:T(4,128)(2,1)S(1)} %get-tuple-element.49), channel_id=1, source_target_pairs={{0,2},{1,7},{2,0},{3,5},{4,6},{5,3},{6,4},{7,1},{8,10},{9,15},{10,... | collective-permute-start | bytes 124424 | tf_op jit(solution)/shard_map/ppermute | solution.py:503
  8.7 4.0 %collective-permute-start.3 = (bf16[4,5184]{1,0:T(4,128)(2,1)S(1)}, bf16[4,5184]{1,0:T(4,128)(2,1)S(1)}, u32[]{:S(2)}, u32[]{:S(2)}) collective-permute-start(bf16[4,5184]{1,0:T(4,128)(2,1)S(1)} %get-tuple-element.48), channel_id=1, source_target_pairs={{0,4},{2,6},{4,0},{6,2},{8,12},{10,14},{12,8},{14,10},{1,5},{3,7},... | collective-permute-start | bytes 124424 | tf_op jit(solution)/shard_map/ppermute | solution.py:23
  10.8 1.2 %collective-permute-start.2 = (bf16[4,5184]{1,0:T(4,128)(2,1)S(1)}, bf16[4,5184]{1,0:T(4,128)(2,1)S(1)}, u32[]{:S(2)}, u32[]{:S(2)}) collective-permute-start(bf16[4,5184]{1,0:T(4,128)(2,1)S(1)} %collective-permute-done.1), channel_id=1, source_target_pairs={{0,1},{1,0},{2,3},{3,2},{4,5},{5,4},{6,7},{7,6},{8,9},{9,8},{10,11... | collective-permute-start | bytes 124424 | tf_op jit(solution)/shard_map/ppermute | solution.py:23
  12.7 13.3 %copy-start.1 = (f32[4608]{0:T(1024)S(1)}, f32[4608]{0:T(1024)}, u32[]{:S(2)}) copy-start(f32[4608]{0:T(1024)} %param.11) | copy-start | bytes 55300
  13.7 1.3 %collective-permute-start.4 = (bf16[16,2304]{1,0:T(8,128)(2,1)S(1)}, bf16[16,2304]{1,0:T(8,128)(2,1)S(1)}, u32[]{:S(2)}, u32[]{:S(2)}) collective-permute-start(bf16[16,2304]{1,0:T(8,128)(2,1)S(1)} %get-tuple-element.30), channel_id=1, source_target_pairs={{0,1},{1,0},{2,3},{3,2},{4,5},{5,4},{6,7},{7,6},{8,9},{9,8},{10,11... | collective-permute-start | bytes 221192 | tf_op jit(solution)/shard_map/ppermute | solution.py:23
  15.1 5.8 %collective-permute-start.7 = (bf16[16,2304]{1,0:T(8,128)(2,1)S(1)}, bf16[16,2304]{1,0:T(8,128)(2,1)S(1)}, u32[]{:S(2)}, u32[]{:S(2)}) collective-permute-start(bf16[16,2304]{1,0:T(8,128)(2,1)S(1)} %get-tuple-element.44), channel_id=1, source_target_pairs={{0,6},{2,4},{4,2},{6,0},{8,14},{10,12},{12,10},{14,8},{1,7},{3,5},... | collective-permute-start | bytes 221192 | tf_op jit(solution)/shard_map/ppermute | solution.py:23
  17.4 4.4 %collective-permute-start.6 = (bf16[16,2304]{1,0:T(8,128)(2,1)S(1)}, bf16[16,2304]{1,0:T(8,128)(2,1)S(1)}, u32[]{:S(2)}, u32[]{:S(2)}) collective-permute-start(bf16[16,2304]{1,0:T(8,128)(2,1)S(1)} %get-tuple-element.44), channel_id=1, source_target_pairs={{0,4},{2,6},{4,0},{6,2},{8,12},{10,14},{12,8},{14,10},{1,5},{3,7},... | collective-permute-start | bytes 221192 | tf_op jit(solution)/shard_map/ppermute | solution.py:23
  17.9 4.4 %collective-permute-start.5 = (bf16[16,2304]{1,0:T(8,128)(2,1)S(1)}, bf16[16,2304]{1,0:T(8,128)(2,1)S(1)}, u32[]{:S(2)}, u32[]{:S(2)}) collective-permute-start(bf16[16,2304]{1,0:T(8,128)(2,1)S(1)} %get-tuple-element.44), channel_id=1, source_target_pairs={{0,2},{2,0},{4,6},{6,4},{8,10},{10,8},{12,14},{14,12},{1,3},{3,1},... | collective-permute-start | bytes 221192 | tf_op jit(solution)/shard_map/ppermute | solution.py:23
  22.3 6.5 %collective-permute-start.8 = (bf16[16,2592]{1,0:T(8,128)(2,1)S(1)}, bf16[16,2592]{1,0:T(8,128)(2,1)S(1)}, u32[]{:S(2)}, u32[]{:S(2)}) collective-permute-start(bf16[16,2592]{1,0:T(8,128)(2,1)S(1)} %get-tuple-element.33), channel_id=1, source_target_pairs={{0,12},{2,14},{4,8},{6,10},{8,4},{10,6},{12,0},{14,2},{1,13},{3,15... | collective-permute-start | bytes 248840 | tf_op jit(solution)/shard_map/ppermute | solution.py:23
  28.9 1.3 %collective-permute-start.9 = (bf16[16,2304]{1,0:T(8,128)(2,1)S(1)}, bf16[16,2304]{1,0:T(8,128)(2,1)S(1)}, u32[]{:S(2)}, u32[]{:S(2)}) collective-permute-start(bf16[16,2304]{1,0:T(8,128)(2,1)S(1)} %settle.1.grad_ref.mine_ref), channel_id=1, source_target_pairs={{0,1},{1,0},{2,3},{3,2},{4,5},{5,4},{6,7},{7,6},{8,9},{9,8},{10,11... | collective-permute-start | bytes 221192 | tf_op jit(solution)/shard_map/ppermute | solution.py:23

commit v10 on v9

--- a/solution.py
+++ b/solution.py
@@ -24,10 +24,16 @@
 
 
 def core_columns(half):
-    core = lax.axis_index("latent")
+    core = lax.axis_index("latent") ^ (lax.axis_index("dp") // 4 % 2)
     here = pl.ds(pl.multiple_of(core * half, 128), half)
     there = pl.ds(pl.multiple_of((1 - core) * half, 128), half)
     return here, there
+
+
+def across(value, distance):
+    size = lax.axis_size("dp")
+    pairs = [(2 * k + c, 2 * (k ^ distance) + 1 - c) for k in range(size) for c in range(2)]
+    return lax.ppermute(value, ("dp", "latent"), pairs)
 
 
 def flip_rows(value, distance):
@@ -484,7 +490,7 @@
     rides = rest == 2
     turn = 2 if rides else 0
 
-    came = exchange(cur_rows, "dp", 4)
+    came = across(cur_rows, 4)
     ordered, cur_copy, weight = order(cur_rows, cached_rows, shuffle_perm, weight, turn)
     near = jnp.concatenate([cur_copy, came], axis=0)
     distance = 8
@@ -497,11 +503,11 @@
     ]
     roles = (1, 3)
     core = lax.axis_index("latent")
-    pairs = [(2 * k + c, 2 * (k ^ roles[c]) + c) for k in range(dp) for c in range(2)]
+    pairs = [(2 * k + c, 2 * (k ^ roles[1 - c]) + 1 - c) for k in range(dp) for c in range(2)]
     parts = [near, None, None, None]
-    parts[2] = exchange(messages[2], "dp", 2)
+    parts[2] = across(messages[2], 2)
     fetched = lax.ppermute(
-        jnp.where(core == 0, messages[roles[0]], messages[roles[1]]), ("dp", "latent"), pairs
+        jnp.where(core == 0, messages[roles[1]], messages[roles[0]]), ("dp", "latent"), pairs
     )
     handed = exchange(fetched, "latent", 1)
     parts[roles[0]] = jnp.where(core == 0, fetched, handed)
@@ -523,7 +529,11 @@
     )
     distance = 4
     while distance < dp:
-        arrived = exchange(sent, "dp", distance + turn)
+        arrived = (
+            across(sent, distance + turn)
+            if distance == 4
+            else exchange(sent, "dp", distance + turn)
+        )
         row_distance = distance // 4 * own + turn * rest * own
         if 2 * distance < dp:
             total, sent = merge(total, [arrived], (row_distance,))

time: 32.7 us -> 32 us (0.979)
  waiting for transfers between devices: 10.3 us -> 9.91 us
    ppermute x9 -> x6, starting transfers between devices: 13 us -> 4.76 us  [exchange(): return lax.ppermute(value, axis, [(k, k ^ distance) for k in range(size)])]
    ppermute x1 -> x4, starting transfers between devices: 1.96 us -> 9.95 us  [the longest x3 7.12 us: across(): return lax.ppermute(value, ('dp', 'latent'), pairs)]
    ppermute x9 -> x6, waiting for transfers between devices: 9.72 us -> 5.36 us  [exchange(): return lax.ppermute(value, axis, [(k, k ^ distance) for k in range(size)])]
    ppermute x1 -> x4, waiting for transfers between devices: 0.61 us -> 4.55 us  [the longest x3 3.18 us: across(): return lax.ppermute(value, ('dp', 'latent'), pairs)]
  transfers between devices with their start and end apart: 10 -> 10, of which waited for: 10 -> 9; matrix products, arithmetic and copies ran while one was open for 0% -> 0% of each run, Pallas kernels for 9% -> 9%
where the time goes in v10:
time: 32 us; the launch traced here: 31.9 us
  starting transfers between devices  14.7 us (46%)
  waiting for transfers between devices  9.91 us (31%)
  Pallas kernels  6.35 us (20%)
  between operations  0.71 us (2%)
    ppermute x3, starting transfers between devices, across(): return lax.ppermute(value, ('dp', 'latent'), pairs)  7.12 us
    ppermute x6, waiting for transfers between devices, exchange(): return lax.ppermute(value, axis, [(k, k ^ distance) for k in range(size)])  5.36 us
    ppermute x6, starting transfers between devices, exchange(): return lax.ppermute(value, axis, [(k, k ^ distance) for k in range(size)])  4.76 us
    ppermute x3, waiting for transfers between devices, across(): return lax.ppermute(value, ('dp', 'latent'), pairs)  3.18 us
    ppermute x1, starting transfers between devices, per_device(): lax.ppermute(jnp.where(core == 0, messages[roles[1]], messages[roles[0]])...  2.84 us
    pallas_call x1, Pallas kernels, finish(): pl.pallas_call(functools.partial(finish_kernel, tile, span, bool(riders),...  2.31 us
    pallas_call x1, Pallas kernels, order(): pl.pallas_call(functools.partial(order_kernel, turn), out_shape=(jax.Shap...  1.75 us
    ppermute x1, waiting for transfers between devices, per_device(): lax.ppermute(jnp.where(core == 0, messages[roles[1]], messages[roles[0]])...  1.37 us
  transfers between devices with their start and end apart: 10, of which 9 were waited for; matrix products, arithmetic and copies ran while one was open for 0% of the time, Pallas kernels for 9%

profile of v10, /device:TPU:0, one launch (start us, length us, event | category | flops | bytes accessed | tf_op | source)
XLA Modules:
  0.0 31.9 jit_solution(11374498556449098514)
XLA Ops:
  0.6 0.0 copy-start
  0.6 3.5 %collective-permute-start = (bf16[2,4608]{1,0:T(2,128)(2,1)}, bf16[2,4608]{1,0:T(2,128)(2,1)S(1)}, u32[]{:S(2)}, u32[]{:S(2)}) collective-permute-start(bf16[2,4608]{1,0:T(2,128)(2,1)} %cur_hbm.1), channel_id=1, source_target_pairs={{0,9},{1,8},{2,11},{3,10},{4,13},{5,12},{6,15},{7,14},{8,1},{9,0},... | collective-permute-start | bytes 55304 | tf_op jit(solution)/shard_map/ppermute | solution.py:36
  4.2 1.8 %order.1 = (bf16[16,576]{1,0:T(8,128)(2,1)S(1)}, bf16[2,4608]{1,0:T(2,128)(2,1)S(1)}, bf16[256,4608]{1,0:T(8,128)(2,1)S(1)}) custom-call(bf16[2,4608]{1,0:T(2,128)(2,1)} %cur_hbm.1, bf16[16,576]{1,0:T(8,128)(2,1)} %cached_hbm.1, s32[1,16]{1,0:T(1,128)} %bitcast.4, bf16[256,4608]{1,0:T(8,128)(2,1)} %weight_hbm.1), custom_call_target="tpu_custom_call" | custom-call | flops 4000000 | bytes 2000000 | tf_op jit(solution)/shard_map/order/pallas_call | solution.py:93
  6.0 0.0 collective-permute-done
  6.0 0.1 pad_maximum_fusion.1
  6.0 2.8 %collective-permute-start.1 = (bf16[4,5184]{1,0:T(4,128)(2,1)S(1)}, bf16[4,5184]{1,0:T(4,128)(2,1)S(1)}, u32[]{:S(2)}, u32[]{:S(2)}) collective-permute-start(bf16[4,5184]{1,0:T(4,128)(2,1)S(1)} %get-tuple-element.49), channel_id=1, source_target_pairs={{0,7},{1,2},{2,5},{3,0},{4,3},{5,6},{6,1},{7,4},{8,15},{9,10},{10,... | collective-permute-start | bytes 124424 | tf_op jit(solution)/shard_map/ppermute | solution.py:509
  8.9 0.5 %collective-permute-start.3 = (bf16[4,5184]{1,0:T(4,128)(2,1)S(1)}, bf16[4,5184]{1,0:T(4,128)(2,1)S(1)}, u32[]{:S(2)}, u32[]{:S(2)}) collective-permute-start(bf16[4,5184]{1,0:T(4,128)(2,1)S(1)} %get-tuple-element.48), channel_id=1, source_target_pairs={{0,5},{1,4},{2,7},{3,6},{4,1},{5,0},{6,3},{7,2},{8,13},{9,12},{10,... | collective-permute-start | bytes 124424 | tf_op jit(solution)/shard_map/ppermute | solution.py:36
  9.4 1.4 %collective-permute-done.1 = bf16[4,5184]{1,0:T(4,128)(2,1)S(1)} collective-permute-done((bf16[4,5184]{1,0:T(4,128)(2,1)S(1)}, bf16[4,5184]{1,0:T(4,128)(2,1)S(1)}, u32[]{:S(2)}, u32[]{:S(2)}) %collective-permute-start.1) | collective-permute-done | bytes 41504 | tf_op jit(solution)/shard_map/ppermute | solution.py:509
  10.7 0.4 %collective-permute-start.2 = (bf16[4,5184]{1,0:T(4,128)(2,1)S(1)}, bf16[4,5184]{1,0:T(4,128)(2,1)S(1)}, u32[]{:S(2)}, u32[]{:S(2)}) collective-permute-start(bf16[4,5184]{1,0:T(4,128)(2,1)S(1)} %collective-permute-done.1), channel_id=1, source_target_pairs={{0,1},{1,0},{2,3},{3,2},{4,5},{5,4},{6,7},{7,6},{8,9},{9,8},{10,11... | collective-permute-start | bytes 124424 | tf_op jit(solution)/shard_map/ppermute | solution.py:23
  11.2 0.8 %collective-permute-done.2 = bf16[4,5184]{1,0:T(4,128)(2,1)S(1)} collective-permute-done((bf16[4,5184]{1,0:T(4,128)(2,1)S(1)}, bf16[4,5184]{1,0:T(4,128)(2,1)S(1)}, u32[]{:S(2)}, u32[]{:S(2)}) %collective-permute-start.2) | collective-permute-done | bytes 41504 | tf_op jit(solution)/shard_map/ppermute | solution.py:23
  12.0 0.3 collective-permute-done.3.third_ref.refs_2_
  12.3 0.0 copy-done
  12.3 0.0 copy-start.1
  12.3 1.0 %encode.1 = (bf16[16,2304]{1,0:T(8,128)(2,1)S(1)}, bf16[16,4608]{1,0:T(8,128)(2,1)S(1)}, f32[16,256]{1,0:T(8,128)S(1)}, f32[16,256]{1,0:T(8,128)S(1)}, f32[16,1]{1,0:T(8,128)S(1)}) custom-call(bf16[4,4608]{1,0:T(4,128)(2,1)S(1)} %pad_maximum_fusion.2.first_ref, bf16[4,5184]{1,0:T(4,128)(2,1)S(1)} %get-tuple-element.47.second_ref.refs_1_, ...), custom_call_target="tpu_custom_call" | custom-call | tf_op jit(solution)/shard_map/encode/pallas_call | solution.py:172
  13.3 0.1 collective-permute-start.4
  13.5 0.7 %keep.1 = (f32[16,2304]{1,0:T(8,128)S(1)}, f32[16,256]{1,0:T(8,128)S(1)}, f32[1,256]{1,0:T(1,128)S(1)}, f32[256,1]{1,0:T(8,128)S(1)}, bf16[16,288]{1,0:T(8,128)(2,1)S(1)}, /*index=5*/f32[4,2,576]{2,1,0:T(2,128)S(1)}) custom-call(f32[16,256]{1,0:T(8,128)S(1)} %get-tuple-element.27.latents_ref, f32[16,256]{1,0:T(8,128)S(1)} %get-tuple-element.28.sharp_ref, ...), custom_call_target="tpu_custom_call" | custom-call | flops 18874368 | bytes 1179648 | tf_op jit(solution)/shard_map/keep/pallas_call | solution.py:240
  14.2 0.5 %collective-permute-done.4 = bf16[16,2304]{1,0:T(8,128)(2,1)S(1)} collective-permute-done((bf16[16,2304]{1,0:T(8,128)(2,1)S(1)}, bf16[16,2304]{1,0:T(8,128)(2,1)S(1)}, u32[]{:S(2)}, u32[]{:S(2)}) %collective-permute-start.4) | collective-permute-done | bytes 73760 | tf_op jit(solution)/shard_map/ppermute | solution.py:23
  14.7 2.6 %collective-permute-start.7 = (bf16[16,2304]{1,0:T(8,128)(2,1)S(1)}, bf16[16,2304]{1,0:T(8,128)(2,1)S(1)}, u32[]{:S(2)}, u32[]{:S(2)}) collective-permute-start(bf16[16,2304]{1,0:T(8,128)(2,1)S(1)} %get-tuple-element.44), channel_id=1, source_target_pairs={{0,6},{2,4},{4,2},{6,0},{8,14},{10,12},{12,10},{14,8},{1,7},{3,5},... | collective-permute-start | bytes 221192 | tf_op jit(solution)/shard_map/ppermute | solution.py:23
  17.3 0.1 collective-permute-start.6
  17.4 0.8 %collective-permute-start.5 = (bf16[16,2304]{1,0:T(8,128)(2,1)S(1)}, bf16[16,2304]{1,0:T(8,128)(2,1)S(1)}, u32[]{:S(2)}, u32[]{:S(2)}) collective-permute-start(bf16[16,2304]{1,0:T(8,128)(2,1)S(1)} %get-tuple-element.44), channel_id=1, source_target_pairs={{0,2},{2,0},{4,6},{6,4},{8,10},{10,8},{12,14},{14,12},{1,3},{3,1},... | collective-permute-start | bytes 221192 | tf_op jit(solution)/shard_map/ppermute | solution.py:23
  18.2 2.0 %collective-permute-done.7.refs_2_ = bf16[16,2304]{1,0:T(8,128)(2,1)S(1)} collective-permute-done((bf16[16,2304]{1,0:T(8,128)(2,1)S(1)}, bf16[16,2304]{1,0:T(8,128)(2,1)S(1)}, u32[]{:S(2)}, u32[]{:S(2)}) %collective-permute-start.7) | collective-permute-done | bytes 73760 | tf_op jit(solution)/shard_map/ppermute | solution.py:23
  20.3 1.4 %collective-permute-done.6.refs_1_ = bf16[16,2304]{1,0:T(8,128)(2,1)S(1)} collective-permute-done((bf16[16,2304]{1,0:T(8,128)(2,1)S(1)}, bf16[16,2304]{1,0:T(8,128)(2,1)S(1)}, u32[]{:S(2)}, u32[]{:S(2)}) %collective-permute-start.6) | collective-permute-done | bytes 73760 | tf_op jit(solution)/shard_map/ppermute | solution.py:23
  21.7 0.1 collective-permute-done.5.refs_0_
  21.8 0.1 merge.1
  21.9 3.1 %collective-permute-start.8 = (bf16[16,2592]{1,0:T(8,128)(2,1)S(1)}, bf16[16,2592]{1,0:T(8,128)(2,1)S(1)}, u32[]{:S(2)}, u32[]{:S(2)}) collective-permute-start(bf16[16,2592]{1,0:T(8,128)(2,1)S(1)} %get-tuple-element.33), channel_id=1, source_target_pairs={{0,13},{1,12},{2,15},{3,14},{4,9},{5,8},{6,11},{7,10},{8,5},{9,4},... | collective-permute-start | bytes 248840 | tf_op jit(solution)/shard_map/ppermute | solution.py:36
  25.0 0.0 copy-done.1
  25.0 2.9 %collective-permute-done.8.arrived_ref.refs_0_ = bf16[16,2592]{1,0:T(8,128)(2,1)S(1)} collective-permute-done((bf16[16,2592]{1,0:T(8,128)(2,1)S(1)}, bf16[16,2592]{1,0:T(8,128)(2,1)S(1)}, u32[]{:S(2)}, u32[]{:S(2)}) %collective-permute-start.8) | collective-permute-done | bytes 82976 | tf_op jit(solution)/shard_map/ppermute | solution.py:36
  27.9 0.1 settle.1.grad_ref.mine_ref
  28.0 0.7 %collective-permute-start.9 = (bf16[16,2304]{1,0:T(8,128)(2,1)S(1)}, bf16[16,2304]{1,0:T(8,128)(2,1)S(1)}, u32[]{:S(2)}, u32[]{:S(2)}) collective-permute-start(bf16[16,2304]{1,0:T(8,128)(2,1)S(1)} %settle.1.grad_ref.mine_ref), channel_id=1, source_target_pairs={{0,1},{1,0},{2,3},{3,2},{4,5},{5,4},{6,7},{7,6},{8,9},{9,8},{10,11... | collective-permute-start | bytes 221192 | tf_op jit(solution)/shard_map/ppermute | solution.py:23
  28.7 0.4 %early.1.early_ref = f32[16,256]{1,0:T(8,128)S(1)} custom-call(bf16[16,2304]{1,0:T(8,128)(2,1)S(1)} %settle.1.grad_ref.mine_ref, bf16[256,4608]{1,0:T(8,128)(2,1)S(1)} %get-tuple-element.26.weight_ref, f32[1,256]{1,0:T(1,128)S(1)} %get-tuple-element.36.norms_ref), custom_call_target="tpu_custom_call" | custom-call | flops 18874368 | bytes 589824 | tf_op jit(solution)/shard_map/early/pallas_call | solution.py:317
  29.1 0.5 %collective-permute-done.9.other_ref = bf16[16,2304]{1,0:T(8,128)(2,1)S(1)} collective-permute-done((bf16[16,2304]{1,0:T(8,128)(2,1)S(1)}, bf16[16,2304]{1,0:T(8,128)(2,1)S(1)}, u32[]{:S(2)}, u32[]{:S(2)}) %collective-permute-start.9) | collective-permute-done | bytes 73760 | tf_op jit(solution)/shard_map/ppermute | solution.py:23
  29.6 2.3 %finish.1 = (bf16[256,4608]{1,0:T(8,128)(2,1)}, f32[1,256]{1,0:T(1,128)}, f32[288]{0:T(512)}, bf16[2,4608]{1,0:T(2,128)(2,1)}) custom-call(bf16[16,2304]{1,0:T(8,128)(2,1)S(1)} %settle.1.grad_ref.mine_ref, bf16[16,2304]{1,0:T(8,128)(2,1)S(1)} %collective-permute-done.9.other_ref, f32[16,256]{1,0:T(8,128)S(1)} %early.1.early_ref, ...), custom_call_target="tpu_custom_call" | custom-call | tf_op jit(solution)/shard_map/finish/pallas_call | solution.py:454
  (5 shorter events, 0.1 us)
Async XLA Ops:
  0.6 11.7 %copy-start = (f32[256]{0:T(256)S(1)}, f32[256]{0:T(256)}, u32[]{:S(2)}) copy-start(f32[256]{0:T(256)} %param.10) | copy-start | bytes 3076
  0.6 5.3 %collective-permute-start = (bf16[2,4608]{1,0:T(2,128)(2,1)}, bf16[2,4608]{1,0:T(2,128)(2,1)S(1)}, u32[]{:S(2)}, u32[]{:S(2)}) collective-permute-start(bf16[2,4608]{1,0:T(2,128)(2,1)} %cur_hbm.1), channel_id=1, source_target_pairs={{0,9},{1,8},{2,11},{3,10},{4,13},{5,12},{6,15},{7,14},{8,1},{9,0},... | collective-permute-start | bytes 55304 | tf_op jit(solution)/shard_map/ppermute | solution.py:36
  6.0 4.7 %collective-permute-start.1 = (bf16[4,5184]{1,0:T(4,128)(2,1)S(1)}, bf16[4,5184]{1,0:T(4,128)(2,1)S(1)}, u32[]{:S(2)}, u32[]{:S(2)}) collective-permute-start(bf16[4,5184]{1,0:T(4,128)(2,1)S(1)} %get-tuple-element.49), channel_id=1, source_target_pairs={{0,7},{1,2},{2,5},{3,0},{4,3},{5,6},{6,1},{7,4},{8,15},{9,10},{10,... | collective-permute-start | bytes 124424 | tf_op jit(solution)/shard_map/ppermute | solution.py:509
  8.9 3.4 %collective-permute-start.3 = (bf16[4,5184]{1,0:T(4,128)(2,1)S(1)}, bf16[4,5184]{1,0:T(4,128)(2,1)S(1)}, u32[]{:S(2)}, u32[]{:S(2)}) collective-permute-start(bf16[4,5184]{1,0:T(4,128)(2,1)S(1)} %get-tuple-element.48), channel_id=1, source_target_pairs={{0,5},{1,4},{2,7},{3,6},{4,1},{5,0},{6,3},{7,2},{8,13},{9,12},{10,... | collective-permute-start | bytes 124424 | tf_op jit(solution)/shard_map/ppermute | solution.py:36
  10.7 1.2 %collective-permute-start.2 = (bf16[4,5184]{1,0:T(4,128)(2,1)S(1)}, bf16[4,5184]{1,0:T(4,128)(2,1)S(1)}, u32[]{:S(2)}, u32[]{:S(2)}) collective-permute-start(bf16[4,5184]{1,0:T(4,128)(2,1)S(1)} %collective-permute-done.1), channel_id=1, source_target_pairs={{0,1},{1,0},{2,3},{3,2},{4,5},{5,4},{6,7},{7,6},{8,9},{9,8},{10,11... | collective-permute-start | bytes 124424 | tf_op jit(solution)/shard_map/ppermute | solution.py:23
  12.3 12.6 %copy-start.1 = (f32[4608]{0:T(1024)S(1)}, f32[4608]{0:T(1024)}, u32[]{:S(2)}) copy-start(f32[4608]{0:T(1024)} %param.11) | copy-start | bytes 55300
  13.3 1.3 %collective-permute-start.4 = (bf16[16,2304]{1,0:T(8,128)(2,1)S(1)}, bf16[16,2304]{1,0:T(8,128)(2,1)S(1)}, u32[]{:S(2)}, u32[]{:S(2)}) collective-permute-start(bf16[16,2304]{1,0:T(8,128)(2,1)S(1)} %get-tuple-element.30), channel_id=1, source_target_pairs={{0,1},{1,0},{2,3},{3,2},{4,5},{5,4},{6,7},{7,6},{8,9},{9,8},{10,11... | collective-permute-start | bytes 221192 | tf_op jit(solution)/shard_map/ppermute | solution.py:23
  14.7 5.6 %collective-permute-start.7 = (bf16[16,2304]{1,0:T(8,128)(2,1)S(1)}, bf16[16,2304]{1,0:T(8,128)(2,1)S(1)}, u32[]{:S(2)}, u32[]{:S(2)}) collective-permute-start(bf16[16,2304]{1,0:T(8,128)(2,1)S(1)} %get-tuple-element.44), channel_id=1, source_target_pairs={{0,6},{2,4},{4,2},{6,0},{8,14},{10,12},{12,10},{14,8},{1,7},{3,5},... | collective-permute-start | bytes 221192 | tf_op jit(solution)/shard_map/ppermute | solution.py:23
  17.3 4.4 %collective-permute-start.6 = (bf16[16,2304]{1,0:T(8,128)(2,1)S(1)}, bf16[16,2304]{1,0:T(8,128)(2,1)S(1)}, u32[]{:S(2)}, u32[]{:S(2)}) collective-permute-start(bf16[16,2304]{1,0:T(8,128)(2,1)S(1)} %get-tuple-element.44), channel_id=1, source_target_pairs={{0,4},{2,6},{4,0},{6,2},{8,12},{10,14},{12,8},{14,10},{1,5},{3,7},... | collective-permute-start | bytes 221192 | tf_op jit(solution)/shard_map/ppermute | solution.py:23
  17.4 4.4 %collective-permute-start.5 = (bf16[16,2304]{1,0:T(8,128)(2,1)S(1)}, bf16[16,2304]{1,0:T(8,128)(2,1)S(1)}, u32[]{:S(2)}, u32[]{:S(2)}) collective-permute-start(bf16[16,2304]{1,0:T(8,128)(2,1)S(1)} %get-tuple-element.44), channel_id=1, source_target_pairs={{0,2},{2,0},{4,6},{6,4},{8,10},{10,8},{12,14},{14,12},{1,3},{3,1},... | collective-permute-start | bytes 221192 | tf_op jit(solution)/shard_map/ppermute | solution.py:23
  21.9 6.0 %collective-permute-start.8 = (bf16[16,2592]{1,0:T(8,128)(2,1)S(1)}, bf16[16,2592]{1,0:T(8,128)(2,1)S(1)}, u32[]{:S(2)}, u32[]{:S(2)}) collective-permute-start(bf16[16,2592]{1,0:T(8,128)(2,1)S(1)} %get-tuple-element.33), channel_id=1, source_target_pairs={{0,13},{1,12},{2,15},{3,14},{4,9},{5,8},{6,11},{7,10},{8,5},{9,4},... | collective-permute-start | bytes 248840 | tf_op jit(solution)/shard_map/ppermute | solution.py:36
  28.0 1.6 %collective-permute-start.9 = (bf16[16,2304]{1,0:T(8,128)(2,1)S(1)}, bf16[16,2304]{1,0:T(8,128)(2,1)S(1)}, u32[]{:S(2)}, u32[]{:S(2)}) collective-permute-start(bf16[16,2304]{1,0:T(8,128)(2,1)S(1)} %settle.1.grad_ref.mine_ref), channel_id=1, source_target_pairs={{0,1},{1,0},{2,3},{3,2},{4,5},{5,4},{6,7},{7,6},{8,9},{9,8},{10,11... | collective-permute-start | bytes 221192 | tf_op jit(solution)/shard_map/ppermute | solution.py:23
